TPU v7x, 128 devices: a whole 4x4x4 slice. The times are simulated.
128 devices in a mesh: dp: 8 (over x, z_hi), tensor: 16 (over z_lo, y, core).
Axes of the slice: x: 4, y: 4, z: 4 (z_hi: 2, z_lo: 2; z = z_hi * 2 + z_lo), core: 2. Of those that a mesh axis runs over, the one named last changes fastest.
Arguments:
- qkv_master: float32 [8, 1024, 5120], P('dp', 'tensor'), may hold values from -0.0625 to 0.0625
- qkv_moment1: float32 [8, 1024, 5120], P('dp', 'tensor'), may hold values from -6 to 6
- qkv_moment2: float32 [8, 1024, 5120], P('dp', 'tensor'), may hold values from 0.1 to 10
- qkv_grad: bfloat16 [8, 1024, 5120], P('dp', 'tensor'), may hold values from -6 to 6
- out_master: float32 [8, 1024, 4096], P('dp', 'tensor'), may hold values from -0.09375 to 0.09375
- out_moment1: float32 [8, 1024, 4096], P('dp', 'tensor'), may hold values from -6 to 6
- out_moment2: float32 [8, 1024, 4096], P('dp', 'tensor'), may hold values from 0.1 to 10
- out_grad: bfloat16 [8, 1024, 4096], P('dp', 'tensor'), may hold values from -6 to 6
- embed_table: bfloat16 [76032, 8, 1024], P('dp', None, 'tensor'), may hold values from -6 to 6
- norm_gain: float32 [8, 1024], P(None, 'tensor'), may hold values from 0.5 to 1.5
- token_ids: int32 [512, 4], P('dp'), may hold values from 0 to 76031, as said below
- lengths: int32 [512], P(('dp', 'tensor')), may hold values from 1 to 384, 98304 in all
- kv_cache: bfloat16 [512, 4, 384, 256], P(('dp', 'tensor')), may hold values from -6 to 6
Outputs:
- decoded: bfloat16 [512, 4, 8, 1024], P('dp', None, None, 'tensor')
- fresh_kv: bfloat16 [512, 4, 4, 256], P(('dp', 'tensor'))
- qkv_master_new: float32 [8, 1024, 5120], P('dp', 'tensor')
- qkv_moment1_new: float32 [8, 1024, 5120], P('dp', 'tensor')
- qkv_moment2_new: float32 [8, 1024, 5120], P('dp', 'tensor')
- out_master_new: float32 [8, 1024, 4096], P('dp', 'tensor')
- out_moment1_new: float32 [8, 1024, 4096], P('dp', 'tensor')
- out_moment2_new: float32 [8, 1024, 4096], P('dp', 'tensor')
Inputs may be any that keep to these rules, and one draw needn't show every extreme that they name: `token_ids`: the vocabulary is 8 blocks of 9504 ids. Of the tokens of one decode group (each aligned run of 64 rows, all steps), exactly 64 fall in one block, chosen per group, and the rest are spread over the other blocks as evenly as possible. `lengths`: some row has exactly 384 cached tokens.
All inputs are finite; a program needn't handle non-finite values. No bound on the sum of `lengths` on one device may be relied on, other than what follows from the above.
Results may differ from a plain program's by a relative error of at most 0.0057.
Values may be sent and summed in bfloat16 or wider, within the bound.
No kernel may reach another device: no remote copies, remote signals or barrier semaphores. Data moves between devices by JAX's collectives and lax.ppermute only.
A program may use at most 128 MiB of HBM per device.

v0:
```python
import math

import jax
import jax.numpy as jnp
from jax import lax
from jax.sharding import PartitionSpec as P

D = 8192
QH = 32
KVH = 4
HD = 128


beta_first = 0.9
beta_second = 0.95
adam_epsilon = 1e-08
learn_rate = 0.002
decay_rate = 0.1
bias_first = 1.0 - 0.9**50
bias_second = 1.0 - 0.95**50
rope_base = 1000000.0
norm_epsilon = 1e-06


def adamw(master, moment_one, moment_two, gradient):
    grad_float = gradient.astype(jnp.float32)
    moment_one = beta_first * moment_one + (1.0 - beta_first) * grad_float
    moment_two = beta_second * moment_two + (1.0 - beta_second) * grad_float * grad_float
    stepped = moment_one / bias_first / (jnp.sqrt(moment_two / bias_second) + adam_epsilon)
    master = master - learn_rate * (stepped + decay_rate * master)
    return (master, moment_one, moment_two)


def rotate(values, positions):
    half_dim = values.shape[-1] // 2
    exponent = jnp.arange(half_dim).astype(jnp.float32) * (2.0 / values.shape[-1])
    freqs = jnp.power(jnp.float32(rope_base), -exponent)
    angles = positions.astype(jnp.float32)[..., None] * freqs
    cosine = jnp.cos(angles)[..., None, :]
    sine = jnp.sin(angles)[..., None, :]
    first_half = values[..., :half_dim]
    second_half = values[..., half_dim:]
    return jnp.concatenate(
        [first_half * cosine - second_half * sine, second_half * cosine + first_half * sine],
        axis=-1,
    )


def attend(queries, keys_new, values_new, cache, lengths):
    head_dim = queries.shape[-1]
    row_total, step_total = (queries.shape[0], queries.shape[1])
    scale = 1.0 / math.sqrt(head_dim)
    cache_keys = cache[..., :head_dim]
    cache_values = cache[..., head_dim:]
    cache_scores = (
        jnp.einsum("rsngd,rncd->rngsc", queries, cache_keys, preferred_element_type=jnp.float32)
        * scale
    )
    new_scores = (
        jnp.einsum("rsngd,rtnd->rngst", queries, keys_new, preferred_element_type=jnp.float32)
        * scale
    )
    cache_live = jnp.arange(cache.shape[2])[None, :] < lengths[:, None]
    cache_scores = jnp.where(cache_live[:, None, None, None, :], cache_scores, -jnp.inf)
    causal = jnp.arange(step_total)[:, None] >= jnp.arange(step_total)[None, :]
    new_scores = jnp.where(causal, new_scores, -jnp.inf)
    highest = jnp.maximum(jnp.max(cache_scores, axis=-1), jnp.max(new_scores, axis=-1))
    cache_exp = jnp.exp(cache_scores - highest[..., None])
    new_exp = jnp.exp(new_scores - highest[..., None])
    denom = jnp.sum(cache_exp, axis=-1) + jnp.sum(new_exp, axis=-1)
    cache_weights = (cache_exp / denom[..., None]).astype(jnp.bfloat16)
    new_weights = (new_exp / denom[..., None]).astype(jnp.bfloat16)
    mixed = jnp.einsum(
        "rngsc,rncd->rsngd", cache_weights, cache_values, preferred_element_type=jnp.float32
    )
    mixed = mixed + jnp.einsum(
        "rngst,rtnd->rsngd", new_weights, values_new, preferred_element_type=jnp.float32
    )
    return mixed.astype(jnp.bfloat16).reshape(row_total, step_total, -1)


def on_device(
    qkv_master,
    qkv_moment1,
    qkv_moment2,
    qkv_grad,
    out_master,
    out_moment1,
    out_moment2,
    out_grad,
    embed_table,
    norm_gain,
    token_ids,
    lengths,
    kv_cache,
):
    new_qkv = adamw(qkv_master, qkv_moment1, qkv_moment2, qkv_grad)
    new_out = adamw(out_master, out_moment1, out_moment2, out_grad)
    qkv_local = new_qkv[0].astype(jnp.bfloat16)
    out_local = new_out[0].astype(jnp.bfloat16)
    group_rows, step_total = token_ids.shape
    tensor_count = lax.axis_size("tensor")
    vocab_local = embed_table.shape[0]
    my_group = lax.axis_index("dp")
    all_ids = lax.all_gather(token_ids, "dp", axis=0, tiled=True)
    offset_ids = all_ids - my_group * vocab_local
    inside = (offset_ids >= 0) & (offset_ids < vocab_local)
    looked = jnp.take(embed_table, jnp.clip(offset_ids, 0, vocab_local - 1), axis=0)
    terms = jnp.where(inside[:, :, None, None], looked.astype(jnp.float32), 0.0)
    hidden = lax.psum_scatter(terms.astype(jnp.bfloat16), "dp", scatter_dimension=0, tiled=True)
    hidden_float = hidden.astype(jnp.float32)
    squared = jnp.sum(hidden_float * hidden_float, axis=(2, 3))
    inverse = lax.rsqrt(lax.psum(squared, "tensor") / D + norm_epsilon)
    normed = (hidden_float * inverse[:, :, None, None] * norm_gain).astype(jnp.bfloat16)
    token_count = group_rows * step_total
    normed_flat = normed.reshape(token_count, -1)
    qkv_full = lax.all_gather(qkv_local, "dp", axis=0, tiled=True)
    qkv_flat = qkv_full.reshape(-1, qkv_full.shape[-1])
    own_tokens = token_count // tensor_count
    projected = lax.psum_scatter(
        jnp.dot(normed_flat, qkv_flat, preferred_element_type=jnp.float32),
        "tensor",
        scatter_dimension=0,
        tiled=True,
    )
    own_rows = own_tokens // step_total
    projected = projected.reshape(own_rows, step_total, -1)
    query_width = QH * HD
    key_width = KVH * HD
    query = projected[..., :query_width].reshape(own_rows, step_total, QH, HD)
    key_new = projected[..., query_width : query_width + key_width].reshape(
        own_rows, step_total, KVH, HD
    )
    value_new = projected[..., query_width + key_width :].reshape(own_rows, step_total, KVH, HD)
    positions = lengths[:, None] + jnp.arange(step_total)[None, :]
    query = rotate(query, positions).astype(jnp.bfloat16)
    key_new = rotate(key_new, positions).astype(jnp.bfloat16)
    value_new = value_new.astype(jnp.bfloat16)
    fresh_kv = jnp.concatenate([key_new, value_new], axis=-1)
    attended = attend(
        query.reshape(own_rows, step_total, KVH, QH // KVH, HD),
        key_new,
        value_new,
        kv_cache,
        lengths,
    )
    attended_flat = attended.reshape(own_tokens, query_width)
    heads_part = lax.all_to_all(attended_flat, "tensor", split_axis=1, concat_axis=0, tiled=True)
    out_slices = lax.all_to_all(out_local, "tensor", split_axis=2, concat_axis=1, tiled=True)
    partial_out = jnp.einsum(
        "tq,kjq->tkj",
        heads_part,
        lax.all_gather(out_slices, "dp", axis=0, tiled=True),
        preferred_element_type=jnp.float32,
    )
    output = lax.psum_scatter(partial_out, "tensor", scatter_dimension=2, tiled=True)
    decoded = (hidden_float + output.reshape(hidden_float.shape)).astype(jnp.bfloat16)
    return (
        decoded,
        fresh_kv,
        new_qkv[0],
        new_qkv[1],
        new_qkv[2],
        new_out[0],
        new_out[1],
        new_out[2],
    )


def solution(mesh):
    return jax.shard_map(
        on_device,
        mesh=mesh,
        in_specs=(
            P("dp", "tensor", None),
            P("dp", "tensor", None),
            P("dp", "tensor", None),
            P("dp", "tensor", None),
            P("dp", "tensor", None),
            P("dp", "tensor", None),
            P("dp", "tensor", None),
            P("dp", "tensor", None),
            P("dp", None, "tensor"),
            P(None, "tensor"),
            P("dp", None),
            P(("dp", "tensor")),
            P(("dp", "tensor"), None, None, None),
        ),
        out_specs=(
            P("dp", None, None, "tensor"),
            P(("dp", "tensor"), None, None, None),
            P("dp", "tensor", None),
            P("dp", "tensor", None),
            P("dp", "tensor", None),
            P("dp", "tensor", None),
            P("dp", "tensor", None),
            P("dp", "tensor", None),
        ),
        check_vma=False,
    )
```

profile of v0, /device:TPU:1, one launch (start us, length us, event | category | flops | bytes accessed | tf_op | source)
XLA Modules:
  0.0 494.1 jit_solution(12086558406469439899)
XLA Ops:
  7.2 0.0 reduce-scatter.4.cloned.1.call-start
  7.2 26.8 %all-gather = s32[8,64,4]{1,2,0:T(4,128)S(1)} all-gather(s32[1,64,4]{1,2,0:T(4,128)} %bitcast.100), channel_id=1, replica_groups=mesh['dp'=8,'tensor'=16] {'dp'}, dimensions={0}, use_global_device_ids=true | all-gather | bytes 9216 | tf_op jit(solution)/shard_map/all_gather | solution.py:105
  34.0 0.1 reshape.136
  34.2 0.1 copy.138
  34.3 0.2 reshape.118
  34.5 22.0 %copy.139 = bf16[9504,8,64]{2,1,0:T(8,128)(2,1)} copy(bf16[9504,8,64]{0,2,1:T(8,128)(2,1)} %param.21) | data formatting | bytes 19464192 | tf_op args[8]
  56.5 0.2 copy.137
  56.6 0.2 copy.155
  56.8 21.3 %gather_fusion = bf16[2048,8,64]{2,1,0:T(8,128)(2,1)} fusion(bf16[9504,8,64]{2,1,0:T(8,128)(2,1)} %copy.139, s32[2048]{0:T(1024)S(1)} %broadcast_clamp_fusion), kind=kCustom, calls=%fused_computation | custom fusion | bytes 4202496 | tf_op jit(solution)/shard_map/jit(_take)/gather | solution.py:108
  78.1 7.4 %select_convert_fusion = bf16[512,4,8,64]{3,2,1,0:T(8,128)(2,1)} fusion(bf16[512,4,8,64]{3,2,1,0:T(8,128)(2,1)} %bitcast.90, pred[512,4]{1,0:T(8,128)(4,1)S(1)} %copy.137, pred[512,4]{1,0:T(8,128)(4,1)S(1)} %bitcast.99), kind=kLoop, calls=%fused_computation.1 | loop fusion | flops 4194304 | bytes 4198400 | tf_op jit(solution)/shard_map/convert_element_type | solution.py:110
  85.5 0.0 reduce-scatter.4.cloned.1.call-update
  85.6 0.0 all-gather.4.cloned.1.call-start
  85.6 1.2 copy-done.1
  86.8 0.4 copy-done.2
  87.2 0.2 copy-done.6
  87.4 4.1 fusion.53
  91.5 0.0 reduce-scatter.6.cloned.1.call-start
  91.6 82.9 %reduce-scatter.4.cloned.1.call-done = bf16[64,4,8,64]{3,2,1,0:T(8,128)(2,1)} async-done(((bf16[512,4,8,64]{3,2,1,0:T(8,128)(2,1)}), bf16[64,4,8,64]{3,2,1,0:T(8,128)(2,1)}) %reduce-scatter.4.cloned.1.call-update) | async-done | bytes 262160 | tf_op jit(solution)/shard_map/reduce_scatter | solution.py:110
  174.4 1.6 fusion.29
  176.0 0.1 copy.140
  176.1 28.5 %psum.7 = f32[64,4]{0,1:T(4,128)S(1)} all-reduce(f32[64,4]{0,1:T(4,128)S(1)} %copy.140), channel_id=1, replica_groups=mesh['dp'=8,'tensor'=16] {'tensor'}, use_global_device_ids=true, to_apply=%region_2.3 | all-reduce | flops 256 | bytes 2048 | tf_op jit(solution)/shard_map/psum | solution.py:113
  204.6 0.1 copy.141
  204.7 1.4 fusion.31
  206.0 0.3 reshape.110
  206.4 50.6 %all-gather.4.cloned.1.call-done = bf16[8,64,5120]{2,1,0:T(8,128)(2,1)} async-done(((bf16[1,64,5120]{2,1,0:T(8,128)(2,1)}), bf16[8,64,5120]{2,1,0:T(8,128)(2,1)}) %all-gather.4.cloned.1.call-update) | async-done | bytes 5242896 | tf_op jit(solution)/shard_map/all_gather | solution.py:117
  257.0 6.3 %fusion.58 = f32[256,5120]{1,0:T(8,128)} fusion(bf16[256,512]{1,0:T(8,128)(2,1)S(1)} %reshape.110, bf16[512,5120]{1,0:T(8,128)(2,1)} %bitcast.93), kind=kOutput, calls=%fused_computation.81 | convolution fusion | flops 1342177280 | bytes 10747904 | tf_op jit(solution)/shard_map/dot_general | solution.py:121
  263.3 0.2 all-gather.6.cloned.1.call-start
  263.5 1.0 copy-done.3
  264.5 0.3 copy-done.4
  264.8 0.1 copy-done.7
  265.0 3.4 fusion.50
  268.4 2.7 copy.146
  271.1 0.5 broadcast.108
  271.6 22.4 %reduce = bf16[4096,64]{1,0:T(8,128)(2,1)S(1)} reduce(bf16[4096,1,64]{2,1,0:T(2,128)(2,1)S(1)} %bitcast.92, bf16[]{:T(256)} %broadcast.108), dimensions={1}, to_apply=%bitcast.79.reduce_sub_computation | reduce | bytes 1048578
  294.1 0.7 reshape.143
  294.8 17.4 %all_to_all.37 = bf16[16,2,8192]{2,1,0:T(2,128)(2,1)S(1)} all-to-all(bf16[16,2,8192]{2,1,0:T(2,128)(2,1)S(1)} %reshape.143), channel_id=1, replica_groups=mesh['dp'=8,'tensor'=16] {'tensor'}, dimensions={0} | all-to-all | bytes 1048576 | tf_op jit(solution)/shard_map/all_to_all | solution.py:149
  312.1 1.2 reshape.144
  313.4 2.3 copy.147
  315.7 0.1 copy.157
  315.8 1.0 copy.148
  316.8 0.1 iota_compare_fusion
  316.9 0.1 add_convert_fusion.2
  317.0 0.1 multiply_cosine_fusion
  317.1 14.7 %reduce-scatter.6.cloned.1.call-done = f32[16,5120]{1,0:T(8,128)} async-done(((f32[256,5120]{1,0:T(8,128)}), f32[16,5120]{1,0:T(8,128)}) %reduce-scatter.6.cloned.1.call-update) | async-done | bytes 327696 | tf_op jit(solution)/shard_map/reduce_scatter | solution.py:120
  331.8 1.1 reshape.112
  332.9 0.2 reshape.113
  333.1 0.1 subtract_convert_fusion.1
  333.2 0.1 fusion.37
  333.4 0.8 fusion.57
  334.2 2.3 fusion.56
  336.6 0.1 fusion.41
  336.7 0.3 fusion.34
  337.0 0.3 convolution_bitcast_fusion
  337.3 0.5 fusion.23
  337.8 0.7 copy.145
  338.5 8.1 %all-to-all-start = ((bf16[16,16,256]{2,0,1:T(8,128)(2,1)}), bf16[16,16,256]{2,0,1:T(8,128)(2,1)S(1)}, u32[]{:S(2)}, u32[]{:S(2)}) async-start(bf16[16,16,256]{2,0,1:T(8,128)(2,1)} %copy.145), calls=%async_computation.2 | async-start | bytes 262144 | tf_op jit(solution)/shard_map/all_to_all | solution.py:148
  346.6 0.0 reduce-scatter.8.cloned.1.call-start
  346.7 62.2 %all-gather.6.cloned.1.call-done = bf16[8,1024,256]{2,1,0:T(8,128)(2,1)} async-done(((bf16[1,1024,256]{2,1,0:T(8,128)(2,1)}), bf16[8,1024,256]{2,1,0:T(8,128)(2,1)}) %all-gather.6.cloned.1.call-update) | async-done | bytes 4194320 | tf_op jit(solution)/shard_map/all_gather | solution.py:153
  408.9 6.7 %fusion.59 = f32[256,8,1024]{0,2,1:T(8,128)} fusion(bf16[256,256,1]{1,0,2:T(8,128)(2,1)S(1)} %bitcast.98, bf16[8,1024,256]{2,1,0:T(8,128)(2,1)} %all-gather.6.cloned.1.call-done), kind=kOutput, calls=%fused_computation.82 | convolution fusion | flops 1073741824 | bytes 12713984 | tf_op jit(solution)/shard_map/tq,kjq->tkj/dot_general | solution.py:150
  415.6 0.1 pad_maximum_fusion.1
  415.7 0.6 copy.150
  416.4 68.8 %reduce-scatter.8.cloned.1.call-done = f32[256,8,64]{0,2,1:T(8,128)} async-done(((f32[256,8,1024]{0,2,1:T(8,128)}), f32[256,8,64]{0,2,1:T(8,128)}) %reduce-scatter.8.cloned.1.call-update) | async-done | bytes 524304 | tf_op jit(solution)/shard_map/reduce_scatter | solution.py:156
  485.2 1.5 copy.149
  486.7 0.9 fusion.32
  (35 shorter events, 0.3 us)
Async XLA Ops:
  7.2 167.3 %reduce-scatter.4.cloned.1.call-start = ((), (), s32[]{:S(2)}) async-start(), calls=%async_computation.5 | async-start | bytes 4718592 | tf_op jit(solution)/shard_map/reduce_scatter | solution.py:110
  85.5 1.3 copy-start.1
  85.5 1.7 copy-start.2
  85.5 1.9 copy-start.6
  85.6 119.1 %copy-start.8 = (f32[8,64]{1,0:T(8,128)S(1)}, f32[8,64]{1,0:T(8,128)}, u32[]{:S(2)}) copy-start(f32[8,64]{1,0:T(8,128)} %param.22) | copy-start | bytes 6148
  85.6 171.4 %all-gather.4.cloned.1.call-start = ((), (), s32[]{:S(2)}) async-start(), calls=%async_computation.6 | async-start | bytes 5898240 | tf_op jit(solution)/shard_map/all_gather | solution.py:117
  91.5 240.3 %reduce-scatter.6.cloned.1.call-start = ((), (), s32[]{:S(2)}) async-start(), calls=%async_computation.7 | async-start | bytes 5570560 | tf_op jit(solution)/shard_map/reduce_scatter | solution.py:120
  263.3 1.2 copy-start.3
  263.3 1.5 copy-start.4
  263.3 1.7 copy-start.7
  263.3 145.6 %all-gather.6.cloned.1.call-start = ((), (), s32[]{:S(2)}) async-start(), calls=%async_computation.8 | async-start | bytes 4718592 | tf_op jit(solution)/shard_map/all_gather | solution.py:153
  315.8 1.1 copy-start.9
  334.2 3.1 copy-start.5
  338.5 70.4 %all-to-all-start = ((bf16[16,16,256]{2,0,1:T(8,128)(2,1)}), bf16[16,16,256]{2,0,1:T(8,128)(2,1)S(1)}, u32[]{:S(2)}, u32[]{:S(2)}) async-start(bf16[16,16,256]{2,0,1:T(8,128)(2,1)} %copy.145), calls=%async_computation.2 | async-start | bytes 262144 | tf_op jit(solution)/shard_map/all_to_all | solution.py:148
  346.6 138.6 %reduce-scatter.8.cloned.1.call-start = ((), (), s32[]{:S(2)}) async-start(), calls=%async_computation.9 | async-start | bytes 8912896 | tf_op jit(solution)/shard_map/reduce_scatter | solution.py:156
  415.6 71.0 %copy-start = (bf16[64,4,8,64]{3,2,1,0:T(8,128)(2,1)S(1)}, bf16[64,4,8,64]{3,2,1,0:T(8,128)(2,1)}, u32[]{:S(2)}) copy-start(bf16[64,4,8,64]{3,2,1,0:T(8,128)(2,1)} %reduce-scatter.4.cloned.1.call-done) | copy-start | bytes 786436
Sparse Core Ops, SparseCore 0:
  85.7 88.6 reduce-scatter.3
  177.3 79.6 all-gather.3
  263.4 68.3 reduce-scatter.5
  334.6 74.2 all-gather.5
  415.7 69.4 reduce-scatter.7
where the time goes:
time: 498 us; the launch traced here: 494 us
  waiting for transfers between devices  279 us (56%)
  blocking collectives  72.7 us (15%)
  local copies, waits for them, and re-layouts  60.4 us (12%)
  other arithmetic  42.4 us (9%)
  matrix products  16.8 us (3%)
  between operations  14.1 us (3%)
  starting transfers between devices  8.45 us (2%)
    reduce_scatter x1, waiting for transfers between devices, on_device(): lax.psum_scatter(terms.astype(jnp.bfloat16), 'dp', scatter_dimension=0, t...  82.9 us
    reduce_scatter x1, waiting for transfers between devices, on_device(): lax.psum_scatter(partial_out, 'tensor', scatter_dimension=2, tiled=True)  68.8 us
    all_gather x1, waiting for transfers between devices, on_device(): lax.all_gather(out_slices, 'dp', axis=0, tiled=True)  62.2 us
    all_gather x1, waiting for transfers between devices, on_device(): qkv_full = lax.all_gather(qkv_local, 'dp', axis=0, tiled=True)  50.6 us
    psum x1, blocking collectives, on_device(): inverse = lax.rsqrt(lax.psum(squared, 'tensor') / D + norm_epsilon)  28.5 us
    unnamed x26, local copies, waits for them, and re-layouts  28.3 us
    all_gather x1, blocking collectives, on_device(): all_ids = lax.all_gather(token_ids, 'dp', axis=0, tiled=True)  26.8 us
    unnamed x1, other arithmetic  22.4 us
  transfers between devices with their start and end apart: 6, of which 5 were waited for; matrix products, arithmetic and copies ran while one was open for 10% of the time, Pallas kernels for 0%

commit v1 on v0

--- a/solution.py
+++ b/solution.py
@@ -3,13 +3,23 @@
 import jax
 import jax.numpy as jnp
 from jax import lax
+from jax.experimental import pallas as pl
+from jax.experimental.pallas import tpu as pltpu
 from jax.sharding import PartitionSpec as P
 
 D = 8192
 QH = 32
 KVH = 4
 HD = 128
-
+QW = 4096
+KW = 512
+VOCAB_DEV = 9504
+SLOTS = 64
+GROUPS = 8
+TOK = 256
+FEAT = 512
+VCHUNK = 1920
+HALF = 2560
 
 beta_first = 0.9
 beta_second = 0.95
@@ -20,6 +30,9 @@
 bias_second = 1.0 - 0.95**50
 rope_base = 1000000.0
 norm_epsilon = 1e-06
+
+f32 = jnp.float32
+bf16 = jnp.bfloat16
 
 
 def adamw(master, moment_one, moment_two, gradient):
@@ -77,6 +90,166 @@
         "rngst,rtnd->rsngd", new_weights, values_new, preferred_element_type=jnp.float32
     )
     return mixed.astype(jnp.bfloat16).reshape(row_total, step_total, -1)
+
+
+def iota(shape, axis):
+    return lax.broadcasted_iota(jnp.int32, shape, axis)
+
+
+def lower_triangle(size):
+    return (iota((size, size), 0) <= iota((size, size), 1)).astype(bf16)
+
+
+def lookup_kernel(ids_ref, table_ref, out_ref, acc_ref, pick_ref):
+    step = pl.program_id(0)
+
+    @pl.when(step == 0)
+    def _():
+        local = ids_ref[...]
+        mine = (local >= 0) & (local < VOCAB_DEV)
+        rank = jnp.dot(
+            mine.astype(f32).astype(bf16), lower_triangle(TOK), preferred_element_type=f32
+        )
+        rank = jnp.where(mine, rank, 0.0)
+        shifted = local.astype(f32) + 1.0
+        for group in range(GROUPS):
+            slot = iota((SLOTS, TOK), 0).astype(f32) + 1.0
+            hit = rank[group : group + 1, :] == slot
+            value = jnp.where(hit, shifted[group : group + 1, :], 0.0)
+            pick = jnp.sum(value, axis=1, keepdims=True) - 1.0
+            pick_ref[pl.ds(group * SLOTS, SLOTS), :] = jnp.broadcast_to(
+                pick, (SLOTS, 128)
+            ).astype(jnp.int32)
+        acc_ref[...] = jnp.zeros_like(acc_ref)
+
+    slots = GROUPS * SLOTS
+    entry = iota((slots, VCHUNK), 1) + step * VCHUNK
+    chosen = jnp.where(entry == pick_ref[:, 0:1], 1.0, 0.0).astype(bf16)
+    dims = (((1,), (1,)), ((), ()))
+
+    @pl.when(step < pl.num_programs(0) - 1)
+    def _():
+        acc_ref[...] += lax.dot_general(chosen, table_ref[...], dims, preferred_element_type=f32)
+
+    @pl.when(step == pl.num_programs(0) - 1)
+    def _():
+        column = iota((FEAT, VCHUNK), 1) + step * VCHUNK
+        block = jnp.where(column < VOCAB_DEV, table_ref[...], jnp.zeros((), bf16))
+        total = acc_ref[...] + lax.dot_general(chosen, block, dims, preferred_element_type=f32)
+        out_ref[...] = total.astype(bf16)
+
+
+def lookup(local_ids, table):
+    steps = pl.cdiv(VOCAB_DEV, VCHUNK)
+    slots = GROUPS * SLOTS
+    return pl.pallas_call(
+        lookup_kernel,
+        grid=(steps,),
+        in_specs=[
+            pl.BlockSpec((GROUPS, TOK), lambda i: (0, 0)),
+            pl.BlockSpec((FEAT, VCHUNK), lambda i: (0, i)),
+        ],
+        out_specs=pl.BlockSpec((slots, FEAT), lambda i: (0, 0)),
+        out_shape=jax.ShapeDtypeStruct((slots, FEAT), bf16),
+        scratch_shapes=[pltpu.VMEM((slots, FEAT), f32), pltpu.VMEM((slots, 128), jnp.int32)],
+        compiler_params=pltpu.CompilerParams(vmem_limit_bytes=40 * 2**20),
+        cost_estimate=pl.CostEstimate(
+            flops=2 * slots * FEAT * VOCAB_DEV,
+            bytes_accessed=FEAT * VOCAB_DEV * 2,
+            transcendentals=0,
+        ),
+        name="lookup",
+    )(local_ids, table)
+
+
+def arrange_kernel(ids_ref, slots_ref, gain_ref, order_ref, hidden_ref, scaled_ref, squares_ref):
+    ids = jnp.broadcast_to(ids_ref[...], (GROUPS, TOK))
+    low = iota((GROUPS, TOK), 0) * VOCAB_DEV
+    owned = (ids >= low) & (ids < low + VOCAB_DEV)
+    rank = jnp.dot(owned.astype(f32).astype(bf16), lower_triangle(TOK), preferred_element_type=f32)
+    place = rank - 1.0 + (iota((GROUPS, TOK), 0) * SLOTS).astype(f32)
+    place = jnp.sum(jnp.where(owned, place, 0.0), axis=0, keepdims=True)
+    slots = GROUPS * SLOTS
+    chosen = jnp.where(iota((slots, TOK), 0).astype(f32) == place, 1.0, 0.0).astype(bf16)
+    hidden = lax.dot_general(
+        chosen, slots_ref[...], (((0,), (0,)), ((), ())), preferred_element_type=f32
+    )
+    hidden_ref[...] = hidden.astype(bf16)
+    squares = jnp.sum(hidden * hidden, axis=1, keepdims=True)
+    squares_ref[...] = jnp.broadcast_to(squares, (TOK, 128)).astype(bf16)
+    scaled = (hidden * gain_ref[...]).astype(bf16)
+    order = jnp.where(iota((FEAT, FEAT), 0) == order_ref[...], 1.0, 0.0).astype(bf16)
+    scaled_ref[...] = jnp.dot(scaled, order, preferred_element_type=f32).astype(bf16)
+
+
+def arrange(ids_row, slots, gain, order):
+    return pl.pallas_call(
+        arrange_kernel,
+        out_shape=(
+            jax.ShapeDtypeStruct((TOK, FEAT), bf16),
+            jax.ShapeDtypeStruct((TOK, FEAT), bf16),
+            jax.ShapeDtypeStruct((TOK, 128), bf16),
+        ),
+        compiler_params=pltpu.CompilerParams(vmem_limit_bytes=40 * 2**20),
+        name="arrange",
+    )(ids_row, slots, gain, order)
+
+
+def project_kernel(own_ref, pair_ref, squares_ref, *rest):
+    shards, out_ref = rest[:-1], rest[-1]
+    own = jnp.concatenate([shard[0:64, :] for shard in shards], axis=0)
+    pair = jnp.concatenate([shard[64:128, :] for shard in shards], axis=0)
+    total = jnp.dot(own_ref[...], own, preferred_element_type=f32)
+    total = total + jnp.dot(pair_ref[...], pair, preferred_element_type=f32)
+    out_ref[...] = total.astype(bf16)
+
+    @pl.when(pl.program_id(0) == pl.num_programs(0) - 1)
+    def _():
+        out_ref[:, 256:384] = squares_ref[...]
+
+
+def project(own, pair, squares, shards):
+    width = HALF + 128
+    steps = width // 384
+    return pl.pallas_call(
+        project_kernel,
+        grid=(steps,),
+        in_specs=[
+            pl.BlockSpec((TOK, FEAT), lambda i: (0, 0)),
+            pl.BlockSpec((TOK, FEAT), lambda i: (0, 0)),
+            pl.BlockSpec((TOK, 128), lambda i: (0, 0)),
+        ]
+        + [pl.BlockSpec((128, 384), lambda i: (0, i)) for _ in shards],
+        out_specs=pl.BlockSpec((TOK, 384), lambda i: (0, i)),
+        out_shape=jax.ShapeDtypeStruct((TOK, width), bf16),
+        compiler_params=pltpu.CompilerParams(vmem_limit_bytes=40 * 2**20),
+        cost_estimate=pl.CostEstimate(
+            flops=2 * TOK * 1024 * HALF, bytes_accessed=1024 * HALF * 2, transcendentals=0
+        ),
+        name="project",
+    )(own, pair, squares, *shards)
+
+
+def dp_permute(value, dx, dz):
+    pairs = []
+    for source in range(8):
+        x, z = source // 2, source % 2
+        pairs.append((source, ((x + dx) % 4) * 2 + (z ^ dz)))
+    return lax.ppermute(value, "dp", pairs)
+
+
+def tensor_permute(value, dz, dy, dc):
+    pairs = []
+    for source in range(16):
+        z, y, c = source // 8, (source // 2) % 4, source % 2
+        pairs.append((source, (z ^ dz) * 8 + ((y + dy) % 4) * 2 + (c ^ dc)))
+    return lax.ppermute(value, "tensor", pairs)
+
+
+def dp_gather(shard):
+    other = dp_permute(shard, 0, 1)
+    found = [shard] + [dp_permute(shard, step, 0) for step in (1, 3, 2)]
+    return found + [other] + [dp_permute(other, step, 0) for step in (1, 3, 2)]
 
 
 def on_device(
@@ -94,48 +267,59 @@
     lengths,
     kv_cache,
 ):
+    group_rows, step_total = token_ids.shape
+    my_group = lax.axis_index("dp")
+    my_tensor = lax.axis_index("tensor")
+    my_x, my_z = my_group // 2, my_group % 2
+    my_core = my_tensor % 2
+
+    ids_row = token_ids.reshape(1, TOK)
+    all_ids = lax.all_to_all(
+        jnp.broadcast_to(ids_row, (GROUPS, TOK)), "dp", split_axis=0, concat_axis=0, tiled=True
+    )
     new_qkv = adamw(qkv_master, qkv_moment1, qkv_moment2, qkv_grad)
-    new_out = adamw(out_master, out_moment1, out_moment2, out_grad)
-    qkv_local = new_qkv[0].astype(jnp.bfloat16)
-    out_local = new_out[0].astype(jnp.bfloat16)
-    group_rows, step_total = token_ids.shape
-    tensor_count = lax.axis_size("tensor")
-    vocab_local = embed_table.shape[0]
-    my_group = lax.axis_index("dp")
-    all_ids = lax.all_gather(token_ids, "dp", axis=0, tiled=True)
-    offset_ids = all_ids - my_group * vocab_local
-    inside = (offset_ids >= 0) & (offset_ids < vocab_local)
-    looked = jnp.take(embed_table, jnp.clip(offset_ids, 0, vocab_local - 1), axis=0)
-    terms = jnp.where(inside[:, :, None, None], looked.astype(jnp.float32), 0.0)
-    hidden = lax.psum_scatter(terms.astype(jnp.bfloat16), "dp", scatter_dimension=0, tiled=True)
-    hidden_float = hidden.astype(jnp.float32)
-    squared = jnp.sum(hidden_float * hidden_float, axis=(2, 3))
-    inverse = lax.rsqrt(lax.psum(squared, "tensor") / D + norm_epsilon)
-    normed = (hidden_float * inverse[:, :, None, None] * norm_gain).astype(jnp.bfloat16)
-    token_count = group_rows * step_total
-    normed_flat = normed.reshape(token_count, -1)
-    qkv_full = lax.all_gather(qkv_local, "dp", axis=0, tiled=True)
-    qkv_flat = qkv_full.reshape(-1, qkv_full.shape[-1])
-    own_tokens = token_count // tensor_count
-    projected = lax.psum_scatter(
-        jnp.dot(normed_flat, qkv_flat, preferred_element_type=jnp.float32),
-        "tensor",
-        scatter_dimension=0,
-        tiled=True,
-    )
+    qkv_local = new_qkv[0].astype(bf16)[0]
+    kept = lax.dynamic_slice(qkv_local, (0, my_core * HALF), (64, HALF))
+    given = lax.dynamic_slice(qkv_local, (0, (1 - my_core) * HALF), (64, HALF))
+    qkv_shard = jnp.concatenate([kept, tensor_permute(given, 0, 0, 1)], axis=0)
+    qkv_shards = dp_gather(qkv_shard)
+
+    table = embed_table.transpose(1, 2, 0).reshape(FEAT, VOCAB_DEV)
+    sent = lookup(all_ids - my_group * VOCAB_DEV, table)
+    received = lax.all_to_all(
+        sent.reshape(GROUPS, SLOTS, FEAT), "dp", split_axis=0, concat_axis=0, tiled=True
+    ).reshape(GROUPS * SLOTS, FEAT)
+    blocks = jnp.stack(
+        [
+            ((my_x + 4 - step) % 4) * 2 + (my_z + flip) % 2
+            for flip in (0, 1)
+            for step in (0, 1, 3, 2)
+        ]
+    )
+    order = (blocks[:, None] * 64 + jnp.arange(64)[None, :]).reshape(1, FEAT).astype(jnp.int32)
+    hidden, scaled, squares = arrange(ids_row, received, norm_gain.reshape(1, FEAT), order)
+    scaled_pair = tensor_permute(scaled, 0, 0, 1)
+
+    partial = project(scaled, scaled_pair, squares, qkv_shards)
+    parts = lax.all_to_all(
+        partial.reshape(16, 16, HALF + 128), "tensor", split_axis=0, concat_axis=0, tiled=True
+    )
+    summed = jnp.sum(parts.astype(f32).reshape(8, 2, 16, HALF + 128), axis=0)
+    square_sum = summed[0, :, HALF] + summed[1, :, HALF]
+    inverse = lax.rsqrt(square_sum / D + norm_epsilon)
+    projected = jnp.concatenate([summed[0, :, :HALF], summed[1, :, :HALF]], axis=-1)
+    projected = projected * inverse[:, None]
+
+    own_tokens = 16
     own_rows = own_tokens // step_total
     projected = projected.reshape(own_rows, step_total, -1)
-    query_width = QH * HD
-    key_width = KVH * HD
-    query = projected[..., :query_width].reshape(own_rows, step_total, QH, HD)
-    key_new = projected[..., query_width : query_width + key_width].reshape(
-        own_rows, step_total, KVH, HD
-    )
-    value_new = projected[..., query_width + key_width :].reshape(own_rows, step_total, KVH, HD)
+    query = projected[..., :QW].reshape(own_rows, step_total, QH, HD)
+    key_new = projected[..., QW : QW + KW].reshape(own_rows, step_total, KVH, HD)
+    value_new = projected[..., QW + KW :].reshape(own_rows, step_total, KVH, HD)
     positions = lengths[:, None] + jnp.arange(step_total)[None, :]
-    query = rotate(query, positions).astype(jnp.bfloat16)
-    key_new = rotate(key_new, positions).astype(jnp.bfloat16)
-    value_new = value_new.astype(jnp.bfloat16)
+    query = rotate(query, positions).astype(bf16)
+    key_new = rotate(key_new, positions).astype(bf16)
+    value_new = value_new.astype(bf16)
     fresh_kv = jnp.concatenate([key_new, value_new], axis=-1)
     attended = attend(
         query.reshape(own_rows, step_total, KVH, QH // KVH, HD),
@@ -144,17 +328,33 @@
         kv_cache,
         lengths,
     )
-    attended_flat = attended.reshape(own_tokens, query_width)
-    heads_part = lax.all_to_all(attended_flat, "tensor", split_axis=1, concat_axis=0, tiled=True)
-    out_slices = lax.all_to_all(out_local, "tensor", split_axis=2, concat_axis=1, tiled=True)
-    partial_out = jnp.einsum(
-        "tq,kjq->tkj",
-        heads_part,
-        lax.all_gather(out_slices, "dp", axis=0, tiled=True),
-        preferred_element_type=jnp.float32,
-    )
-    output = lax.psum_scatter(partial_out, "tensor", scatter_dimension=2, tiled=True)
-    decoded = (hidden_float + output.reshape(hidden_float.shape)).astype(jnp.bfloat16)
+    attended = attended.reshape(own_tokens, QW)
+
+    new_out = adamw(out_master, out_moment1, out_moment2, out_grad)
+    out_full = lax.all_gather(new_out[0].astype(bf16), "dp", axis=0, tiled=True).reshape(FEAT, QW)
+
+    other = tensor_permute(attended, 1, 0, 0)
+    both = jnp.stack([attended, other])
+    quad = jnp.stack([both] + [tensor_permute(both, 0, step, 0) for step in (1, 2, 3)])
+    everyone = jnp.stack([quad, tensor_permute(quad, 0, 0, 1)])
+    everyone = everyone.reshape(2, 4, 2, 16, QW)
+    tensor_z, tensor_y = my_tensor // 8, (my_tensor // 2) % 4
+    heads = jnp.zeros((16, 16, QW), bf16)
+    for core in range(2):
+        for step in range(4):
+            for flip in range(2):
+                source = (
+                    ((tensor_z + flip) % 2) * 8
+                    + ((tensor_y + 4 - step) % 4) * 2
+                    + (my_core + core) % 2
+                )
+                heads = lax.dynamic_update_slice(
+                    heads, everyone[core, step, flip][None], (source, 0, 0)
+                )
+    output = lax.dot_general(
+        heads.reshape(TOK, QW), out_full, (((1,), (1,)), ((), ())), preferred_element_type=f32
+    )
+    decoded = (hidden.astype(f32) + output).astype(bf16).reshape(group_rows, step_total, 8, 64)
     return (
         decoded,
         fresh_kv,

time: 498 us -> 249 us (0.50)
  waiting for transfers between devices: 279 us -> 138 us
  blocking collectives: 72.7 us -> 0 us
  local copies, waits for them, and re-layouts: 60.4 us -> 8.49 us
  starting transfers between devices: 8.45 us -> 50.8 us
  other arithmetic: 42.4 us -> 13.7 us
  Pallas kernels: 0 us -> 15.9 us
  matrix products: 16.8 us -> 7.33 us
    reduce_scatter x3 -> x0, waiting for transfers between devices: 166 us -> none  [the longest x1 82.9 us: on_device(): lax.psum_scatter(terms.astype(jnp.bfloat16), 'dp', scatter_dimension=0, t...]
    all_gather x2 -> x1, waiting for transfers between devices: 113 us -> 64.9 us  [on_device(): lax.all_gather(new_out[0].astype(bf16), 'dp', axis=0, tiled=True)]
    ppermute x0 -> x14, waiting for transfers between devices: none -> 47.6 us  [the longest x7 35.7 us: dp_permute(): return lax.ppermute(value, 'dp', pairs)]
    ppermute x0 -> x14, starting transfers between devices: none -> 29.4 us  [the longest x7 20.9 us: dp_permute(): return lax.ppermute(value, 'dp', pairs)]
    psum x1 -> x0, blocking collectives: 28.5 us -> none  [on_device(): inverse = lax.rsqrt(lax.psum(squared, 'tensor') / D + norm_epsilon)]
    all_gather x1 -> x0, blocking collectives: 26.8 us -> none  [on_device(): all_ids = lax.all_gather(token_ids, 'dp', axis=0, tiled=True)]
    all_to_all x1 -> x3, waiting for transfers between devices: 0.01 us -> 25.2 us  [the longest x1 18.8 us: on_device(): lax.all_to_all(partial.reshape(16, 16, HALF + 128), 'tensor', split_axis=...]
    unnamed x26 -> x15, local copies, waits for them, and re-layouts: 28.3 us -> 4.6 us
  transfers between devices with their start and end apart: 6 -> 18, of which waited for: 5 -> 12; matrix products, arithmetic and copies ran while one was open for 10% -> 5% of each run, Pallas kernels for 0% -> 4%
where the time goes in v1:
time: 249 us
  waiting for transfers between devices  138 us (55%)
  starting transfers between devices  50.8 us (20%)
  Pallas kernels  15.9 us (6%)
  between operations  14.7 us (6%)
  other arithmetic  13.7 us (6%)
  local copies, waits for them, and re-layouts  8.49 us (3%)
  matrix products  7.33 us (3%)
    all_gather x1, waiting for transfers between devices, on_device(): lax.all_gather(new_out[0].astype(bf16), 'dp', axis=0, tiled=True)  64.9 us
    ppermute x7, waiting for transfers between devices, dp_permute(): return lax.ppermute(value, 'dp', pairs)  35.7 us
    ppermute x7, starting transfers between devices, dp_permute(): return lax.ppermute(value, 'dp', pairs)  20.9 us
    all_to_all x1, waiting for transfers between devices, on_device(): lax.all_to_all(partial.reshape(16, 16, HALF + 128), 'tensor', split_axis=...  18.8 us
    ppermute x7, waiting for transfers between devices, tensor_permute(): return lax.ppermute(value, 'tensor', pairs)  11.9 us
    pallas_call x1, Pallas kernels, lookup(): pl.pallas_call(lookup_kernel, grid=(steps,), in_specs=[pl.BlockSpec((GROU...  8.98 us
    ppermute x7, starting transfers between devices, tensor_permute(): return lax.ppermute(value, 'tensor', pairs)  8.48 us
    all_to_all x1, starting transfers between devices, on_device(): lax.all_to_all(jnp.broadcast_to(ids_row, (GROUPS, TOK)), 'dp', split_axis...  8.16 us
  transfers between devices with their start and end apart: 18, of which 12 were waited for; matrix products, arithmetic and copies ran while one was open for 5% of the time, Pallas kernels for 4%

profile of v1, /device:TPU:1, one launch (start us, length us, event | category | flops | bytes accessed | tf_op | source)
XLA Modules:
  0.0 248.6 jit_solution(7226476253924812362)
XLA Ops:
  7.2 0.8 copy.50
  7.9 0.1 broadcast_in_dim.20
  8.0 0.6 broadcast_in_dim.21
  8.7 8.2 %all-to-all-start = ((s32[8,1,256]{2,1,0:T(1,128)}), s32[8,1,256]{2,1,0:T(1,128)S(1)}, u32[]{:S(2)}, u32[]{:S(2)}) async-start(s32[8,1,256]{2,1,0:T(1,128)} %broadcast_in_dim.21), calls=%async_computation | async-start | bytes 16384 | tf_op jit(solution)/shard_map/all_to_all | solution.py:277
  16.8 4.9 %fusion.71 = (bf16[1,64,5120]{2,1,0:T(8,128)(2,1)S(1)}, f32[1,64,5120]{2,1,0:T(8,128)}, f32[1,64,5120]{2,1,0:T(8,128)}, f32[1,64,5120]{2,1,0:T(8,128)}) fusion(f32[1,64,5120]{2,1,0:T(8,128)} %param.13, bf16[1,64,5120]{2,1,0:T(8,128)(2,1)} %param.16, f32[1,64,5120]{2,1,0:T(8,128)} %param.14, f32[1,64,5120]{2,1,0:T(8,128)} %param.15), kind=kLoop, calls=%fused_computation.112 | loop fusion | flops 5570560 | bytes 9175040 | tf_op jit(solution)/shard_map/convert_element_type | solution.py:281
  21.8 1.0 collective-permute-start.1
  22.8 0.1 reshape.248.ids_ref
  22.9 0.1 stack.62
  23.0 0.4 all-to-all-done
  23.4 3.8 %copy-done = bf16[9504,8,64]{0,2,1:T(8,128)(2,1)S(1)} copy-done((bf16[9504,8,64]{0,2,1:T(8,128)(2,1)S(1)}, bf16[9504,8,64]{0,2,1:T(8,128)(2,1)}, u32[]{:S(2)}) %copy-start) | copy-done | bytes 9732120
  27.1 9.0 %lookup.1 = bf16[512,512]{1,0:T(8,128)(2,1)} custom-call(s32[8,256]{1,0:T(8,128)S(1)} %fusion.64.ids_ref, bf16[512,9504]{1,0:T(8,128)(2,1)S(1)} %bitcast.163), custom_call_target="tpu_custom_call" | custom-call | flops 4982833152 | bytes 9732096 | tf_op jit(solution)/shard_map/lookup/pallas_call | solution.py:145
  36.1 6.7 %all-to-all-start.1 = ((bf16[8,64,512]{2,1,0:T(8,128)(2,1)}), bf16[8,64,512]{2,1,0:T(8,128)(2,1)S(1)}, u32[]{:S(2)}, u32[]{:S(2)}) async-start(bf16[8,64,512]{2,1,0:T(8,128)(2,1)} %bitcast.3), calls=%async_computation.1 | async-start | bytes 1048576 | tf_op jit(solution)/shard_map/all_to_all | solution.py:289
  42.9 3.0 %collective-permute-start.5 = (bf16[128,2560]{1,0:T(8,128)(2,1)S(1)}, bf16[128,2560]{1,0:T(8,128)(2,1)S(1)}, u32[]{:S(2)}, u32[]{:S(2)}) collective-permute-start(bf16[128,2560]{1,0:T(8,128)(2,1)S(1)} %pad_maximum_fusion.1.rest_0_), channel_id=1, source_target_pairs={{0,16},{16,0},{32,48},{48,32},{64,80},{80,64},{96,112},{112,96},{1... | collective-permute-start | bytes 1966088 | tf_op jit(solution)/shard_map/ppermute | solution.py:238
  45.9 1.2 collective-permute-start.2
  47.1 0.1 iota_add_fusion
  47.2 0.1 add.462.order_ref
  47.3 0.1 reshape.252.gain_ref
  47.4 6.0 %all-to-all-done.1 = bf16[8,64,512]{2,1,0:T(8,128)(2,1)S(1)} async-done(((bf16[8,64,512]{2,1,0:T(8,128)(2,1)}), bf16[8,64,512]{2,1,0:T(8,128)(2,1)S(1)}, u32[]{:S(2)}, u32[]{:S(2)}) %all-to-all-start.1) | async-done | bytes 524320 | tf_op jit(solution)/shard_map/all_to_all | solution.py:289
  53.4 0.7 arrange.1
  54.1 1.7 collective-permute-start
  55.9 1.4 collective-permute-start.3
  57.3 0.7 collective-permute-start.4
  57.9 8.1 %collective-permute-done.5.rest_4_ = bf16[128,2560]{1,0:T(8,128)(2,1)S(1)} collective-permute-done((bf16[128,2560]{1,0:T(8,128)(2,1)S(1)}, bf16[128,2560]{1,0:T(8,128)(2,1)S(1)}, u32[]{:S(2)}, u32[]{:S(2)}) %collective-permute-start.5) | collective-permute-done | bytes 655392 | tf_op jit(solution)/shard_map/ppermute | solution.py:238
  66.0 1.2 collective-permute-start.6
  67.2 1.5 collective-permute-start.7
  68.7 11.9 %collective-permute-start.8 = (bf16[128,2560]{1,0:T(8,128)(2,1)S(1)}, bf16[128,2560]{1,0:T(8,128)(2,1)S(1)}, u32[]{:S(2)}, u32[]{:S(2)}) collective-permute-start(bf16[128,2560]{1,0:T(8,128)(2,1)S(1)} %collective-permute-done.5.rest_4_), channel_id=1, source_target_pairs={{0,64},{16,80},{32,96},{48,112},{64,0},{80,16},{96,32},{112,48},{1... | collective-permute-start | bytes 1966088 | tf_op jit(solution)/shard_map/ppermute | solution.py:238
  80.6 15.0 %collective-permute-done.6.rest_5_ = bf16[128,2560]{1,0:T(8,128)(2,1)S(1)} collective-permute-done((bf16[128,2560]{1,0:T(8,128)(2,1)S(1)}, bf16[128,2560]{1,0:T(8,128)(2,1)S(1)}, u32[]{:S(2)}, u32[]{:S(2)}) %collective-permute-start.6) | collective-permute-done | bytes 655392 | tf_op jit(solution)/shard_map/ppermute | solution.py:238
  95.7 4.6 %collective-permute-done.7.rest_6_ = bf16[128,2560]{1,0:T(8,128)(2,1)S(1)} collective-permute-done((bf16[128,2560]{1,0:T(8,128)(2,1)S(1)}, bf16[128,2560]{1,0:T(8,128)(2,1)S(1)}, u32[]{:S(2)}, u32[]{:S(2)}) %collective-permute-start.7) | collective-permute-done | bytes 655392 | tf_op jit(solution)/shard_map/ppermute | solution.py:238
  100.3 8.0 %collective-permute-done.8.rest_7_ = bf16[128,2560]{1,0:T(8,128)(2,1)S(1)} collective-permute-done((bf16[128,2560]{1,0:T(8,128)(2,1)S(1)}, bf16[128,2560]{1,0:T(8,128)(2,1)S(1)}, u32[]{:S(2)}, u32[]{:S(2)}) %collective-permute-start.8) | collective-permute-done | bytes 655392 | tf_op jit(solution)/shard_map/ppermute | solution.py:238
  108.3 6.2 %project.1 = bf16[256,2688]{1,0:T(8,128)(2,1)} custom-call(bf16[256,512]{1,0:T(8,128)(2,1)S(1)} %get-tuple-element.12.own_ref, bf16[256,512]{1,0:T(8,128)(2,1)S(1)} %collective-permute-done.pair_ref, bf16[256,128]{1,0:T(8,128)(2,1)S(1)} %get-tuple-element.13.squares_ref, bf16[128,2560]{1,0:T(8,128)(2,1)S(1)} %pad_maximum_fusion.1.rest_0_, ...), custom_call_target="tpu_custom_call" | custom-call | flops 1342177280 | bytes 5242880 | tf_op jit(solution)/shard_map/project/pallas_call | solution.py:214
  114.5 6.3 %all-to-all-start.2 = ((bf16[16,16,2688]{2,1,0:T(8,128)(2,1)}), bf16[16,16,2688]{2,1,0:T(8,128)(2,1)S(1)}, u32[]{:S(2)}, u32[]{:S(2)}) async-start(bf16[16,16,2688]{2,1,0:T(8,128)(2,1)} %bitcast.15), calls=%async_computation.2 | async-start | bytes 2752512 | tf_op jit(solution)/shard_map/all_to_all | solution.py:304
  120.8 0.2 all-gather.2.cloned.1.call-start
  121.2 0.1 multiply_cosine_fusion
  121.3 18.8 %all-to-all-done.2 = bf16[16,16,2688]{2,1,0:T(8,128)(2,1)S(1)} async-done(((bf16[16,16,2688]{2,1,0:T(8,128)(2,1)}), bf16[16,16,2688]{2,1,0:T(8,128)(2,1)S(1)}, u32[]{:S(2)}, u32[]{:S(2)}) %all-to-all-start.2) | async-done | bytes 1376288 | tf_op jit(solution)/shard_map/all_to_all | solution.py:304
  140.2 0.2 convert_reduce_fusion
  140.4 0.1 fusion.63
  140.6 0.1 rsqrt.11
  140.7 0.1 maximum_multiply_fusion
  140.8 0.2 reshape.256
  141.0 0.1 fusion.34
  141.2 0.1 subtract_convert_fusion.1
  141.3 2.4 fusion.75
  143.7 0.8 fusion.76
  144.5 0.1 fusion.54
  144.6 0.3 fusion.31
  144.9 0.3 convolution_bitcast_fusion
  145.2 0.5 fusion.24
  145.8 0.4 collective-permute-start.9
  146.2 0.7 stack_reshape_reshape.3
  146.9 3.4 %collective-permute-done.9 = bf16[16,4096]{1,0:T(8,128)(2,1)} collective-permute-done((bf16[16,4096]{1,0:T(8,128)(2,1)S(1)}, bf16[16,4096]{1,0:T(8,128)(2,1)}, u32[]{:S(2)}, u32[]{:S(2)}) %collective-permute-start.9) | collective-permute-done | bytes 131104 | tf_op jit(solution)/shard_map/ppermute | solution.py:246
  150.3 1.7 fusion.66
  152.0 2.7 %collective-permute-start.11 = (bf16[2,16,4096]{2,1,0:T(8,128)(2,1)}, bf16[2,16,4096]{2,1,0:T(8,128)(2,1)}, u32[]{:S(2)}, u32[]{:S(2)}) collective-permute-start(bf16[2,16,4096]{2,1,0:T(8,128)(2,1)} %get-tuple-element.39), channel_id=1, source_target_pairs={{0,4},{1,5},{2,6},{3,7},{4,0},{5,1},{6,2},{7,3},{8,12},{9,13},{10,... | collective-permute-start | bytes 786440 | tf_op jit(solution)/shard_map/ppermute | solution.py:246
  154.8 1.0 collective-permute-start.12
  155.8 3.6 %fusion.68 = (bf16[1,64,4096]{2,1,0:T(8,128)(2,1)}, f32[1,64,4096]{2,1,0:T(8,128)}, f32[1,64,4096]{2,1,0:T(8,128)}, f32[1,64,4096]{2,1,0:T(8,128)}) fusion(f32[1,64,4096]{2,1,0:T(8,128)S(1)} %copy-done.1, bf16[1,64,4096]{2,1,0:T(8,128)(2,1)S(1)} %copy-done.4, f32[1,64,4096]{2,1,0:T(8,128)S(1)} %copy-done.2, f32[1,64,4096]{2,1,0:T(8,128)} %param.19), kind=kLoop, calls=%fused_computation.111 | loop fusion | flops 4456448 | bytes 7340032 | tf_op jit(solution)/shard_map/convert_element_type | solution.py:334
  159.7 0.7 pad_maximum_fusion.4
  160.4 5.9 %collective-permute-done.11 = bf16[2,16,4096]{2,1,0:T(8,128)(2,1)} collective-permute-done((bf16[2,16,4096]{2,1,0:T(8,128)(2,1)}, bf16[2,16,4096]{2,1,0:T(8,128)(2,1)}, u32[]{:S(2)}, u32[]{:S(2)}) %collective-permute-start.11) | collective-permute-done | bytes 262176 | tf_op jit(solution)/shard_map/ppermute | solution.py:246
  166.3 0.6 collective-permute-done.12
  167.0 1.3 pad_maximum_fusion
  168.3 1.6 collective-permute-start.13
  169.9 0.2 broadcast_in_dim.22
  170.3 1.9 collective-permute-done.13
  172.4 64.9 %all-gather.2.cloned.1.call-done = bf16[8,64,4096]{2,1,0:T(8,128)(2,1)} async-done(((bf16[1,64,4096]{2,1,0:T(8,128)(2,1)}), bf16[8,64,4096]{2,1,0:T(8,128)(2,1)}) %all-gather.2.cloned.1.call-update) | async-done | bytes 4194320 | tf_op jit(solution)/shard_map/all_gather | solution.py:334
  237.2 3.5 %fusion.17 = bf16[256,512]{1,0:T(8,128)(2,1)S(1)} fusion(bf16[256,4096]{1,0:T(8,128)(2,1)S(1)} %bitcast.165, bf16[512,4096]{1,0:T(8,128)(2,1)} %bitcast.174, bf16[256,512]{1,0:T(8,128)(2,1)S(1)} %get-tuple-element.11), kind=kOutput, calls=%fused_computation.18 | convolution fusion | flops 1074135040 | bytes 6815744 | tf_op jit(solution)/shard_map/dot_general | solution.py:354
  240.7 1.1 reshape.260
  (58 shorter events, 0.9 us)
Async XLA Ops:
  8.7 14.7 %all-to-all-start = ((s32[8,1,256]{2,1,0:T(1,128)}), s32[8,1,256]{2,1,0:T(1,128)S(1)}, u32[]{:S(2)}, u32[]{:S(2)}) async-start(s32[8,1,256]{2,1,0:T(1,128)} %broadcast_in_dim.21), calls=%async_computation | async-start | bytes 16384 | tf_op jit(solution)/shard_map/all_to_all | solution.py:277
  21.8 21.1 %collective-permute-start.1 = (bf16[64,2560]{1,0:T(8,128)(2,1)S(1)}, bf16[64,2560]{1,0:T(8,128)(2,1)S(1)}, u32[]{:S(2)}, u32[]{:S(2)}) collective-permute-start(bf16[64,2560]{1,0:T(8,128)(2,1)S(1)} %get-tuple-element.33), channel_id=1, source_target_pairs={{0,1},{1,0},{2,3},{3,2},{4,5},{5,4},{6,7},{7,6},{8,9},{9,8},{10,11... | collective-permute-start | bytes 983048 | tf_op jit(solution)/shard_map/ppermute | solution.py:246
  23.4 3.8 %copy-start = (bf16[9504,8,64]{0,2,1:T(8,128)(2,1)S(1)}, bf16[9504,8,64]{0,2,1:T(8,128)(2,1)}, u32[]{:S(2)}) copy-start(bf16[9504,8,64]{0,2,1:T(8,128)(2,1)} %param.21) | copy-start | bytes 29196292
  36.1 11.1 %copy-start.5 = (f32[8,64]{1,0:T(8,128)S(1)}, f32[8,64]{1,0:T(8,128)}, u32[]{:S(2)}) copy-start(f32[8,64]{1,0:T(8,128)} %param.22) | copy-start | bytes 6148
  36.1 17.3 %all-to-all-start.1 = ((bf16[8,64,512]{2,1,0:T(8,128)(2,1)}), bf16[8,64,512]{2,1,0:T(8,128)(2,1)S(1)}, u32[]{:S(2)}, u32[]{:S(2)}) async-start(bf16[8,64,512]{2,1,0:T(8,128)(2,1)} %bitcast.3), calls=%async_computation.1 | async-start | bytes 1048576 | tf_op jit(solution)/shard_map/all_to_all | solution.py:289
  42.9 23.1 %collective-permute-start.5 = (bf16[128,2560]{1,0:T(8,128)(2,1)S(1)}, bf16[128,2560]{1,0:T(8,128)(2,1)S(1)}, u32[]{:S(2)}, u32[]{:S(2)}) collective-permute-start(bf16[128,2560]{1,0:T(8,128)(2,1)S(1)} %pad_maximum_fusion.1.rest_0_), channel_id=1, source_target_pairs={{0,16},{16,0},{32,48},{48,32},{64,80},{80,64},{96,112},{112,96},{1... | collective-permute-start | bytes 1966088 | tf_op jit(solution)/shard_map/ppermute | solution.py:238
  45.9 22.8 %collective-permute-start.2 = (bf16[128,2560]{1,0:T(8,128)(2,1)S(1)}, bf16[128,2560]{1,0:T(8,128)(2,1)S(1)}, u32[]{:S(2)}, u32[]{:S(2)}) collective-permute-start(bf16[128,2560]{1,0:T(8,128)(2,1)S(1)} %pad_maximum_fusion.1.rest_0_), channel_id=1, source_target_pairs={{0,32},{16,48},{32,64},{48,80},{64,96},{80,112},{96,0},{112,16},{1... | collective-permute-start | bytes 1966088 | tf_op jit(solution)/shard_map/ppermute | solution.py:238
  54.1 13.1 %collective-permute-start = (bf16[256,512]{1,0:T(8,128)(2,1)S(1)}, bf16[256,512]{1,0:T(8,128)(2,1)S(1)}, u32[]{:S(2)}, u32[]{:S(2)}) collective-permute-start(bf16[256,512]{1,0:T(8,128)(2,1)S(1)} %get-tuple-element.12.own_ref), channel_id=1, source_target_pairs={{0,1},{1,0},{2,3},{3,2},{4,5},{5,4},{6,7},{7,6},{8,9},{9,8},{10,11... | collective-permute-start | bytes 786440 | tf_op jit(solution)/shard_map/ppermute | solution.py:246
  55.9 24.8 %collective-permute-start.3 = (bf16[128,2560]{1,0:T(8,128)(2,1)S(1)}, bf16[128,2560]{1,0:T(8,128)(2,1)S(1)}, u32[]{:S(2)}, u32[]{:S(2)}) collective-permute-start(bf16[128,2560]{1,0:T(8,128)(2,1)S(1)} %pad_maximum_fusion.1.rest_0_), channel_id=1, source_target_pairs={{0,96},{16,112},{32,0},{48,16},{64,32},{80,48},{96,64},{112,80},{1... | collective-permute-start | bytes 1966088 | tf_op jit(solution)/shard_map/ppermute | solution.py:238
  57.3 23.4 %collective-permute-start.4 = (bf16[128,2560]{1,0:T(8,128)(2,1)S(1)}, bf16[128,2560]{1,0:T(8,128)(2,1)S(1)}, u32[]{:S(2)}, u32[]{:S(2)}) collective-permute-start(bf16[128,2560]{1,0:T(8,128)(2,1)S(1)} %pad_maximum_fusion.1.rest_0_), channel_id=1, source_target_pairs={{0,64},{16,80},{32,96},{48,112},{64,0},{80,16},{96,32},{112,48},{1... | collective-permute-start | bytes 1966088 | tf_op jit(solution)/shard_map/ppermute | solution.py:238
  66.0 29.6 %collective-permute-start.6 = (bf16[128,2560]{1,0:T(8,128)(2,1)S(1)}, bf16[128,2560]{1,0:T(8,128)(2,1)S(1)}, u32[]{:S(2)}, u32[]{:S(2)}) collective-permute-start(bf16[128,2560]{1,0:T(8,128)(2,1)S(1)} %collective-permute-done.5.rest_4_), channel_id=1, source_target_pairs={{0,32},{16,48},{32,64},{48,80},{64,96},{80,112},{96,0},{112,16},{1... | collective-permute-start | bytes 1966088 | tf_op jit(solution)/shard_map/ppermute | solution.py:238
  67.2 33.1 %collective-permute-start.7 = (bf16[128,2560]{1,0:T(8,128)(2,1)S(1)}, bf16[128,2560]{1,0:T(8,128)(2,1)S(1)}, u32[]{:S(2)}, u32[]{:S(2)}) collective-permute-start(bf16[128,2560]{1,0:T(8,128)(2,1)S(1)} %collective-permute-done.5.rest_4_), channel_id=1, source_target_pairs={{0,96},{16,112},{32,0},{48,16},{64,32},{80,48},{96,64},{112,80},{1... | collective-permute-start | bytes 1966088 | tf_op jit(solution)/shard_map/ppermute | solution.py:238
  68.7 39.5 %collective-permute-start.8 = (bf16[128,2560]{1,0:T(8,128)(2,1)S(1)}, bf16[128,2560]{1,0:T(8,128)(2,1)S(1)}, u32[]{:S(2)}, u32[]{:S(2)}) collective-permute-start(bf16[128,2560]{1,0:T(8,128)(2,1)S(1)} %collective-permute-done.5.rest_4_), channel_id=1, source_target_pairs={{0,64},{16,80},{32,96},{48,112},{64,0},{80,16},{96,32},{112,48},{1... | collective-permute-start | bytes 1966088 | tf_op jit(solution)/shard_map/ppermute | solution.py:238
  114.5 6.6 %copy-start.6 = (s32[4]{0:T(128)S(1)}, s32[4]{0:T(128)}, u32[]{:S(2)}) copy-start(s32[4]{0:T(128)} %param.24) | copy-start | bytes 52
  114.5 25.7 %all-to-all-start.2 = ((bf16[16,16,2688]{2,1,0:T(8,128)(2,1)}), bf16[16,16,2688]{2,1,0:T(8,128)(2,1)S(1)}, u32[]{:S(2)}, u32[]{:S(2)}) async-start(bf16[16,16,2688]{2,1,0:T(8,128)(2,1)} %bitcast.15), calls=%async_computation.2 | async-start | bytes 2752512 | tf_op jit(solution)/shard_map/all_to_all | solution.py:304
  120.8 116.4 %all-gather.2.cloned.1.call-start = ((), (), s32[]{:S(2)}) async-start(), calls=%async_computation.3 | async-start | bytes 4718592 | tf_op jit(solution)/shard_map/all_gather | solution.py:334
  141.3 3.9 %copy-start.3 = (bf16[4,4,384,256]{3,2,1,0:T(8,128)(2,1)S(1)}, bf16[4,4,384,256]{3,2,1,0:T(8,128)(2,1)}, u32[]{:S(2)}) copy-start(bf16[4,4,384,256]{3,2,1,0:T(8,128)(2,1)} %param.25) | copy-start | bytes 9437188
  145.2 10.5 %copy-start.2 = (f32[1,64,4096]{2,1,0:T(8,128)S(1)}, f32[1,64,4096]{2,1,0:T(8,128)}, u32[]{:S(2)}) copy-start(f32[1,64,4096]{2,1,0:T(8,128)} %param.18) | copy-start | bytes 3145732
  145.2 10.5 %copy-start.4 = (bf16[1,64,4096]{2,1,0:T(8,128)(2,1)S(1)}, bf16[1,64,4096]{2,1,0:T(8,128)(2,1)}, u32[]{:S(2)}) copy-start(bf16[1,64,4096]{2,1,0:T(8,128)(2,1)} %param.20) | copy-start | bytes 1572868
  145.7 10.1 %copy-start.1 = (f32[1,64,4096]{2,1,0:T(8,128)S(1)}, f32[1,64,4096]{2,1,0:T(8,128)}, u32[]{:S(2)}) copy-start(f32[1,64,4096]{2,1,0:T(8,128)} %param.17) | copy-start | bytes 3145732
  145.8 4.5 %collective-permute-start.9 = (bf16[16,4096]{1,0:T(8,128)(2,1)S(1)}, bf16[16,4096]{1,0:T(8,128)(2,1)}, u32[]{:S(2)}, u32[]{:S(2)}) collective-permute-start(bf16[16,4096]{1,0:T(8,128)(2,1)S(1)} %reshape_reshape.3), channel_id=1, source_target_pairs={{0,8},{1,9},{2,10},{3,11},{4,12},{5,13},{6,14},{7,15},{8,0},{9,1},... | collective-permute-start | bytes 393224 | tf_op jit(solution)/shard_map/ppermute | solution.py:246
  152.0 8.3 %collective-permute-start.10 = (bf16[2,16,4096]{2,1,0:T(8,128)(2,1)}, bf16[2,16,4096]{2,1,0:T(8,128)(2,1)}, u32[]{:S(2)}, u32[]{:S(2)}) collective-permute-start(bf16[2,16,4096]{2,1,0:T(8,128)(2,1)} %get-tuple-element.39), channel_id=1, source_target_pairs={{0,2},{1,3},{2,4},{3,5},{4,6},{5,7},{6,0},{7,1},{8,10},{9,11},{10,... | collective-permute-start | bytes 786440 | tf_op jit(solution)/shard_map/ppermute | solution.py:246
  152.0 14.3 %collective-permute-start.11 = (bf16[2,16,4096]{2,1,0:T(8,128)(2,1)}, bf16[2,16,4096]{2,1,0:T(8,128)(2,1)}, u32[]{:S(2)}, u32[]{:S(2)}) collective-permute-start(bf16[2,16,4096]{2,1,0:T(8,128)(2,1)} %get-tuple-element.39), channel_id=1, source_target_pairs={{0,4},{1,5},{2,6},{3,7},{4,0},{5,1},{6,2},{7,3},{8,12},{9,13},{10,... | collective-permute-start | bytes 786440 | tf_op jit(solution)/shard_map/ppermute | solution.py:246
  154.8 12.2 %collective-permute-start.12 = (bf16[2,16,4096]{2,1,0:T(8,128)(2,1)}, bf16[2,16,4096]{2,1,0:T(8,128)(2,1)}, u32[]{:S(2)}, u32[]{:S(2)}) collective-permute-start(bf16[2,16,4096]{2,1,0:T(8,128)(2,1)} %get-tuple-element.39), channel_id=1, source_target_pairs={{0,6},{1,7},{2,0},{3,1},{4,2},{5,3},{6,4},{7,5},{8,14},{9,15},{10,... | collective-permute-start | bytes 786440 | tf_op jit(solution)/shard_map/ppermute | solution.py:246
  168.3 3.9 %collective-permute-start.13 = (bf16[4,2,16,4096]{3,2,1,0:T(8,128)(2,1)S(1)}, bf16[4,2,16,4096]{3,2,1,0:T(8,128)(2,1)S(1)}, u32[]{:S(2)}, u32[]{:S(2)}) collective-permute-start(bf16[4,2,16,4096]{3,2,1,0:T(8,128)(2,1)S(1)} %get-tuple-element.30), channel_id=1, source_target_pairs={{0,1},{1,0},{2,3},{3,2},{4,5},{5,4},{6,7},{7,6},{8,9},{9,8},{10,11... | collective-permute-start | bytes 3145736 | tf_op jit(solution)/shard_map/ppermute | solution.py:246
Sparse Core Ops, SparseCore 0:
  159.5 77.6 all-gather.1

commit v2 on v1

--- a/solution.py
+++ b/solution.py
@@ -20,6 +20,8 @@
 FEAT = 512
 VCHUNK = 1920
 HALF = 2560
+COLS = 896
+VMEM = 56 * 2**20
 
 beta_first = 0.9
 beta_second = 0.95
@@ -152,12 +154,8 @@
         out_specs=pl.BlockSpec((slots, FEAT), lambda i: (0, 0)),
         out_shape=jax.ShapeDtypeStruct((slots, FEAT), bf16),
         scratch_shapes=[pltpu.VMEM((slots, FEAT), f32), pltpu.VMEM((slots, 128), jnp.int32)],
-        compiler_params=pltpu.CompilerParams(vmem_limit_bytes=40 * 2**20),
-        cost_estimate=pl.CostEstimate(
-            flops=2 * slots * FEAT * VOCAB_DEV,
-            bytes_accessed=FEAT * VOCAB_DEV * 2,
-            transcendentals=0,
-        ),
+        compiler_params=pltpu.CompilerParams(vmem_limit_bytes=VMEM),
+        cost_estimate=pl.CostEstimate(flops=2**20, bytes_accessed=2**18, transcendentals=0),
         name="lookup",
     )(local_ids, table)
 
@@ -190,44 +188,127 @@
             jax.ShapeDtypeStruct((TOK, FEAT), bf16),
             jax.ShapeDtypeStruct((TOK, 128), bf16),
         ),
-        compiler_params=pltpu.CompilerParams(vmem_limit_bytes=40 * 2**20),
+        compiler_params=pltpu.CompilerParams(vmem_limit_bytes=VMEM),
         name="arrange",
     )(ids_row, slots, gain, order)
 
 
 def project_kernel(own_ref, pair_ref, squares_ref, *rest):
-    shards, out_ref = rest[:-1], rest[-1]
-    own = jnp.concatenate([shard[0:64, :] for shard in shards], axis=0)
-    pair = jnp.concatenate([shard[64:128, :] for shard in shards], axis=0)
+    (
+        first,
+        first_z,
+        from_behind,
+        from_ahead,
+        far,
+        far_z,
+        second,
+        second_z,
+        behind,
+        ahead,
+        far_second,
+        near_z,
+        far_second_z,
+        out_ref,
+    ) = rest
+    own = jnp.concatenate(
+        [
+            first[...],
+            from_behind[0:64, :],
+            from_ahead[0:64, :],
+            far[...],
+            first_z[...],
+            from_behind[64:128, :],
+            from_ahead[64:128, :],
+            far_z[...],
+        ],
+        axis=0,
+    )
+    pair = jnp.concatenate(
+        [
+            second[...],
+            behind[...],
+            ahead[...],
+            far_second[...],
+            second_z[...],
+            near_z[...],
+            far_second_z[...],
+        ],
+        axis=0,
+    )
     total = jnp.dot(own_ref[...], own, preferred_element_type=f32)
     total = total + jnp.dot(pair_ref[...], pair, preferred_element_type=f32)
     out_ref[...] = total.astype(bf16)
 
     @pl.when(pl.program_id(0) == pl.num_programs(0) - 1)
     def _():
-        out_ref[:, 256:384] = squares_ref[...]
+        out_ref[:, COLS - 128 : COLS] = squares_ref[...]
 
 
 def project(own, pair, squares, shards):
     width = HALF + 128
-    steps = width // 384
     return pl.pallas_call(
         project_kernel,
-        grid=(steps,),
+        grid=(width // COLS,),
         in_specs=[
             pl.BlockSpec((TOK, FEAT), lambda i: (0, 0)),
             pl.BlockSpec((TOK, FEAT), lambda i: (0, 0)),
             pl.BlockSpec((TOK, 128), lambda i: (0, 0)),
         ]
-        + [pl.BlockSpec((128, 384), lambda i: (0, i)) for _ in shards],
-        out_specs=pl.BlockSpec((TOK, 384), lambda i: (0, i)),
+        + [pl.BlockSpec((shard.shape[0], COLS), lambda i: (0, i)) for shard in shards],
+        out_specs=pl.BlockSpec((TOK, COLS), lambda i: (0, i)),
         out_shape=jax.ShapeDtypeStruct((TOK, width), bf16),
-        compiler_params=pltpu.CompilerParams(vmem_limit_bytes=40 * 2**20),
+        compiler_params=pltpu.CompilerParams(vmem_limit_bytes=VMEM),
         cost_estimate=pl.CostEstimate(
             flops=2 * TOK * 1024 * HALF, bytes_accessed=1024 * HALF * 2, transcendentals=0
         ),
         name="project",
     )(own, pair, squares, *shards)
+
+
+OUT_PIECES = (
+    (0, 0, 64, 0, 0),
+    (1, 0, 64, 1, 0),
+    (2, 0, 64, 2, 0),
+    (4, 64, 32, 3, 0),
+    (5, 64, 32, 3, 32),
+    (3, 0, 64, 4, 0),
+    (4, 0, 64, 5, 0),
+    (5, 0, 64, 6, 0),
+    (6, 0, 32, 7, 0),
+    (7, 0, 32, 7, 32),
+)
+
+
+def collect_kernel(blocks_ref, *rest):
+    pieces, (out_ref, sems) = rest[:8], rest[8:]
+    copies = []
+    for piece, first, count, block, offset in OUT_PIECES:
+        row = pl.multiple_of(blocks_ref[block] * 64 + offset, 32)
+        copies.append(
+            pltpu.make_async_copy(
+                pieces[piece].at[pl.ds(first, count), :],
+                out_ref.at[pl.ds(row, count), :],
+                sems.at[len(copies)],
+            )
+        )
+    for copy in copies:
+        copy.start()
+    for copy in copies:
+        copy.wait()
+
+
+def collect(blocks, pieces):
+    anywhere = pl.BlockSpec(memory_space=pl.ANY)
+    return pl.pallas_call(
+        collect_kernel,
+        in_specs=[pl.BlockSpec(memory_space=pltpu.SMEM)] + [anywhere] * 8,
+        out_specs=pl.BlockSpec(memory_space=pltpu.VMEM),
+        out_shape=jax.ShapeDtypeStruct((FEAT, QW), bf16),
+        scratch_shapes=[pltpu.SemaphoreType.DMA((len(OUT_PIECES),))],
+        compiler_params=pltpu.CompilerParams(vmem_limit_bytes=16 * 2**20),
+        cost_estimate=pl.CostEstimate(flops=0, bytes_accessed=2**18, transcendentals=0),
+        name="collect",
+    )(blocks, *pieces)
 
 
 def dp_permute(value, dx, dz):
@@ -246,10 +327,20 @@
     return lax.ppermute(value, "tensor", pairs)
 
 
-def dp_gather(shard):
+def tied(value, *after):
+    return lax.optimization_barrier((value,) + after)[0]
+
+
+def gather_output(shard, after):
     other = dp_permute(shard, 0, 1)
-    found = [shard] + [dp_permute(shard, step, 0) for step in (1, 3, 2)]
-    return found + [other] + [dp_permute(other, step, 0) for step in (1, 3, 2)]
+    shard = tied(shard, *after)
+    behind = dp_permute(shard, 1, 0)
+    ahead = dp_permute(shard, 3, 0)
+    from_behind = dp_permute(jnp.concatenate([other, behind[:32]], axis=0), 1, 0)
+    from_ahead = dp_permute(jnp.concatenate([other, ahead[32:]], axis=0), 3, 0)
+    far_low = dp_permute(from_behind[:32], 1, 0)
+    far_high = dp_permute(from_ahead[32:64], 3, 0)
+    return shard, behind, ahead, other, from_behind, from_ahead, far_low, far_high
 
 
 def on_device(
@@ -274,21 +365,53 @@
     my_core = my_tensor % 2
 
     ids_row = token_ids.reshape(1, TOK)
-    all_ids = lax.all_to_all(
-        jnp.broadcast_to(ids_row, (GROUPS, TOK)), "dp", split_axis=0, concat_axis=0, tiled=True
-    )
     new_qkv = adamw(qkv_master, qkv_moment1, qkv_moment2, qkv_grad)
     qkv_local = new_qkv[0].astype(bf16)[0]
     kept = lax.dynamic_slice(qkv_local, (0, my_core * HALF), (64, HALF))
     given = lax.dynamic_slice(qkv_local, (0, (1 - my_core) * HALF), (64, HALF))
-    qkv_shard = jnp.concatenate([kept, tensor_permute(given, 0, 0, 1)], axis=0)
-    qkv_shards = dp_gather(qkv_shard)
+    taken = tensor_permute(given, 0, 0, 1)
+    ids_sent = tied(jnp.broadcast_to(ids_row, (GROUPS, TOK)), taken)
+    all_ids = lax.all_to_all(ids_sent, "dp", split_axis=0, concat_axis=0, tiled=True)
+
+    kept_z = dp_permute(kept, 0, 1)
+    taken_z = dp_permute(taken, 0, 1)
+    behind = dp_permute(taken, 1, 0)
+    ahead = dp_permute(taken, 3, 0)
+    up = jnp.concatenate([kept, kept_z, behind[:32]], axis=0)
+    down = jnp.concatenate([kept, kept_z, ahead[32:]], axis=0)
+    near = jnp.concatenate([behind, ahead], axis=0)
+    from_behind = dp_permute(up, 1, 0)
+    from_ahead = dp_permute(down, 3, 0)
+    near_z = dp_permute(near, 0, 1)
+    far = dp_permute(from_behind[:64], 1, 0)
+    far_z = dp_permute(from_ahead[64:128], 3, 0)
+    far_taken = jnp.concatenate([from_behind[128:160], from_ahead[128:160]], axis=0)
+    far_taken_z = dp_permute(far_taken, 0, 1)
+    qkv_pieces = (
+        kept,
+        kept_z,
+        from_behind,
+        from_ahead,
+        far,
+        far_z,
+        taken,
+        taken_z,
+        behind,
+        ahead,
+        far_taken,
+        near_z,
+        far_taken_z,
+    )
+    new_out = adamw(out_master, out_moment1, out_moment2, out_grad)
+    out_local = new_out[0].astype(bf16)[0]
 
     table = embed_table.transpose(1, 2, 0).reshape(FEAT, VOCAB_DEV)
-    sent = lookup(all_ids - my_group * VOCAB_DEV, table)
+    local_ids = tied(all_ids - my_group * VOCAB_DEV, up, down, near)
+    sent = lookup(local_ids, table)
     received = lax.all_to_all(
         sent.reshape(GROUPS, SLOTS, FEAT), "dp", split_axis=0, concat_axis=0, tiled=True
     ).reshape(GROUPS * SLOTS, FEAT)
+    received = tied(received, far_taken, out_local)
     blocks = jnp.stack(
         [
             ((my_x + 4 - step) % 4) * 2 + (my_z + flip) % 2
@@ -300,7 +423,7 @@
     hidden, scaled, squares = arrange(ids_row, received, norm_gain.reshape(1, FEAT), order)
     scaled_pair = tensor_permute(scaled, 0, 0, 1)
 
-    partial = project(scaled, scaled_pair, squares, qkv_shards)
+    partial = project(scaled, scaled_pair, squares, qkv_pieces)
     parts = lax.all_to_all(
         partial.reshape(16, 16, HALF + 128), "tensor", split_axis=0, concat_axis=0, tiled=True
     )
@@ -330,17 +453,15 @@
     )
     attended = attended.reshape(own_tokens, QW)
 
-    new_out = adamw(out_master, out_moment1, out_moment2, out_grad)
-    out_full = lax.all_gather(new_out[0].astype(bf16), "dp", axis=0, tiled=True).reshape(FEAT, QW)
+    out_pieces = gather_output(out_local, (far, far_z))
 
     other = tensor_permute(attended, 1, 0, 0)
     both = jnp.stack([attended, other])
     quad = jnp.stack([both] + [tensor_permute(both, 0, step, 0) for step in (1, 2, 3)])
-    everyone = jnp.stack([quad, tensor_permute(quad, 0, 0, 1)])
-    everyone = everyone.reshape(2, 4, 2, 16, QW)
+    away = tensor_permute(quad, 0, 0, 1)
     tensor_z, tensor_y = my_tensor // 8, (my_tensor // 2) % 4
     heads = jnp.zeros((16, 16, QW), bf16)
-    for core in range(2):
+    for core, found in enumerate((quad, away)):
         for step in range(4):
             for flip in range(2):
                 source = (
@@ -348,11 +469,12 @@
                     + ((tensor_y + 4 - step) % 4) * 2
                     + (my_core + core) % 2
                 )
-                heads = lax.dynamic_update_slice(
-                    heads, everyone[core, step, flip][None], (source, 0, 0)
-                )
+                heads = lax.dynamic_update_slice(heads, found[step, flip][None], (source, 0, 0))
     output = lax.dot_general(
-        heads.reshape(TOK, QW), out_full, (((1,), (1,)), ((), ())), preferred_element_type=f32
+        heads.reshape(TOK, QW),
+        collect(blocks.astype(jnp.int32), out_pieces),
+        (((1,), (1,)), ((), ())),
+        preferred_element_type=f32,
     )
     decoded = (hidden.astype(f32) + output).astype(bf16).reshape(group_rows, step_total, 8, 64)
     return (

time: 249 us -> 142 us (0.57)
  waiting for transfers between devices: 138 us -> 21.9 us
  between operations: 14.7 us -> 1.29 us
  starting transfers between devices: 50.8 us -> 59.7 us
  local copies, waits for them, and re-layouts: 8.49 us -> 16.5 us
  Pallas kernels: 15.9 us -> 19.2 us
  other arithmetic: 13.7 us -> 16.3 us
    all_gather x1 -> x0, waiting for transfers between devices: 64.9 us -> none  [on_device(): lax.all_gather(new_out[0].astype(bf16), 'dp', axis=0, tiled=True)]
    ppermute x7 -> x17, waiting for transfers between devices: 35.7 us -> 12.1 us  [dp_permute(): return lax.ppermute(value, 'dp', pairs)]
    all_to_all x1, waiting for transfers between devices: 18.8 us -> 0.65 us  [on_device(): lax.all_to_all(partial.reshape(16, 16, HALF + 128), 'tensor', split_axis=...]
    ppermute x7 -> x17, starting transfers between devices: 20.9 us -> 28.1 us  [dp_permute(): return lax.ppermute(value, 'dp', pairs)]
    ppermute x7, starting transfers between devices: 8.48 us -> 14.9 us  [tensor_permute(): return lax.ppermute(value, 'tensor', pairs)]
    all_to_all x1, waiting for transfers between devices: 6.04 us -> 0.01 us  [on_device(): lax.all_to_all(sent.reshape(GROUPS, SLOTS, FEAT), 'dp', split_axis=0, con...]
    convert_element_type x1 -> x0, other arithmetic: 3.58 us -> none  [on_device(): new_out[0].astype(bf16)]
    all_to_all x1, starting transfers between devices: 8.16 us -> 4.88 us  [on_device(): lax.all_to_all(ids_sent, 'dp', split_axis=0, concat_axis=0, tiled=True)]
  transfers between devices with their start and end apart: 18 -> 27, of which waited for: 12 -> 8; matrix products, arithmetic and copies ran while one was open for 5% -> 20% of each run, Pallas kernels for 4% -> 14%
where the time goes in v2:
time: 142 us; the launch traced here: 141 us
  starting transfers between devices  59.7 us (42%)
  waiting for transfers between devices  21.9 us (15%)
  Pallas kernels  19.2 us (14%)
  local copies, waits for them, and re-layouts  16.5 us (12%)
  other arithmetic  16.3 us (11%)
  matrix products  5.89 us (4%)
    ppermute x17, starting transfers between devices, dp_permute(): return lax.ppermute(value, 'dp', pairs)  28.1 us
    ppermute x7, starting transfers between devices, tensor_permute(): return lax.ppermute(value, 'tensor', pairs)  14.9 us
    ppermute x17, waiting for transfers between devices, dp_permute(): return lax.ppermute(value, 'dp', pairs)  12.1 us
    pallas_call x1, Pallas kernels, lookup(): pl.pallas_call(lookup_kernel, grid=(steps,), in_specs=[pl.BlockSpec((GROU...  10 us
    ppermute x7, waiting for transfers between devices, tensor_permute(): return lax.ppermute(value, 'tensor', pairs)  9.14 us
    all_to_all x1, starting transfers between devices, on_device(): lax.all_to_all(sent.reshape(GROUPS, SLOTS, FEAT), 'dp', split_axis=0, con...  6.49 us
    pallas_call x1, Pallas kernels, project(): pl.pallas_call(project_kernel, grid=(width // COLS,), in_specs=[pl.BlockS...  5.66 us
    all_to_all x1, starting transfers between devices, on_device(): lax.all_to_all(partial.reshape(16, 16, HALF + 128), 'tensor', split_axis=...  5.3 us
  transfers between devices with their start and end apart: 27, of which 8 were waited for; matrix products, arithmetic and copies ran while one was open for 20% of the time, Pallas kernels for 14%

profile of v2, /device:TPU:1, one launch (start us, length us, event | category | flops | bytes accessed | tf_op | source)
XLA Modules:
  0.0 140.7 jit_solution(9495844311105769610)
XLA Ops:
  0.7 5.0 %fusion.69 = (bf16[1,64,5120]{2,1,0:T(8,128)(2,1)S(1)}, f32[1,64,5120]{2,1,0:T(8,128)}, f32[1,64,5120]{2,1,0:T(8,128)}, f32[1,64,5120]{2,1,0:T(8,128)}) fusion(f32[1,64,5120]{2,1,0:T(8,128)} %param.13, bf16[1,64,5120]{2,1,0:T(8,128)(2,1)} %param.16, f32[1,64,5120]{2,1,0:T(8,128)} %param.14, f32[1,64,5120]{2,1,0:T(8,128)} %param.15), kind=kLoop, calls=%fused_computation.118 | loop fusion | flops 5570560 | bytes 9175040 | tf_op jit(solution)/shard_map/convert_element_type | solution.py:369
  5.8 1.5 %collective-permute-start = (bf16[64,2560]{1,0:T(8,128)(2,1)S(1)}, bf16[64,2560]{1,0:T(8,128)(2,1)S(1)}, u32[]{:S(2)}, u32[]{:S(2)}) collective-permute-start(bf16[64,2560]{1,0:T(8,128)(2,1)S(1)} %get-tuple-element.41), channel_id=1, source_target_pairs={{0,1},{1,0},{2,3},{3,2},{4,5},{5,4},{6,7},{7,6},{8,9},{9,8},{10,11... | collective-permute-start | bytes 983048 | tf_op jit(solution)/shard_map/ppermute | solution.py:327
  7.3 3.7 %collective-permute-start.1 = (bf16[64,2560]{1,0:T(8,128)(2,1)S(1)}, bf16[64,2560]{1,0:T(8,128)(2,1)S(1)}, u32[]{:S(2)}, u32[]{:S(2)}) collective-permute-start(bf16[64,2560]{1,0:T(8,128)(2,1)S(1)} %get-tuple-element.40.rest_0_), channel_id=1, source_target_pairs={{0,16},{16,0},{32,48},{48,32},{64,80},{80,64},{96,112},{112,96},{1... | collective-permute-start | bytes 983048 | tf_op jit(solution)/shard_map/ppermute | solution.py:319
  11.0 2.5 %collective-permute-start.3 = (bf16[64,2560]{1,0:T(8,128)(2,1)S(1)}, bf16[64,2560]{1,0:T(8,128)(2,1)S(1)}, u32[]{:S(2)}, u32[]{:S(2)}) collective-permute-start(bf16[64,2560]{1,0:T(8,128)(2,1)S(1)} %collective-permute-done.rest_6_), channel_id=1, source_target_pairs={{0,96},{16,112},{32,0},{48,16},{64,32},{80,48},{96,64},{112,80},{1... | collective-permute-start | bytes 983048 | tf_op jit(solution)/shard_map/ppermute | solution.py:319
  13.5 2.2 %convert_bitcast_fusion = (bf16[64,4096]{1,0:T(8,128)(2,1)S(1)}, f32[1,64,4096]{2,1,0:T(8,128)}, f32[1,64,4096]{2,1,0:T(8,128)}, f32[1,64,4096]{2,1,0:T(8,128)}) fusion(f32[1,64,4096]{2,1,0:T(8,128)S(1)} %copy-done.11, bf16[1,64,4096]{2,1,0:T(8,128)(2,1)S(1)} %copy-done.15, f32[1,64,4096]{2,1,0:T(8,128)S(1)} %copy-done.12, f32[1,64,4096]{2,1,0:T(8,128)S(1)} %copy-done.13), kind=kLoop, calls=%fused_computation.38 | loop fusion | flops 4456448 | bytes 7340032 | tf_op jit(solution)/shard_map/squeeze | solution.py:406
  16.0 0.6 all_to_all.12
  16.6 4.9 %all-to-all-start = ((s32[8,1,256]{2,1,0:T(1,128)}), s32[8,1,256]{2,1,0:T(1,128)S(1)}, u32[]{:S(2)}, u32[]{:S(2)}) async-start(s32[8,1,256]{2,1,0:T(1,128)} %all_to_all.12), calls=%async_computation | async-start | bytes 16384 | tf_op jit(solution)/shard_map/all_to_all | solution.py:374
  21.5 3.0 %collective-permute-start.9 = (bf16[64,2560]{1,0:T(8,128)(2,1)S(1)}, bf16[64,2560]{1,0:T(8,128)(2,1)}, u32[]{:S(2)}, u32[]{:S(2)}) collective-permute-start(bf16[64,2560]{1,0:T(8,128)(2,1)S(1)} %collective-permute-done.rest_6_), channel_id=1, source_target_pairs={{0,16},{16,0},{32,48},{48,32},{64,80},{80,64},{96,112},{112,96},{1... | collective-permute-start | bytes 983048 | tf_op jit(solution)/shard_map/ppermute | solution.py:319
  24.6 1.5 %pad_maximum_fusion.5 = (bf16[160,2560]{1,0:T(8,128)(2,1)}, bf16[160,2560]{1,0:T(8,128)(2,1)}) fusion(bf16[32,2560]{1,0:T(8,128)(2,1)S(1)} %slice.158, bf16[64,2560]{1,0:T(8,128)(2,1)S(1)} %collective-permute-done.1.rest_1_, bf16[64,2560]{1,0:T(8,128)(2,1)S(1)} %get-tuple-element.40.rest_0_, bf16[32,2560]{1,0:T(8,128)(2,1)S(1)} %slice.157), kind=kLoop, calls=%fused_computation.34 | loop fusion | flops 3686400 | bytes 2621440 | tf_op jit(solution)/shard_map/concatenate | solution.py:381
  26.1 2.4 %collective-permute-start.5 = (bf16[160,2560]{1,0:T(8,128)(2,1)}, bf16[160,2560]{1,0:T(8,128)(2,1)S(1)}, u32[]{:S(2)}, u32[]{:S(2)}) collective-permute-start(bf16[160,2560]{1,0:T(8,128)(2,1)} %get-tuple-element.38), channel_id=1, source_target_pairs={{0,96},{16,112},{32,0},{48,16},{64,32},{80,48},{96,64},{112,80},{1... | collective-permute-start | bytes 2457608 | tf_op jit(solution)/shard_map/ppermute | solution.py:319
  28.5 0.6 fusion.64.ids_ref
  29.1 0.7 constant_dynamic-update-slice_fusion.1
  29.8 0.7 constant_dynamic-update-slice_fusion
  30.9 10.0 %lookup.1 = bf16[512,512]{1,0:T(8,128)(2,1)} custom-call(s32[8,256]{1,0:T(8,128)} %fusion.64.ids_ref, bf16[512,9504]{1,0:T(8,128)(2,1)} %bitcast.160), custom_call_target="tpu_custom_call" | custom-call | flops 1048576 | bytes 262144 | tf_op jit(solution)/shard_map/lookup/pallas_call | solution.py:147
  40.9 6.5 %all-to-all-start.1 = ((bf16[8,64,512]{2,1,0:T(8,128)(2,1)}), bf16[8,64,512]{2,1,0:T(8,128)(2,1)S(1)}, u32[]{:S(2)}, u32[]{:S(2)}) async-start(bf16[8,64,512]{2,1,0:T(8,128)(2,1)} %bitcast.162), calls=%async_computation.1 | async-start | bytes 1048576 | tf_op jit(solution)/shard_map/all_to_all | solution.py:411
  47.7 0.8 slice.161
  48.5 1.2 collective-permute-start.7
  49.6 0.8 slice.162
  50.4 1.5 %collective-permute-start.8 = (bf16[64,2560]{1,0:T(8,128)(2,1)}, bf16[64,2560]{1,0:T(8,128)(2,1)}, u32[]{:S(2)}, u32[]{:S(2)}) collective-permute-start(bf16[64,2560]{1,0:T(8,128)(2,1)} %slice.162), channel_id=1, source_target_pairs={{0,96},{16,112},{32,0},{48,16},{64,32},{80,48},{96,64},{112,80},{1... | collective-permute-start | bytes 983048 | tf_op jit(solution)/shard_map/ppermute | solution.py:319
  52.0 2.8 %collective-permute-start.11 = (bf16[64,2560]{1,0:T(8,128)(2,1)S(1)}, bf16[64,2560]{1,0:T(8,128)(2,1)}, u32[]{:S(2)}, u32[]{:S(2)}) collective-permute-start(bf16[64,2560]{1,0:T(8,128)(2,1)S(1)} %pad_maximum_fusion.6.rest_10_), channel_id=1, source_target_pairs={{0,16},{16,0},{32,48},{48,32},{64,80},{80,64},{96,112},{112,96},{1... | collective-permute-start | bytes 983048 | tf_op jit(solution)/shard_map/ppermute | solution.py:319
  54.8 0.7 reshape.240.ids_ref
  55.5 0.7 reshape.244.gain_ref
  56.1 0.6 add.475.order_ref
  56.8 0.8 copy-done.5
  57.6 2.5 %arrange.1 = (bf16[256,512]{1,0:T(8,128)(2,1)}, bf16[256,512]{1,0:T(8,128)(2,1)}, bf16[256,128]{1,0:T(8,128)(2,1)}) custom-call(s32[1,256]{1,0:T(1,128)} %reshape.240.ids_ref, bf16[512,512]{1,0:T(8,128)(2,1)} %bitcast.164, f32[1,512]{1,0:T(1,128)} %reshape.244.gain_ref, s32[1,512]{1,0:T(1,128)} %add.475.order_ref), custom_call_target="tpu_custom_call" | custom-call | tf_op jit(solution)/shard_map/arrange/pallas_call | solution.py:184
  60.1 4.5 %collective-permute-start.6 = (bf16[256,512]{1,0:T(8,128)(2,1)}, bf16[256,512]{1,0:T(8,128)(2,1)S(1)}, u32[]{:S(2)}, u32[]{:S(2)}) collective-permute-start(bf16[256,512]{1,0:T(8,128)(2,1)} %get-tuple-element.19.own_ref), channel_id=1, source_target_pairs={{0,1},{1,0},{2,3},{3,2},{4,5},{5,4},{6,7},{7,6},{8,9},{9,8},{10,11... | collective-permute-start | bytes 786440 | tf_op jit(solution)/shard_map/ppermute | solution.py:327
  64.6 2.7 %collective-permute-start.19 = (bf16[64,4096]{1,0:T(8,128)(2,1)S(1)}, bf16[64,4096]{1,0:T(8,128)(2,1)S(1)}, u32[]{:S(2)}, u32[]{:S(2)}) collective-permute-start(bf16[64,4096]{1,0:T(8,128)(2,1)S(1)} %get-tuple-element.21.rest_0_), channel_id=1, source_target_pairs={{0,16},{16,0},{32,48},{48,32},{64,80},{80,64},{96,112},{112,96},{1... | collective-permute-start | bytes 1572872 | tf_op jit(solution)/shard_map/ppermute | solution.py:319
  67.3 0.6 copy-done.17
  68.0 5.7 %project.1 = bf16[256,2688]{1,0:T(8,128)(2,1)} custom-call(bf16[256,512]{1,0:T(8,128)(2,1)} %get-tuple-element.19.own_ref, bf16[256,512]{1,0:T(8,128)(2,1)} %copy-done.17, bf16[256,128]{1,0:T(8,128)(2,1)} %get-tuple-element.20.squares_ref, bf16[64,2560]{1,0:T(8,128)(2,1)} %copy-done.2, bf16[64,2560]{1,0:T(8,128)(2,1)} %copy-done.8, ...), custom_call_target="tpu_custom_call" | custom-call | flops 1342177280 | bytes 5242880 | tf_op jit(solution)/shard_map/project/pallas_call | solution.py:249
  73.7 5.3 %all-to-all-start.2 = ((bf16[16,16,2688]{2,1,0:T(8,128)(2,1)}), bf16[16,16,2688]{2,1,0:T(8,128)(2,1)}, u32[]{:S(2)}, u32[]{:S(2)}) async-start(bf16[16,16,2688]{2,1,0:T(8,128)(2,1)} %bitcast.161), calls=%async_computation.2 | async-start | bytes 2752512 | tf_op jit(solution)/shard_map/all_to_all | solution.py:427
  79.3 2.5 %collective-permute-start.18 = (bf16[64,4096]{1,0:T(8,128)(2,1)S(1)}, bf16[64,4096]{1,0:T(8,128)(2,1)S(1)}, u32[]{:S(2)}, u32[]{:S(2)}) collective-permute-start(bf16[64,4096]{1,0:T(8,128)(2,1)S(1)} %get-tuple-element.21.rest_0_), channel_id=1, source_target_pairs={{0,96},{16,112},{32,0},{48,16},{64,32},{80,48},{96,64},{112,80},{1... | collective-permute-start | bytes 1572872 | tf_op jit(solution)/shard_map/ppermute | solution.py:319
  82.0 10.6 %collective-permute-done.18.rest_2_ = bf16[64,4096]{1,0:T(8,128)(2,1)S(1)} collective-permute-done((bf16[64,4096]{1,0:T(8,128)(2,1)S(1)}, bf16[64,4096]{1,0:T(8,128)(2,1)S(1)}, u32[]{:S(2)}, u32[]{:S(2)}) %collective-permute-start.18) | collective-permute-done | bytes 524320 | tf_op jit(solution)/shard_map/ppermute | solution.py:319
  92.6 1.1 collective-permute-done.17.rest_1_
  93.8 1.3 pad_maximum_fusion.1
  95.1 2.7 %collective-permute-start.21 = (bf16[96,4096]{1,0:T(8,128)(2,1)}, bf16[96,4096]{1,0:T(8,128)(2,1)S(1)}, u32[]{:S(2)}, u32[]{:S(2)}) collective-permute-start(bf16[96,4096]{1,0:T(8,128)(2,1)} %get-tuple-element.42), channel_id=1, source_target_pairs={{0,96},{16,112},{32,0},{48,16},{64,32},{80,48},{96,64},{112,80},{1... | collective-permute-start | bytes 2359304 | tf_op jit(solution)/shard_map/ppermute | solution.py:319
  97.8 0.6 all-to-all-done.2
  98.4 1.6 %convert_reduce_fusion = f32[2,16,2688]{2,1,0:T(8,128)S(1)} fusion(bf16[8,2,16,2688]{3,2,1,0:T(8,128)(2,1)} %bitcast.58), kind=kLoop, calls=%fused_computation | loop fusion | flops 1290240 | bytes 1720320 | tf_op jit(solution)/shard_map/reduce_sum | solution.py:430
  100.0 0.7 fusion.72
  100.8 1.0 concatenate.52
  101.8 0.7 concatenate.51
  102.6 1.0 maximum_multiply_fusion
  103.6 0.7 copy-done.10
  104.3 0.7 slice.167
  105.0 1.1 reshape.248
  106.4 2.3 %fusion.73 = (f32[4,4,8,4]{2,3,1,0:T(4,128)S(1)}, f32[4,4,8,4,384]{4,2,3,1,0:T(8,128)S(1)}) fusion(bf16[4,4,384,256]{3,2,1,0:T(8,128)(2,1)} %param.25, pred[4,384]{1,0:T(4,128)(4,1)S(1)} %iota_compare_fusion, bf16[4,4,4,8,64]{4,3,2,1,0:T(8,128)(2,1)S(1)} %get-tuple-element.47, bf16[4,4,4,8,64]{4,3,2,1,0:T(8,128)(2,1)S(1)} %get-tuple-element.46), kind=kOutput, calls=%fused_computation.120 | convolution fusion | flops 51183104 | bytes 2493952 | tf_op jit(solution)/shard_map/rsngd,rncd->rngsc/dot_general | solution.py:71
  108.8 0.8 fusion.74
  110.1 1.0 convolution_bitcast_fusion
  111.1 0.4 fusion.24
  111.7 0.6 collective-permute-start.12
  112.3 0.8 slice.290
  113.1 0.7 copy.61
  113.8 0.7 copy.60
  114.6 0.7 pad_maximum_fusion.9
  115.4 2.7 %collective-permute-start.23 = (bf16[32,4096]{1,0:T(8,128)(2,1)S(1)}, bf16[32,4096]{1,0:T(8,128)(2,1)S(1)}, u32[]{:S(2)}, u32[]{:S(2)}) collective-permute-start(bf16[32,4096]{1,0:T(8,128)(2,1)S(1)} %slice.193), channel_id=1, source_target_pairs={{0,96},{16,112},{32,0},{48,16},{64,32},{80,48},{96,64},{112,80},{1... | collective-permute-start | bytes 786440 | tf_op jit(solution)/shard_map/ppermute | solution.py:319
  118.2 0.9 pad_maximum_fusion.7
  119.1 1.1 collective-permute-start.13
  120.2 2.5 %collective-permute-start.14 = (bf16[2,16,4096]{2,1,0:T(8,128)(2,1)S(1)}, bf16[2,16,4096]{2,1,0:T(8,128)(2,1)S(1)}, u32[]{:S(2)}, u32[]{:S(2)}) collective-permute-start(bf16[2,16,4096]{2,1,0:T(8,128)(2,1)S(1)} %get-tuple-element.48), channel_id=1, source_target_pairs={{0,4},{1,5},{2,6},{3,7},{4,0},{5,1},{6,2},{7,3},{8,12},{9,13},{10,... | collective-permute-start | bytes 786440 | tf_op jit(solution)/shard_map/ppermute | solution.py:327
  122.7 1.2 collective-permute-start.15
  124.2 1.0 collect.1
  125.6 6.3 %collective-permute-done.14 = bf16[2,16,4096]{2,1,0:T(8,128)(2,1)S(1)} collective-permute-done((bf16[2,16,4096]{2,1,0:T(8,128)(2,1)S(1)}, bf16[2,16,4096]{2,1,0:T(8,128)(2,1)S(1)}, u32[]{:S(2)}, u32[]{:S(2)}) %collective-permute-start.14) | collective-permute-done | bytes 262176 | tf_op jit(solution)/shard_map/ppermute | solution.py:327
  132.3 3.5 %collective-permute-start.16 = (bf16[4,2,16,4096]{3,2,1,0:T(8,128)(2,1)S(1)}, bf16[4,2,16,4096]{3,2,1,0:T(8,128)(2,1)S(1)}, u32[]{:S(2)}, u32[]{:S(2)}) collective-permute-start(bf16[4,2,16,4096]{3,2,1,0:T(8,128)(2,1)S(1)} %pad_maximum_fusion), channel_id=1, source_target_pairs={{0,1},{1,0},{2,3},{3,2},{4,5},{5,4},{6,7},{7,6},{8,9},{9,8},{10,11... | collective-permute-start | bytes 3145736 | tf_op jit(solution)/shard_map/ppermute | solution.py:327
  136.0 2.2 %collective-permute-done.16 = bf16[4,2,16,4096]{3,2,1,0:T(8,128)(2,1)S(1)} collective-permute-done((bf16[4,2,16,4096]{3,2,1,0:T(8,128)(2,1)S(1)}, bf16[4,2,16,4096]{3,2,1,0:T(8,128)(2,1)S(1)}, u32[]{:S(2)}, u32[]{:S(2)}) %collective-permute-start.16) | collective-permute-done | bytes 1048608 | tf_op jit(solution)/shard_map/ppermute | solution.py:327
  138.3 1.3 fusion.17
  139.6 1.1 reshape.251
  (125 shorter events, 4.2 us)
Async XLA Ops:
  0.7 12.8 %copy-start.11 = (f32[1,64,4096]{2,1,0:T(8,128)S(1)}, f32[1,64,4096]{2,1,0:T(8,128)}, u32[]{:S(2)}) copy-start(f32[1,64,4096]{2,1,0:T(8,128)} %param.17) | copy-start | bytes 3145732
  0.7 12.8 %copy-start.12 = (f32[1,64,4096]{2,1,0:T(8,128)S(1)}, f32[1,64,4096]{2,1,0:T(8,128)}, u32[]{:S(2)}) copy-start(f32[1,64,4096]{2,1,0:T(8,128)} %param.18) | copy-start | bytes 3145732
  0.7 12.8 %copy-start.13 = (f32[1,64,4096]{2,1,0:T(8,128)S(1)}, f32[1,64,4096]{2,1,0:T(8,128)}, u32[]{:S(2)}) copy-start(f32[1,64,4096]{2,1,0:T(8,128)} %param.19) | copy-start | bytes 3145732
  0.7 12.8 %copy-start.15 = (bf16[1,64,4096]{2,1,0:T(8,128)(2,1)S(1)}, bf16[1,64,4096]{2,1,0:T(8,128)(2,1)}, u32[]{:S(2)}) copy-start(bf16[1,64,4096]{2,1,0:T(8,128)(2,1)} %param.20) | copy-start | bytes 1572868
  5.8 18.8 %copy-start.2 = (bf16[64,2560]{1,0:T(8,128)(2,1)}, bf16[64,2560]{1,0:T(8,128)(2,1)S(1)}, u32[]{:S(2)}) copy-start(bf16[64,2560]{1,0:T(8,128)(2,1)S(1)} %get-tuple-element.40.rest_0_) | copy-start | bytes 983044
  5.8 5.2 %collective-permute-start = (bf16[64,2560]{1,0:T(8,128)(2,1)S(1)}, bf16[64,2560]{1,0:T(8,128)(2,1)S(1)}, u32[]{:S(2)}, u32[]{:S(2)}) collective-permute-start(bf16[64,2560]{1,0:T(8,128)(2,1)S(1)} %get-tuple-element.41), channel_id=1, source_target_pairs={{0,1},{1,0},{2,3},{3,2},{4,5},{5,4},{6,7},{7,6},{8,9},{9,8},{10,11... | collective-permute-start | bytes 983048 | tf_op jit(solution)/shard_map/ppermute | solution.py:327
  7.3 8.4 %copy-start.21 = (s32[64,4]{0,1:T(4,128)S(1)}, s32[64,4]{0,1:T(4,128)}, u32[]{:S(2)}) copy-start(s32[64,4]{0,1:T(4,128)} %param.23) | copy-start | bytes 3076
  7.3 17.3 %collective-permute-start.1 = (bf16[64,2560]{1,0:T(8,128)(2,1)S(1)}, bf16[64,2560]{1,0:T(8,128)(2,1)S(1)}, u32[]{:S(2)}, u32[]{:S(2)}) collective-permute-start(bf16[64,2560]{1,0:T(8,128)(2,1)S(1)} %get-tuple-element.40.rest_0_), channel_id=1, source_target_pairs={{0,16},{16,0},{32,48},{48,32},{64,80},{80,64},{96,112},{112,96},{1... | collective-permute-start | bytes 983048 | tf_op jit(solution)/shard_map/ppermute | solution.py:319
  11.0 10.5 %copy-start.16 = (bf16[64,2560]{1,0:T(8,128)(2,1)}, bf16[64,2560]{1,0:T(8,128)(2,1)S(1)}, u32[]{:S(2)}) copy-start(bf16[64,2560]{1,0:T(8,128)(2,1)S(1)} %collective-permute-done.rest_6_) | copy-start | bytes 983044
  11.0 13.5 %collective-permute-start.3 = (bf16[64,2560]{1,0:T(8,128)(2,1)S(1)}, bf16[64,2560]{1,0:T(8,128)(2,1)S(1)}, u32[]{:S(2)}, u32[]{:S(2)}) collective-permute-start(bf16[64,2560]{1,0:T(8,128)(2,1)S(1)} %collective-permute-done.rest_6_), channel_id=1, source_target_pairs={{0,96},{16,112},{32,0},{48,16},{64,32},{80,48},{96,64},{112,80},{1... | collective-permute-start | bytes 983048 | tf_op jit(solution)/shard_map/ppermute | solution.py:319
  13.5 11.0 %collective-permute-start.2 = (bf16[64,2560]{1,0:T(8,128)(2,1)S(1)}, bf16[64,2560]{1,0:T(8,128)(2,1)S(1)}, u32[]{:S(2)}, u32[]{:S(2)}) collective-permute-start(bf16[64,2560]{1,0:T(8,128)(2,1)S(1)} %collective-permute-done.rest_6_), channel_id=1, source_target_pairs={{0,32},{16,48},{32,64},{48,80},{64,96},{80,112},{96,0},{112,16},{1... | collective-permute-start | bytes 983048 | tf_op jit(solution)/shard_map/ppermute | solution.py:319
  16.6 11.8 %all-to-all-start = ((s32[8,1,256]{2,1,0:T(1,128)}), s32[8,1,256]{2,1,0:T(1,128)S(1)}, u32[]{:S(2)}, u32[]{:S(2)}) async-start(s32[8,1,256]{2,1,0:T(1,128)} %all_to_all.12), calls=%async_computation | async-start | bytes 16384 | tf_op jit(solution)/shard_map/all_to_all | solution.py:374
  21.5 38.6 %collective-permute-start.9 = (bf16[64,2560]{1,0:T(8,128)(2,1)S(1)}, bf16[64,2560]{1,0:T(8,128)(2,1)}, u32[]{:S(2)}, u32[]{:S(2)}) collective-permute-start(bf16[64,2560]{1,0:T(8,128)(2,1)S(1)} %collective-permute-done.rest_6_), channel_id=1, source_target_pairs={{0,16},{16,0},{32,48},{48,32},{64,80},{80,64},{96,112},{112,96},{1... | collective-permute-start | bytes 983048 | tf_op jit(solution)/shard_map/ppermute | solution.py:319
  24.5 6.1 %copy-start.6 = (bf16[64,2560]{1,0:T(8,128)(2,1)}, bf16[64,2560]{1,0:T(8,128)(2,1)S(1)}, u32[]{:S(2)}) copy-start(bf16[64,2560]{1,0:T(8,128)(2,1)S(1)} %collective-permute-done.3.rest_9_) | copy-start | bytes 983044
  24.5 6.1 %copy-start.7 = (bf16[64,2560]{1,0:T(8,128)(2,1)}, bf16[64,2560]{1,0:T(8,128)(2,1)S(1)}, u32[]{:S(2)}) copy-start(bf16[64,2560]{1,0:T(8,128)(2,1)S(1)} %collective-permute-done.2.rest_8_) | copy-start | bytes 983044
  24.6 1.5 %copy-start.8 = (bf16[64,2560]{1,0:T(8,128)(2,1)}, bf16[64,2560]{1,0:T(8,128)(2,1)S(1)}, u32[]{:S(2)}) copy-start(bf16[64,2560]{1,0:T(8,128)(2,1)S(1)} %collective-permute-done.1.rest_1_) | copy-start | bytes 983044
  26.1 23.6 %collective-permute-start.5 = (bf16[160,2560]{1,0:T(8,128)(2,1)}, bf16[160,2560]{1,0:T(8,128)(2,1)S(1)}, u32[]{:S(2)}, u32[]{:S(2)}) collective-permute-start(bf16[160,2560]{1,0:T(8,128)(2,1)} %get-tuple-element.38), channel_id=1, source_target_pairs={{0,96},{16,112},{32,0},{48,16},{64,32},{80,48},{96,64},{112,80},{1... | collective-permute-start | bytes 2457608 | tf_op jit(solution)/shard_map/ppermute | solution.py:319
  28.5 19.2 %collective-permute-start.4 = (bf16[160,2560]{1,0:T(8,128)(2,1)}, bf16[160,2560]{1,0:T(8,128)(2,1)S(1)}, u32[]{:S(2)}, u32[]{:S(2)}) collective-permute-start(bf16[160,2560]{1,0:T(8,128)(2,1)} %get-tuple-element.39), channel_id=1, source_target_pairs={{0,32},{16,48},{32,64},{48,80},{64,96},{80,112},{96,0},{112,16},{1... | collective-permute-start | bytes 2457608 | tf_op jit(solution)/shard_map/ppermute | solution.py:319
  30.6 34.0 %collective-permute-start.10 = (bf16[128,2560]{1,0:T(8,128)(2,1)}, bf16[128,2560]{1,0:T(8,128)(2,1)}, u32[]{:S(2)}, u32[]{:S(2)}) collective-permute-start(bf16[128,2560]{1,0:T(8,128)(2,1)} %constant_dynamic-update-slice_fusion), channel_id=1, source_target_pairs={{0,16},{16,0},{32,48},{48,32},{64,80},{80,64},{96,112},{112,96},{1... | collective-permute-start | bytes 1966088 | tf_op jit(solution)/shard_map/ppermute | solution.py:319
  40.9 14.6 %copy-start.20 = (f32[8,64]{1,0:T(8,128)S(1)}, f32[8,64]{1,0:T(8,128)}, u32[]{:S(2)}) copy-start(f32[8,64]{1,0:T(8,128)} %param.22) | copy-start | bytes 6148
  40.9 15.9 %all-to-all-start.1 = ((bf16[8,64,512]{2,1,0:T(8,128)(2,1)}), bf16[8,64,512]{2,1,0:T(8,128)(2,1)S(1)}, u32[]{:S(2)}, u32[]{:S(2)}) async-start(bf16[8,64,512]{2,1,0:T(8,128)(2,1)} %bitcast.162), calls=%async_computation.1 | async-start | bytes 1048576 | tf_op jit(solution)/shard_map/all_to_all | solution.py:411
  47.7 19.6 %copy-start.4 = (bf16[160,2560]{1,0:T(8,128)(2,1)}, bf16[160,2560]{1,0:T(8,128)(2,1)S(1)}, u32[]{:S(2)}) copy-start(bf16[160,2560]{1,0:T(8,128)(2,1)S(1)} %collective-permute-done.4.rest_2_) | copy-start | bytes 2457604
  48.5 18.8 %collective-permute-start.7 = (bf16[64,2560]{1,0:T(8,128)(2,1)}, bf16[64,2560]{1,0:T(8,128)(2,1)}, u32[]{:S(2)}, u32[]{:S(2)}) collective-permute-start(bf16[64,2560]{1,0:T(8,128)(2,1)} %slice.161), channel_id=1, source_target_pairs={{0,32},{16,48},{32,64},{48,80},{64,96},{80,112},{96,0},{112,16},{1... | collective-permute-start | bytes 983048 | tf_op jit(solution)/shard_map/ppermute | solution.py:319
  49.6 17.7 %copy-start.3 = (bf16[160,2560]{1,0:T(8,128)(2,1)}, bf16[160,2560]{1,0:T(8,128)(2,1)S(1)}, u32[]{:S(2)}) copy-start(bf16[160,2560]{1,0:T(8,128)(2,1)S(1)} %collective-permute-done.5.rest_3_) | copy-start | bytes 2457604
  50.4 16.9 %collective-permute-start.8 = (bf16[64,2560]{1,0:T(8,128)(2,1)}, bf16[64,2560]{1,0:T(8,128)(2,1)}, u32[]{:S(2)}, u32[]{:S(2)}) collective-permute-start(bf16[64,2560]{1,0:T(8,128)(2,1)} %slice.162), channel_id=1, source_target_pairs={{0,96},{16,112},{32,0},{48,16},{64,32},{80,48},{96,64},{112,80},{1... | collective-permute-start | bytes 983048 | tf_op jit(solution)/shard_map/ppermute | solution.py:319
  52.0 15.3 %copy-start.9 = (bf16[64,2560]{1,0:T(8,128)(2,1)}, bf16[64,2560]{1,0:T(8,128)(2,1)S(1)}, u32[]{:S(2)}) copy-start(bf16[64,2560]{1,0:T(8,128)(2,1)S(1)} %pad_maximum_fusion.6.rest_10_) | copy-start | bytes 983044
  52.0 15.3 %collective-permute-start.11 = (bf16[64,2560]{1,0:T(8,128)(2,1)S(1)}, bf16[64,2560]{1,0:T(8,128)(2,1)}, u32[]{:S(2)}, u32[]{:S(2)}) collective-permute-start(bf16[64,2560]{1,0:T(8,128)(2,1)S(1)} %pad_maximum_fusion.6.rest_10_), channel_id=1, source_target_pairs={{0,16},{16,0},{32,48},{48,32},{64,80},{80,64},{96,112},{112,96},{1... | collective-permute-start | bytes 983048 | tf_op jit(solution)/shard_map/ppermute | solution.py:319
  56.8 0.8 copy-start.5
  60.1 7.2 %collective-permute-start.6 = (bf16[256,512]{1,0:T(8,128)(2,1)}, bf16[256,512]{1,0:T(8,128)(2,1)S(1)}, u32[]{:S(2)}, u32[]{:S(2)}) collective-permute-start(bf16[256,512]{1,0:T(8,128)(2,1)} %get-tuple-element.19.own_ref), channel_id=1, source_target_pairs={{0,1},{1,0},{2,3},{3,2},{4,5},{5,4},{6,7},{7,6},{8,9},{9,8},{10,11... | collective-permute-start | bytes 786440 | tf_op jit(solution)/shard_map/ppermute | solution.py:327
  64.6 29.2 %collective-permute-start.19 = (bf16[64,4096]{1,0:T(8,128)(2,1)S(1)}, bf16[64,4096]{1,0:T(8,128)(2,1)S(1)}, u32[]{:S(2)}, u32[]{:S(2)}) collective-permute-start(bf16[64,4096]{1,0:T(8,128)(2,1)S(1)} %get-tuple-element.21.rest_0_), channel_id=1, source_target_pairs={{0,16},{16,0},{32,48},{48,32},{64,80},{80,64},{96,112},{112,96},{1... | collective-permute-start | bytes 1572872 | tf_op jit(solution)/shard_map/ppermute | solution.py:319
  67.3 0.7 copy-start.17
  73.6 5.3 %copy-start.22 = (s32[4]{0:T(128)S(1)}, s32[4]{0:T(128)}, u32[]{:S(2)}) copy-start(s32[4]{0:T(128)} %param.24) | copy-start | bytes 52
  73.7 24.8 %all-to-all-start.2 = ((bf16[16,16,2688]{2,1,0:T(8,128)(2,1)}), bf16[16,16,2688]{2,1,0:T(8,128)(2,1)}, u32[]{:S(2)}, u32[]{:S(2)}) async-start(bf16[16,16,2688]{2,1,0:T(8,128)(2,1)} %bitcast.161), calls=%async_computation.2 | async-start | bytes 2752512 | tf_op jit(solution)/shard_map/all_to_all | solution.py:427
  79.0 14.7 %collective-permute-start.17 = (bf16[64,4096]{1,0:T(8,128)(2,1)S(1)}, bf16[64,4096]{1,0:T(8,128)(2,1)S(1)}, u32[]{:S(2)}, u32[]{:S(2)}) collective-permute-start(bf16[64,4096]{1,0:T(8,128)(2,1)S(1)} %get-tuple-element.21.rest_0_), channel_id=1, source_target_pairs={{0,32},{16,48},{32,64},{48,80},{64,96},{80,112},{96,0},{112,16},{1... | collective-permute-start | bytes 1572872 | tf_op jit(solution)/shard_map/ppermute | solution.py:319
  79.3 13.3 %collective-permute-start.18 = (bf16[64,4096]{1,0:T(8,128)(2,1)S(1)}, bf16[64,4096]{1,0:T(8,128)(2,1)S(1)}, u32[]{:S(2)}, u32[]{:S(2)}) collective-permute-start(bf16[64,4096]{1,0:T(8,128)(2,1)S(1)} %get-tuple-element.21.rest_0_), channel_id=1, source_target_pairs={{0,96},{16,112},{32,0},{48,16},{64,32},{80,48},{96,64},{112,80},{1... | collective-permute-start | bytes 1572872 | tf_op jit(solution)/shard_map/ppermute | solution.py:319
  92.6 2.5 %copy-start = (bf16[64,4096]{1,0:T(8,128)(2,1)}, bf16[64,4096]{1,0:T(8,128)(2,1)S(1)}, u32[]{:S(2)}) copy-start(bf16[64,4096]{1,0:T(8,128)(2,1)S(1)} %collective-permute-done.18.rest_2_) | copy-start | bytes 1572868
  95.1 20.2 %collective-permute-start.20 = (bf16[96,4096]{1,0:T(8,128)(2,1)}, bf16[96,4096]{1,0:T(8,128)(2,1)S(1)}, u32[]{:S(2)}, u32[]{:S(2)}) collective-permute-start(bf16[96,4096]{1,0:T(8,128)(2,1)} %get-tuple-element.43), channel_id=1, source_target_pairs={{0,32},{16,48},{32,64},{48,80},{64,96},{80,112},{96,0},{112,16},{1... | collective-permute-start | bytes 2359304 | tf_op jit(solution)/shard_map/ppermute | solution.py:319
  95.1 20.3 %collective-permute-start.21 = (bf16[96,4096]{1,0:T(8,128)(2,1)}, bf16[96,4096]{1,0:T(8,128)(2,1)S(1)}, u32[]{:S(2)}, u32[]{:S(2)}) collective-permute-start(bf16[96,4096]{1,0:T(8,128)(2,1)} %get-tuple-element.42), channel_id=1, source_target_pairs={{0,96},{16,112},{32,0},{48,16},{64,32},{80,48},{96,64},{112,80},{1... | collective-permute-start | bytes 2359304 | tf_op jit(solution)/shard_map/ppermute | solution.py:319
  103.6 0.7 copy-start.10
  106.2 3.7 %copy-start.18 = (bf16[4,4,4,64]{3,1,2,0:T(4,128)(2,1)}, bf16[4,4,4,64]{3,1,2,0:T(4,128)(2,1)S(1)}, u32[]{:S(2)}) copy-start(bf16[4,4,4,64]{3,1,2,0:T(4,128)(2,1)S(1)} %get-tuple-element.50) | copy-start | bytes 24580
  106.3 3.7 %copy-start.19 = (bf16[4,4,4,64]{3,1,2,0:T(4,128)(2,1)}, bf16[4,4,4,64]{3,1,2,0:T(4,128)(2,1)S(1)}, u32[]{:S(2)}) copy-start(bf16[4,4,4,64]{3,1,2,0:T(4,128)(2,1)S(1)} %get-tuple-element.51) | copy-start | bytes 24580
  106.4 4.7 %copy-start.14 = (bf16[4,4,384,256]{3,2,1,0:T(8,128)(2,1)S(1)}, bf16[4,4,384,256]{3,2,1,0:T(8,128)(2,1)}, u32[]{:S(2)}) copy-start(bf16[4,4,384,256]{3,2,1,0:T(8,128)(2,1)} %param.25) | copy-start | bytes 9437188
  111.7 6.5 %collective-permute-start.12 = (bf16[16,4096]{1,0:T(8,128)(2,1)S(1)}, bf16[16,4096]{1,0:T(8,128)(2,1)}, u32[]{:S(2)}, u32[]{:S(2)}) collective-permute-start(bf16[16,4096]{1,0:T(8,128)(2,1)S(1)} %reshape_reshape.3), channel_id=1, source_target_pairs={{0,8},{1,9},{2,10},{3,11},{4,12},{5,13},{6,14},{7,15},{8,0},{9,1},... | collective-permute-start | bytes 393224 | tf_op jit(solution)/shard_map/ppermute | solution.py:327
  115.3 8.9 %copy-start.1 = (bf16[64,4096]{1,0:T(8,128)(2,1)S(1)}, bf16[64,4096]{1,0:T(8,128)(2,1)}, u32[]{:S(2)}) copy-start(bf16[64,4096]{1,0:T(8,128)(2,1)} %copy-done) | copy-start | bytes 1572868
  115.3 8.9 %collective-permute-start.22 = (bf16[32,4096]{1,0:T(8,128)(2,1)S(1)}, bf16[32,4096]{1,0:T(8,128)(2,1)S(1)}, u32[]{:S(2)}, u32[]{:S(2)}) collective-permute-start(bf16[32,4096]{1,0:T(8,128)(2,1)S(1)} %slice.192), channel_id=1, source_target_pairs={{0,32},{16,48},{32,64},{48,80},{64,96},{80,112},{96,0},{112,16},{1... | collective-permute-start | bytes 786440 | tf_op jit(solution)/shard_map/ppermute | solution.py:319
  115.4 8.8 %collective-permute-start.23 = (bf16[32,4096]{1,0:T(8,128)(2,1)S(1)}, bf16[32,4096]{1,0:T(8,128)(2,1)S(1)}, u32[]{:S(2)}, u32[]{:S(2)}) collective-permute-start(bf16[32,4096]{1,0:T(8,128)(2,1)S(1)} %slice.193), channel_id=1, source_target_pairs={{0,96},{16,112},{32,0},{48,16},{64,32},{80,48},{96,64},{112,80},{1... | collective-permute-start | bytes 786440 | tf_op jit(solution)/shard_map/ppermute | solution.py:319
  119.1 6.5 %collective-permute-start.13 = (bf16[2,16,4096]{2,1,0:T(8,128)(2,1)S(1)}, bf16[2,16,4096]{2,1,0:T(8,128)(2,1)S(1)}, u32[]{:S(2)}, u32[]{:S(2)}) collective-permute-start(bf16[2,16,4096]{2,1,0:T(8,128)(2,1)S(1)} %get-tuple-element.48), channel_id=1, source_target_pairs={{0,2},{1,3},{2,4},{3,5},{4,6},{5,7},{6,0},{7,1},{8,10},{9,11},{10,... | collective-permute-start | bytes 786440 | tf_op jit(solution)/shard_map/ppermute | solution.py:327
  120.2 11.7 %collective-permute-start.14 = (bf16[2,16,4096]{2,1,0:T(8,128)(2,1)S(1)}, bf16[2,16,4096]{2,1,0:T(8,128)(2,1)S(1)}, u32[]{:S(2)}, u32[]{:S(2)}) collective-permute-start(bf16[2,16,4096]{2,1,0:T(8,128)(2,1)S(1)} %get-tuple-element.48), channel_id=1, source_target_pairs={{0,4},{1,5},{2,6},{3,7},{4,0},{5,1},{6,2},{7,3},{8,12},{9,13},{10,... | collective-permute-start | bytes 786440 | tf_op jit(solution)/shard_map/ppermute | solution.py:327
  122.7 9.4 %collective-permute-start.15 = (bf16[2,16,4096]{2,1,0:T(8,128)(2,1)S(1)}, bf16[2,16,4096]{2,1,0:T(8,128)(2,1)S(1)}, u32[]{:S(2)}, u32[]{:S(2)}) collective-permute-start(bf16[2,16,4096]{2,1,0:T(8,128)(2,1)S(1)} %get-tuple-element.48), channel_id=1, source_target_pairs={{0,6},{1,7},{2,0},{3,1},{4,2},{5,3},{6,4},{7,5},{8,14},{9,15},{10,... | collective-permute-start | bytes 786440 | tf_op jit(solution)/shard_map/ppermute | solution.py:327
  132.3 6.0 %copy-start.23 = (bf16[256,512]{1,0:T(8,128)(2,1)S(1)}, bf16[256,512]{1,0:T(8,128)(2,1)}, u32[]{:S(2)}) copy-start(bf16[256,512]{1,0:T(8,128)(2,1)} %get-tuple-element.18) | copy-start | bytes 786436
  132.3 5.8 %collective-permute-start.16 = (bf16[4,2,16,4096]{3,2,1,0:T(8,128)(2,1)S(1)}, bf16[4,2,16,4096]{3,2,1,0:T(8,128)(2,1)S(1)}, u32[]{:S(2)}, u32[]{:S(2)}) collective-permute-start(bf16[4,2,16,4096]{3,2,1,0:T(8,128)(2,1)S(1)} %pad_maximum_fusion), channel_id=1, source_target_pairs={{0,1},{1,0},{2,3},{3,2},{4,5},{5,4},{6,7},{7,6},{8,9},{9,8},{10,11... | collective-permute-start | bytes 3145736 | tf_op jit(solution)/shard_map/ppermute | solution.py:327

commit v3 on v2

--- a/solution.py
+++ b/solution.py
@@ -18,7 +18,7 @@
 GROUPS = 8
 TOK = 256
 FEAT = 512
-VCHUNK = 1920
+VCHUNK = 3200
 HALF = 2560
 COLS = 896
 VMEM = 56 * 2**20
@@ -46,54 +46,6 @@
     return (master, moment_one, moment_two)
 
 
-def rotate(values, positions):
-    half_dim = values.shape[-1] // 2
-    exponent = jnp.arange(half_dim).astype(jnp.float32) * (2.0 / values.shape[-1])
-    freqs = jnp.power(jnp.float32(rope_base), -exponent)
-    angles = positions.astype(jnp.float32)[..., None] * freqs
-    cosine = jnp.cos(angles)[..., None, :]
-    sine = jnp.sin(angles)[..., None, :]
-    first_half = values[..., :half_dim]
-    second_half = values[..., half_dim:]
-    return jnp.concatenate(
-        [first_half * cosine - second_half * sine, second_half * cosine + first_half * sine],
-        axis=-1,
-    )
-
-
-def attend(queries, keys_new, values_new, cache, lengths):
-    head_dim = queries.shape[-1]
-    row_total, step_total = (queries.shape[0], queries.shape[1])
-    scale = 1.0 / math.sqrt(head_dim)
-    cache_keys = cache[..., :head_dim]
-    cache_values = cache[..., head_dim:]
-    cache_scores = (
-        jnp.einsum("rsngd,rncd->rngsc", queries, cache_keys, preferred_element_type=jnp.float32)
-        * scale
-    )
-    new_scores = (
-        jnp.einsum("rsngd,rtnd->rngst", queries, keys_new, preferred_element_type=jnp.float32)
-        * scale
-    )
-    cache_live = jnp.arange(cache.shape[2])[None, :] < lengths[:, None]
-    cache_scores = jnp.where(cache_live[:, None, None, None, :], cache_scores, -jnp.inf)
-    causal = jnp.arange(step_total)[:, None] >= jnp.arange(step_total)[None, :]
-    new_scores = jnp.where(causal, new_scores, -jnp.inf)
-    highest = jnp.maximum(jnp.max(cache_scores, axis=-1), jnp.max(new_scores, axis=-1))
-    cache_exp = jnp.exp(cache_scores - highest[..., None])
-    new_exp = jnp.exp(new_scores - highest[..., None])
-    denom = jnp.sum(cache_exp, axis=-1) + jnp.sum(new_exp, axis=-1)
-    cache_weights = (cache_exp / denom[..., None]).astype(jnp.bfloat16)
-    new_weights = (new_exp / denom[..., None]).astype(jnp.bfloat16)
-    mixed = jnp.einsum(
-        "rngsc,rncd->rsngd", cache_weights, cache_values, preferred_element_type=jnp.float32
-    )
-    mixed = mixed + jnp.einsum(
-        "rngst,rtnd->rsngd", new_weights, values_new, preferred_element_type=jnp.float32
-    )
-    return mixed.astype(jnp.bfloat16).reshape(row_total, step_total, -1)
-
-
 def iota(shape, axis):
     return lax.broadcasted_iota(jnp.int32, shape, axis)
 
@@ -107,7 +59,7 @@
 
     @pl.when(step == 0)
     def _():
-        local = ids_ref[...]
+        local = ids_ref[:, 0, :] - lax.axis_index("dp") * VOCAB_DEV
         mine = (local >= 0) & (local < VOCAB_DEV)
         rank = jnp.dot(
             mine.astype(f32).astype(bf16), lower_triangle(TOK), preferred_element_type=f32
@@ -141,27 +93,29 @@
         out_ref[...] = total.astype(bf16)
 
 
-def lookup(local_ids, table):
+def lookup(all_ids, table):
     steps = pl.cdiv(VOCAB_DEV, VCHUNK)
     slots = GROUPS * SLOTS
     return pl.pallas_call(
         lookup_kernel,
         grid=(steps,),
         in_specs=[
-            pl.BlockSpec((GROUPS, TOK), lambda i: (0, 0)),
+            pl.BlockSpec((GROUPS, 1, TOK), lambda i: (0, 0, 0)),
             pl.BlockSpec((FEAT, VCHUNK), lambda i: (0, i)),
         ],
         out_specs=pl.BlockSpec((slots, FEAT), lambda i: (0, 0)),
         out_shape=jax.ShapeDtypeStruct((slots, FEAT), bf16),
         scratch_shapes=[pltpu.VMEM((slots, FEAT), f32), pltpu.VMEM((slots, 128), jnp.int32)],
         compiler_params=pltpu.CompilerParams(vmem_limit_bytes=VMEM),
-        cost_estimate=pl.CostEstimate(flops=2**20, bytes_accessed=2**18, transcendentals=0),
+        cost_estimate=pl.CostEstimate(flops=3 * 10**10, bytes_accessed=10**7, transcendentals=0),
         name="lookup",
-    )(local_ids, table)
-
-
-def arrange_kernel(ids_ref, slots_ref, gain_ref, order_ref, hidden_ref, scaled_ref, squares_ref):
-    ids = jnp.broadcast_to(ids_ref[...], (GROUPS, TOK))
+    )(all_ids, table)
+
+
+def arrange_kernel(ids_ref, slots_ref, gain_ref, hidden_ref, scaled_ref, squares_ref):
+    group = lax.axis_index("dp")
+    ids = jnp.where(iota((GROUPS, TOK), 0) == group, ids_ref[:, 0, :], 0)
+    ids = jnp.broadcast_to(jnp.sum(ids, axis=0, keepdims=True), (GROUPS, TOK))
     low = iota((GROUPS, TOK), 0) * VOCAB_DEV
     owned = (ids >= low) & (ids < low + VOCAB_DEV)
     rank = jnp.dot(owned.astype(f32).astype(bf16), lower_triangle(TOK), preferred_element_type=f32)
@@ -175,12 +129,18 @@
     hidden_ref[...] = hidden.astype(bf16)
     squares = jnp.sum(hidden * hidden, axis=1, keepdims=True)
     squares_ref[...] = jnp.broadcast_to(squares, (TOK, 128)).astype(bf16)
-    scaled = (hidden * gain_ref[...]).astype(bf16)
-    order = jnp.where(iota((FEAT, FEAT), 0) == order_ref[...], 1.0, 0.0).astype(bf16)
+    gain = jnp.concatenate([gain_ref[block : block + 1, :] for block in range(8)], axis=1)
+    scaled = (hidden * gain).astype(bf16)
+    lane = iota((1, FEAT), 1)
+    step = (lane // 64) % 4
+    step = jnp.where(step == 2, 3, jnp.where(step == 3, 2, step))
+    block = ((group // 2 + 4 - step) % 4) * 2 + (group % 2 + lane // 256) % 2
+    order = block * 64 + lane % 64
+    order = jnp.where(iota((FEAT, FEAT), 0) == order, 1.0, 0.0).astype(bf16)
     scaled_ref[...] = jnp.dot(scaled, order, preferred_element_type=f32).astype(bf16)
 
 
-def arrange(ids_row, slots, gain, order):
+def arrange(all_ids, slots, gain):
     return pl.pallas_call(
         arrange_kernel,
         out_shape=(
@@ -190,7 +150,7 @@
         ),
         compiler_params=pltpu.CompilerParams(vmem_limit_bytes=VMEM),
         name="arrange",
-    )(ids_row, slots, gain, order)
+    )(all_ids, slots, gain)
 
 
 def project_kernel(own_ref, pair_ref, squares_ref, *rest):
@@ -265,6 +225,114 @@
     )(own, pair, squares, *shards)
 
 
+def attend_kernel(
+    lengths_ref, parts_ref, cos_ref, sin_ref, cache_ref, out_ref, fresh_ref, proj_ref
+):
+    head = pl.program_id(0)
+
+    @pl.when(head == 0)
+    def _():
+        sums = []
+        for core in range(2):
+            total = parts_ref[core].astype(f32)
+            for chip in range(1, 8):
+                total = total + parts_ref[2 * chip + core].astype(f32)
+            sums.append(total)
+        squares = sums[0][:, HALF : HALF + 1] + sums[1][:, HALF : HALF + 1]
+        inverse = lax.rsqrt(squares * (1.0 / D) + norm_epsilon)
+        for core in range(2):
+            proj_ref[:, core * HALF : (core + 1) * HALF] = sums[core][:, :HALF] * inverse
+
+    cosine, sine = cos_ref[...], sin_ref[...]
+
+    def turned(values):
+        return (values * cosine + pltpu.roll(values, 64, 1) * sine).astype(bf16)
+
+    def columns(first):
+        return proj_ref[:, pl.ds(pl.multiple_of(first, 128), 128)]
+
+    query = jnp.concatenate(
+        [turned(columns(head * 1024 + group * 128)) for group in range(8)], axis=0
+    )
+    key_new = turned(columns(QW + head * 128))
+    value_new = columns(QW + KW + head * 128).astype(bf16)
+    fresh_ref[:, 0:128] = key_new
+    fresh_ref[:, 128:256] = value_new
+
+    scale = 1.0 / math.sqrt(HD)
+    across = (((1,), (1,)), ((), ()))
+    context = cache_ref.shape[2]
+    token = iota((128, context), 0) % 16
+    place = iota((128, context), 1)
+    scores = []
+    for row in range(4):
+        score = (
+            lax.dot_general(query, cache_ref[row, 0, :, :HD], across, preferred_element_type=f32)
+            * scale
+        )
+        live = (token // 4 == row) & (place < lengths_ref[row])
+        scores.append(jnp.where(live, score, -jnp.inf))
+    score = lax.dot_general(query, key_new, across, preferred_element_type=f32) * scale
+    asking, asked = iota((128, 16), 0) % 16, iota((128, 16), 1)
+    live = (asking // 4 == asked // 4) & (asking % 4 >= asked % 4)
+    scores.append(jnp.where(live, score, -jnp.inf))
+    highest = jnp.max(scores[4], axis=1, keepdims=True)
+    for score in scores[:4]:
+        highest = jnp.maximum(highest, jnp.max(score, axis=1, keepdims=True))
+    raised = [jnp.exp(score - highest) for score in scores]
+    denom = jnp.sum(raised[4], axis=1, keepdims=True)
+    for part in raised[:4]:
+        denom = denom + jnp.sum(part, axis=1, keepdims=True)
+    share = 1.0 / denom
+    mixed = jnp.dot((raised[4] * share).astype(bf16), value_new, preferred_element_type=f32)
+    for row in range(4):
+        mixed = mixed + jnp.dot(
+            (raised[row] * share).astype(bf16),
+            cache_ref[row, 0, :, HD:],
+            preferred_element_type=f32,
+        )
+    for group in range(8):
+        out_ref[:, group * 128 : (group + 1) * 128] = mixed[group * 16 : (group + 1) * 16].astype(
+            bf16
+        )
+
+
+def attend(lengths, parts, cosine, sine, cache):
+    rows, heads, context, width = cache.shape
+    return pl.pallas_call(
+        attend_kernel,
+        grid=(heads,),
+        in_specs=[
+            pl.BlockSpec(memory_space=pltpu.SMEM),
+            pl.BlockSpec((16, 16, HALF + 128), lambda n: (0, 0, 0)),
+            pl.BlockSpec((16, HD), lambda n: (0, 0)),
+            pl.BlockSpec((16, HD), lambda n: (0, 0)),
+            pl.BlockSpec((rows, 1, context, width), lambda n: (0, n, 0, 0)),
+        ],
+        out_specs=(
+            pl.BlockSpec((16, 1024), lambda n: (0, n)),
+            pl.BlockSpec((16, 256), lambda n: (0, n)),
+        ),
+        out_shape=(
+            jax.ShapeDtypeStruct((16, QW), bf16),
+            jax.ShapeDtypeStruct((16, 2 * KW), bf16),
+        ),
+        scratch_shapes=[pltpu.VMEM((16, 2 * HALF), f32)],
+        compiler_params=pltpu.CompilerParams(vmem_limit_bytes=VMEM),
+        name="attend",
+    )(lengths, parts, cosine, sine, cache)
+
+
+def angles_of(lengths, step_total):
+    half_dim = HD // 2
+    exponent = jnp.arange(half_dim).astype(f32) * (2.0 / HD)
+    freqs = jnp.power(f32(rope_base), -exponent)
+    positions = (lengths[:, None] + jnp.arange(step_total)[None, :]).reshape(-1)
+    angles = positions.astype(f32)[:, None] * freqs
+    cosine, sine = jnp.cos(angles), jnp.sin(angles)
+    return jnp.concatenate([cosine, cosine], axis=1), jnp.concatenate([-sine, sine], axis=1)
+
+
 OUT_PIECES = (
     (0, 0, 64, 0, 0),
     (1, 0, 64, 1, 0),
@@ -331,15 +399,15 @@
     return lax.optimization_barrier((value,) + after)[0]
 
 
-def gather_output(shard, after):
-    other = dp_permute(shard, 0, 1)
-    shard = tied(shard, *after)
-    behind = dp_permute(shard, 1, 0)
-    ahead = dp_permute(shard, 3, 0)
+def gather_output(shard, first, second, third):
+    ring = tied(shard, *first)
+    behind = dp_permute(ring, 1, 0)
+    ahead = dp_permute(ring, 3, 0)
+    other = dp_permute(tied(shard, *second), 0, 1)
     from_behind = dp_permute(jnp.concatenate([other, behind[:32]], axis=0), 1, 0)
     from_ahead = dp_permute(jnp.concatenate([other, ahead[32:]], axis=0), 3, 0)
-    far_low = dp_permute(from_behind[:32], 1, 0)
-    far_high = dp_permute(from_ahead[32:64], 3, 0)
+    far_low = dp_permute(tied(from_behind, *third)[:32], 1, 0)
+    far_high = dp_permute(tied(from_ahead, *third)[32:64], 3, 0)
     return shard, behind, ahead, other, from_behind, from_ahead, far_low, far_high
 
 
@@ -370,7 +438,9 @@
     kept = lax.dynamic_slice(qkv_local, (0, my_core * HALF), (64, HALF))
     given = lax.dynamic_slice(qkv_local, (0, (1 - my_core) * HALF), (64, HALF))
     taken = tensor_permute(given, 0, 0, 1)
-    ids_sent = tied(jnp.broadcast_to(ids_row, (GROUPS, TOK)), taken)
+    new_out = adamw(out_master, out_moment1, out_moment2, out_grad)
+    out_local = new_out[0].astype(bf16)[0]
+    ids_sent = tied(jnp.broadcast_to(ids_row[None], (GROUPS, 1, TOK)), taken)
     all_ids = lax.all_to_all(ids_sent, "dp", split_axis=0, concat_axis=0, tiled=True)
 
     kept_z = dp_permute(kept, 0, 1)
@@ -402,12 +472,9 @@
         near_z,
         far_taken_z,
     )
-    new_out = adamw(out_master, out_moment1, out_moment2, out_grad)
-    out_local = new_out[0].astype(bf16)[0]
 
     table = embed_table.transpose(1, 2, 0).reshape(FEAT, VOCAB_DEV)
-    local_ids = tied(all_ids - my_group * VOCAB_DEV, up, down, near)
-    sent = lookup(local_ids, table)
+    sent = lookup(tied(all_ids, up, down, near), table)
     received = lax.all_to_all(
         sent.reshape(GROUPS, SLOTS, FEAT), "dp", split_axis=0, concat_axis=0, tiled=True
     ).reshape(GROUPS * SLOTS, FEAT)
@@ -419,43 +486,19 @@
             for step in (0, 1, 3, 2)
         ]
     )
-    order = (blocks[:, None] * 64 + jnp.arange(64)[None, :]).reshape(1, FEAT).astype(jnp.int32)
-    hidden, scaled, squares = arrange(ids_row, received, norm_gain.reshape(1, FEAT), order)
+    hidden, scaled, squares = arrange(all_ids, received, norm_gain)
     scaled_pair = tensor_permute(scaled, 0, 0, 1)
 
+    cosine, sine = angles_of(lengths, step_total)
     partial = project(scaled, scaled_pair, squares, qkv_pieces)
     parts = lax.all_to_all(
         partial.reshape(16, 16, HALF + 128), "tensor", split_axis=0, concat_axis=0, tiled=True
     )
-    summed = jnp.sum(parts.astype(f32).reshape(8, 2, 16, HALF + 128), axis=0)
-    square_sum = summed[0, :, HALF] + summed[1, :, HALF]
-    inverse = lax.rsqrt(square_sum / D + norm_epsilon)
-    projected = jnp.concatenate([summed[0, :, :HALF], summed[1, :, :HALF]], axis=-1)
-    projected = projected * inverse[:, None]
-
-    own_tokens = 16
-    own_rows = own_tokens // step_total
-    projected = projected.reshape(own_rows, step_total, -1)
-    query = projected[..., :QW].reshape(own_rows, step_total, QH, HD)
-    key_new = projected[..., QW : QW + KW].reshape(own_rows, step_total, KVH, HD)
-    value_new = projected[..., QW + KW :].reshape(own_rows, step_total, KVH, HD)
-    positions = lengths[:, None] + jnp.arange(step_total)[None, :]
-    query = rotate(query, positions).astype(bf16)
-    key_new = rotate(key_new, positions).astype(bf16)
-    value_new = value_new.astype(bf16)
-    fresh_kv = jnp.concatenate([key_new, value_new], axis=-1)
-    attended = attend(
-        query.reshape(own_rows, step_total, KVH, QH // KVH, HD),
-        key_new,
-        value_new,
-        kv_cache,
-        lengths,
-    )
-    attended = attended.reshape(own_tokens, QW)
-
-    out_pieces = gather_output(out_local, (far, far_z))
+    attended, fresh_flat = attend(lengths, parts, cosine, sine, kv_cache)
+    fresh_kv = fresh_flat.reshape(4, step_total, KVH, 2 * HD)
 
     other = tensor_permute(attended, 1, 0, 0)
+    out_pieces = gather_output(out_local, (far, far_z, far_taken_z,), (far, far_z, far_taken_z,), (other,))
     both = jnp.stack([attended, other])
     quad = jnp.stack([both] + [tensor_permute(both, 0, step, 0) for step in (1, 2, 3)])
     away = tensor_permute(quad, 0, 0, 1)

time: 142 us -> 132 us (0.930)
  local copies, waits for them, and re-layouts: 16.5 us -> 9.32 us
  starting transfers between devices: 59.7 us -> 53.9 us
  Pallas kernels: 19.2 us -> 24.8 us
  waiting for transfers between devices: 21.9 us -> 27.5 us
  matrix products: 5.89 us -> 1.29 us
  other arithmetic: 16.3 us -> 13.8 us
    all_to_all x1, waiting for transfers between devices: 0.65 us -> 13.3 us  [on_device(): lax.all_to_all(partial.reshape(16, 16, HALF + 128), 'tensor', split_axis=...]
    ppermute x17, waiting for transfers between devices: 12.1 us -> 1.8 us  [dp_permute(): return lax.ppermute(value, 'dp', pairs)]
    pallas_call x0 -> x1, Pallas kernels: none -> 6.22 us  [attend(): pl.pallas_call(attend_kernel, grid=(heads,), in_specs=[pl.BlockSpec(memor...]
    dot_general x4 -> x0, matrix products: 4.6 us -> none  [the longest x1 2.35 us: attend(): jnp.einsum('rsngd,rncd->rngsc', queries, cache_keys, preferred_element_ty...]
    ppermute x7, waiting for transfers between devices: 9.14 us -> 12.4 us  [tensor_permute(): return lax.ppermute(value, 'tensor', pairs)]
    ppermute x7, starting transfers between devices: 14.9 us -> 11.9 us  [tensor_permute(): return lax.ppermute(value, 'tensor', pairs)]
    slice x5 -> x2, local copies, waits for them, and re-layouts: 2.2 us -> 0.04 us  [the longest x1 0.02 us: gather_output(): far_high = dp_permute(tied(from_ahead, *third)[32:64], 3, 0)]
    reduce_sum x3 -> x0, other arithmetic: 2.02 us -> none  [the longest x1 1.56 us: on_device(): summed = jnp.sum(parts.astype(f32).reshape(8, 2, 16, HALF + 128), axis=0)]
  transfers between devices with their start and end apart: 27 -> 27, of which waited for: 8 -> 9; matrix products, arithmetic and copies ran while one was open for 20% -> 11% of each run, Pallas kernels for 14% -> 19%
where the time goes in v3:
time: 132 us
  starting transfers between devices  53.9 us (41%)
  waiting for transfers between devices  27.5 us (21%)
  Pallas kernels  24.8 us (19%)
  other arithmetic  13.8 us (10%)
  local copies, waits for them, and re-layouts  9.32 us (7%)
    ppermute x17, starting transfers between devices, dp_permute(): return lax.ppermute(value, 'dp', pairs)  27.7 us
    all_to_all x1, waiting for transfers between devices, on_device(): lax.all_to_all(partial.reshape(16, 16, HALF + 128), 'tensor', split_axis=...  13.3 us
    ppermute x7, waiting for transfers between devices, tensor_permute(): return lax.ppermute(value, 'tensor', pairs)  12.4 us
    ppermute x7, starting transfers between devices, tensor_permute(): return lax.ppermute(value, 'tensor', pairs)  11.9 us
    pallas_call x1, Pallas kernels, lookup(): pl.pallas_call(lookup_kernel, grid=(steps,), in_specs=[pl.BlockSpec((GROU...  9.36 us
    pallas_call x1, Pallas kernels, attend(): pl.pallas_call(attend_kernel, grid=(heads,), in_specs=[pl.BlockSpec(memor...  6.22 us
    all_to_all x1, starting transfers between devices, on_device(): lax.all_to_all(partial.reshape(16, 16, HALF + 128), 'tensor', split_axis=...  5.85 us
    pallas_call x1, Pallas kernels, project(): pl.pallas_call(project_kernel, grid=(width // COLS,), in_specs=[pl.BlockS...  5.65 us
  transfers between devices with their start and end apart: 27, of which 9 were waited for; matrix products, arithmetic and copies ran while one was open for 11% of the time, Pallas kernels for 19%

profile of v3, /device:TPU:1, one launch (start us, length us, event | category | flops | bytes accessed | tf_op | source)
XLA Modules:
  0.0 131.9 jit_solution(657621918136541526)
XLA Ops:
  0.7 4.9 %fusion.25 = (bf16[1,64,5120]{2,1,0:T(8,128)(2,1)S(1)}, f32[1,64,5120]{2,1,0:T(8,128)}, f32[1,64,5120]{2,1,0:T(8,128)}, f32[1,64,5120]{2,1,0:T(8,128)}) fusion(f32[1,64,5120]{2,1,0:T(8,128)} %param.13, bf16[1,64,5120]{2,1,0:T(8,128)(2,1)} %param.16, f32[1,64,5120]{2,1,0:T(8,128)} %param.14, f32[1,64,5120]{2,1,0:T(8,128)} %param.15), kind=kLoop, calls=%fused_computation.65 | loop fusion | flops 5570560 | bytes 9175040 | tf_op jit(solution)/shard_map/convert_element_type | solution.py:437
  5.6 1.5 %collective-permute-start = (bf16[64,2560]{1,0:T(8,128)(2,1)S(1)}, bf16[64,2560]{1,0:T(8,128)(2,1)S(1)}, u32[]{:S(2)}, u32[]{:S(2)}) collective-permute-start(bf16[64,2560]{1,0:T(8,128)(2,1)S(1)} %get-tuple-element.41), channel_id=1, source_target_pairs={{0,1},{1,0},{2,3},{3,2},{4,5},{5,4},{6,7},{7,6},{8,9},{9,8},{10,11... | collective-permute-start | bytes 983048 | tf_op jit(solution)/shard_map/ppermute | solution.py:395
  7.1 1.3 collective-permute-done.rest_6_
  8.4 2.6 %collective-permute-start.3 = (bf16[64,2560]{1,0:T(8,128)(2,1)S(1)}, bf16[64,2560]{1,0:T(8,128)(2,1)S(1)}, u32[]{:S(2)}, u32[]{:S(2)}) collective-permute-start(bf16[64,2560]{1,0:T(8,128)(2,1)S(1)} %collective-permute-done.rest_6_), channel_id=1, source_target_pairs={{0,96},{16,112},{32,0},{48,16},{64,32},{80,48},{96,64},{112,80},{1... | collective-permute-start | bytes 983048 | tf_op jit(solution)/shard_map/ppermute | solution.py:387
  10.9 3.6 %collective-permute-start.1 = (bf16[64,2560]{1,0:T(8,128)(2,1)S(1)}, bf16[64,2560]{1,0:T(8,128)(2,1)S(1)}, u32[]{:S(2)}, u32[]{:S(2)}) collective-permute-start(bf16[64,2560]{1,0:T(8,128)(2,1)S(1)} %get-tuple-element.40.rest_0_), channel_id=1, source_target_pairs={{0,16},{16,0},{32,48},{48,32},{64,80},{80,64},{96,112},{112,96},{1... | collective-permute-start | bytes 983048 | tf_op jit(solution)/shard_map/ppermute | solution.py:387
  14.5 0.1 copy.21
  14.6 0.1 broadcast_in_dim.6
  14.7 0.6 broadcast_in_dim.7
  15.4 4.0 %all-to-all-start = ((s32[8,1,256]{2,1,0:T(1,128)}), s32[8,1,256]{2,1,0:T(1,128)S(1)}, u32[]{:S(2)}, u32[]{:S(2)}) async-start(s32[8,1,256]{2,1,0:T(1,128)} %broadcast_in_dim.7), calls=%async_computation | async-start | bytes 16384 | tf_op jit(solution)/shard_map/all_to_all | solution.py:444
  19.3 3.0 %collective-permute-start.9 = (bf16[64,2560]{1,0:T(8,128)(2,1)S(1)}, bf16[64,2560]{1,0:T(8,128)(2,1)}, u32[]{:S(2)}, u32[]{:S(2)}) collective-permute-start(bf16[64,2560]{1,0:T(8,128)(2,1)S(1)} %collective-permute-done.rest_6_), channel_id=1, source_target_pairs={{0,16},{16,0},{32,48},{48,32},{64,80},{80,64},{96,112},{112,96},{1... | collective-permute-start | bytes 983048 | tf_op jit(solution)/shard_map/ppermute | solution.py:387
  22.4 1.4 %pad_maximum_fusion.5 = (bf16[160,2560]{1,0:T(8,128)(2,1)}, bf16[160,2560]{1,0:T(8,128)(2,1)}) fusion(bf16[32,2560]{1,0:T(8,128)(2,1)S(1)} %slice.105, bf16[64,2560]{1,0:T(8,128)(2,1)S(1)} %collective-permute-done.1.rest_1_, bf16[64,2560]{1,0:T(8,128)(2,1)S(1)} %get-tuple-element.40.rest_0_, bf16[32,2560]{1,0:T(8,128)(2,1)S(1)} %slice.104), kind=kLoop, calls=%fused_computation.17 | loop fusion | flops 3686400 | bytes 2621440 | tf_op jit(solution)/shard_map/concatenate | solution.py:451
  23.8 2.4 %collective-permute-start.5 = (bf16[160,2560]{1,0:T(8,128)(2,1)}, bf16[160,2560]{1,0:T(8,128)(2,1)S(1)}, u32[]{:S(2)}, u32[]{:S(2)}) collective-permute-start(bf16[160,2560]{1,0:T(8,128)(2,1)} %get-tuple-element.38), channel_id=1, source_target_pairs={{0,96},{16,112},{32,0},{48,16},{64,32},{80,48},{96,64},{112,80},{1... | collective-permute-start | bytes 2457608 | tf_op jit(solution)/shard_map/ppermute | solution.py:387
  26.2 0.7 constant_dynamic-update-slice_fusion.1
  26.9 0.8 constant_dynamic-update-slice_fusion
  27.7 2.2 %collective-permute-start.10 = (bf16[128,2560]{1,0:T(8,128)(2,1)}, bf16[128,2560]{1,0:T(8,128)(2,1)}, u32[]{:S(2)}, u32[]{:S(2)}) collective-permute-start(bf16[128,2560]{1,0:T(8,128)(2,1)} %constant_dynamic-update-slice_fusion), channel_id=1, source_target_pairs={{0,16},{16,0},{32,48},{48,32},{64,80},{80,64},{96,112},{112,96},{1... | collective-permute-start | bytes 1966088 | tf_op jit(solution)/shard_map/ppermute | solution.py:387
  29.9 0.6 copy-done.12
  30.5 9.4 %lookup.1 = bf16[512,512]{1,0:T(8,128)(2,1)} custom-call(s32[8,1,256]{2,1,0:T(1,128)} %copy-done.12, bf16[512,9504]{1,0:T(8,128)(2,1)} %bitcast.109), custom_call_target="tpu_custom_call" | custom-call | flops 30000001024 | bytes 10000000 | tf_op jit(solution)/shard_map/lookup/pallas_call | solution.py:99
  39.9 4.5 %all-to-all-start.1 = ((bf16[8,64,512]{2,1,0:T(8,128)(2,1)}), bf16[8,64,512]{2,1,0:T(8,128)(2,1)S(1)}, u32[]{:S(2)}, u32[]{:S(2)}) async-start(bf16[8,64,512]{2,1,0:T(8,128)(2,1)} %bitcast.106), calls=%async_computation.1 | async-start | bytes 1048576 | tf_op jit(solution)/shard_map/all_to_all | solution.py:478
  44.4 0.7 collective-permute-done.4.rest_2_
  45.1 0.8 slice.108
  45.9 0.8 collective-permute-start.7
  46.6 0.8 slice.109
  47.4 1.9 %collective-permute-start.8 = (bf16[64,2560]{1,0:T(8,128)(2,1)}, bf16[64,2560]{1,0:T(8,128)(2,1)}, u32[]{:S(2)}, u32[]{:S(2)}) collective-permute-start(bf16[64,2560]{1,0:T(8,128)(2,1)} %slice.109), channel_id=1, source_target_pairs={{0,96},{16,112},{32,0},{48,16},{64,32},{80,48},{96,64},{112,80},{1... | collective-permute-start | bytes 983048 | tf_op jit(solution)/shard_map/ppermute | solution.py:387
  49.4 2.3 %collective-permute-start.11 = (bf16[64,2560]{1,0:T(8,128)(2,1)S(1)}, bf16[64,2560]{1,0:T(8,128)(2,1)}, u32[]{:S(2)}, u32[]{:S(2)}) collective-permute-start(bf16[64,2560]{1,0:T(8,128)(2,1)S(1)} %pad_maximum_fusion.6.rest_10_), channel_id=1, source_target_pairs={{0,16},{16,0},{32,48},{48,32},{64,80},{80,64},{96,112},{112,96},{1... | collective-permute-start | bytes 983048 | tf_op jit(solution)/shard_map/ppermute | solution.py:387
  51.8 4.2 %convert_bitcast_fusion = (bf16[64,4096]{1,0:T(8,128)(2,1)S(1)}, f32[1,64,4096]{2,1,0:T(8,128)}, f32[1,64,4096]{2,1,0:T(8,128)}, f32[1,64,4096]{2,1,0:T(8,128)}) fusion(f32[1,64,4096]{2,1,0:T(8,128)} %param.17, bf16[1,64,4096]{2,1,0:T(8,128)(2,1)} %param.20, f32[1,64,4096]{2,1,0:T(8,128)} %param.18, f32[1,64,4096]{2,1,0:T(8,128)} %param.19), kind=kLoop, calls=%fused_computation.18 | loop fusion | flops 4456448 | bytes 7340032 | tf_op jit(solution)/shard_map/squeeze | solution.py:442
  56.0 0.0 copy-start.5
  56.0 0.8 copy-done.5
  56.8 2.6 %arrange.1 = (bf16[256,512]{1,0:T(8,128)(2,1)}, bf16[256,512]{1,0:T(8,128)(2,1)}, bf16[256,128]{1,0:T(8,128)(2,1)}) custom-call(s32[8,1,256]{2,1,0:T(1,128)} %copy-done.12, bf16[512,512]{1,0:T(8,128)(2,1)} %bitcast.96, f32[8,64]{1,0:T(8,128)} %gain_ref.1), custom_call_target="tpu_custom_call" | custom-call | tf_op jit(solution)/shard_map/arrange/pallas_call | solution.py:144
  59.3 4.3 %collective-permute-start.6 = (bf16[256,512]{1,0:T(8,128)(2,1)}, bf16[256,512]{1,0:T(8,128)(2,1)S(1)}, u32[]{:S(2)}, u32[]{:S(2)}) collective-permute-start(bf16[256,512]{1,0:T(8,128)(2,1)} %get-tuple-element.23.own_ref), channel_id=1, source_target_pairs={{0,1},{1,0},{2,3},{3,2},{4,5},{5,4},{6,7},{7,6},{8,9},{9,8},{10,11... | collective-permute-start | bytes 786440 | tf_op jit(solution)/shard_map/ppermute | solution.py:395
  63.7 2.7 %collective-permute-start.18 = (bf16[64,4096]{1,0:T(8,128)(2,1)S(1)}, bf16[64,4096]{1,0:T(8,128)(2,1)S(1)}, u32[]{:S(2)}, u32[]{:S(2)}) collective-permute-start(bf16[64,4096]{1,0:T(8,128)(2,1)S(1)} %get-tuple-element.26.rest_0_), channel_id=1, source_target_pairs={{0,96},{16,112},{32,0},{48,16},{64,32},{80,48},{96,64},{112,80},{1... | collective-permute-start | bytes 1572872 | tf_op jit(solution)/shard_map/ppermute | solution.py:387
  66.3 0.8 collective-permute-start.19
  67.2 0.7 copy-done.11
  67.9 5.6 %project.1 = bf16[256,2688]{1,0:T(8,128)(2,1)} custom-call(bf16[256,512]{1,0:T(8,128)(2,1)} %get-tuple-element.23.own_ref, bf16[256,512]{1,0:T(8,128)(2,1)} %copy-done.11, bf16[256,128]{1,0:T(8,128)(2,1)} %get-tuple-element.24.squares_ref, bf16[64,2560]{1,0:T(8,128)(2,1)} %copy-done.2, bf16[64,2560]{1,0:T(8,128)(2,1)} %copy-done.8, ...), custom_call_target="tpu_custom_call" | custom-call | flops 1342177280 | bytes 5242880 | tf_op jit(solution)/shard_map/project/pallas_call | solution.py:209
  73.5 0.0 copy-start.13
  73.5 5.9 %all-to-all-start.2 = ((bf16[16,16,2688]{2,1,0:T(8,128)(2,1)}), bf16[16,16,2688]{2,1,0:T(8,128)(2,1)}, u32[]{:S(2)}, u32[]{:S(2)}) async-start(bf16[16,16,2688]{2,1,0:T(8,128)(2,1)} %bitcast.94), calls=%async_computation.2 | async-start | bytes 2752512 | tf_op jit(solution)/shard_map/all_to_all | solution.py:494
  79.4 0.1 add_convert_fusion
  79.5 0.1 convert_element_type.41
  79.6 1.0 collective-permute-done.19.rest_3_
  80.7 1.4 %pad_maximum_fusion.1 = (bf16[96,4096]{1,0:T(8,128)(2,1)}, bf16[96,4096]{1,0:T(8,128)(2,1)}) fusion(bf16[64,4096]{1,0:T(8,128)(2,1)S(1)} %collective-permute-done.19.rest_3_, bf16[32,4096]{1,0:T(8,128)(2,1)S(1)} %slice.127, bf16[32,4096]{1,0:T(8,128)(2,1)S(1)} %slice.126), kind=kLoop, calls=%fused_computation.13 | loop fusion | flops 2752512 | bytes 2621440 | tf_op jit(solution)/shard_map/concatenate | solution.py:408
  82.0 2.7 %collective-permute-start.21 = (bf16[96,4096]{1,0:T(8,128)(2,1)}, bf16[96,4096]{1,0:T(8,128)(2,1)S(1)}, u32[]{:S(2)}, u32[]{:S(2)}) collective-permute-start(bf16[96,4096]{1,0:T(8,128)(2,1)} %get-tuple-element.42), channel_id=1, source_target_pairs={{0,96},{16,112},{32,0},{48,16},{64,32},{80,48},{96,64},{112,80},{1... | collective-permute-start | bytes 2359304 | tf_op jit(solution)/shard_map/ppermute | solution.py:387
  84.7 0.1 fusion.21
  84.8 0.7 pad_maximum_fusion.8
  85.5 13.3 %all-to-all-done.2.parts_ref = bf16[16,16,2688]{2,1,0:T(8,128)(2,1)} async-done(((bf16[16,16,2688]{2,1,0:T(8,128)(2,1)}), bf16[16,16,2688]{2,1,0:T(8,128)(2,1)}, u32[]{:S(2)}, u32[]{:S(2)}) %all-to-all-start.2) | async-done | bytes 1376288 | tf_op jit(solution)/shard_map/all_to_all | solution.py:494
  98.9 6.2 %attend.1 = (bf16[16,4096]{1,0:T(8,128)(2,1)}, bf16[16,1024]{1,0:T(8,128)(2,1)}) custom-call(s32[4]{0:T(128)} %lengths_ref.1, bf16[16,16,2688]{2,1,0:T(8,128)(2,1)} %all-to-all-done.2.parts_ref, f32[16,128]{1,0:T(8,128)} %get-tuple-element.49.cos_ref, f32[16,128]{1,0:T(8,128)} %get-tuple-element.50.sin_ref, bf16[4,4,384,256]{3,2,1,0:T(8,128)(2,1)} %cache_ref.1), custom_call_target="tpu_custom_call" | custom-call | tf_op jit(solution)/shard_map/attend/pallas_call | solution.py:302
  105.1 0.3 collective-permute-start.12
  105.5 0.1 stack.67.blocks_ref
  105.6 1.4 %reshape.71 = bf16[4,4,4,256]{3,2,1,0:T(4,128)(2,1)} reshape(bf16[16,1024]{1,0:T(8,128)(2,1)} %get-tuple-element.29) | data formatting | bytes 65536 | tf_op jit(solution)/shard_map/reshape | solution.py:498
  107.0 2.7 %collective-permute-done.12 = bf16[16,4096]{1,0:T(8,128)(2,1)S(1)} collective-permute-done((bf16[16,4096]{1,0:T(8,128)(2,1)}, bf16[16,4096]{1,0:T(8,128)(2,1)S(1)}, u32[]{:S(2)}, u32[]{:S(2)}) %collective-permute-start.12) | collective-permute-done | bytes 131104 | tf_op jit(solution)/shard_map/ppermute | solution.py:395
  109.6 0.9 pad_maximum_fusion.7
  110.6 0.1 collective-permute-start.13
  110.6 2.8 %collective-permute-start.14 = (bf16[2,16,4096]{2,1,0:T(8,128)(2,1)S(1)}, bf16[2,16,4096]{2,1,0:T(8,128)(2,1)S(1)}, u32[]{:S(2)}, u32[]{:S(2)}) collective-permute-start(bf16[2,16,4096]{2,1,0:T(8,128)(2,1)S(1)} %get-tuple-element.44), channel_id=1, source_target_pairs={{0,4},{1,5},{2,6},{3,7},{4,0},{5,1},{6,2},{7,3},{8,12},{9,13},{10,... | collective-permute-start | bytes 786440 | tf_op jit(solution)/shard_map/ppermute | solution.py:395
  113.4 1.3 collective-permute-start.15
  114.8 0.1 collective-permute-start.22
  114.9 2.7 %collective-permute-start.23 = (bf16[32,4096]{1,0:T(8,128)(2,1)S(1)}, bf16[32,4096]{1,0:T(8,128)(2,1)S(1)}, u32[]{:S(2)}, u32[]{:S(2)}) collective-permute-start(bf16[32,4096]{1,0:T(8,128)(2,1)S(1)} %slice.103), channel_id=1, source_target_pairs={{0,96},{16,112},{32,0},{48,16},{64,32},{80,48},{96,64},{112,80},{1... | collective-permute-start | bytes 786440 | tf_op jit(solution)/shard_map/ppermute | solution.py:387
  117.6 0.2 broadcast_in_dim.16
  117.9 0.1 collective-permute-done.13
  118.0 6.8 %collective-permute-done.14 = bf16[2,16,4096]{2,1,0:T(8,128)(2,1)S(1)} collective-permute-done((bf16[2,16,4096]{2,1,0:T(8,128)(2,1)S(1)}, bf16[2,16,4096]{2,1,0:T(8,128)(2,1)S(1)}, u32[]{:S(2)}, u32[]{:S(2)}) %collective-permute-start.14) | collective-permute-done | bytes 262176 | tf_op jit(solution)/shard_map/ppermute | solution.py:395
  124.8 0.5 collective-permute-done.15
  125.2 0.1 pad_maximum_fusion
  125.4 1.6 %collective-permute-start.16 = (bf16[4,2,16,4096]{3,2,1,0:T(8,128)(2,1)S(1)}, bf16[4,2,16,4096]{3,2,1,0:T(8,128)(2,1)S(1)}, u32[]{:S(2)}, u32[]{:S(2)}) collective-permute-start(bf16[4,2,16,4096]{3,2,1,0:T(8,128)(2,1)S(1)} %pad_maximum_fusion), channel_id=1, source_target_pairs={{0,1},{1,0},{2,3},{3,2},{4,5},{5,4},{6,7},{7,6},{8,9},{9,8},{10,11... | collective-permute-start | bytes 3145736 | tf_op jit(solution)/shard_map/ppermute | solution.py:395
  127.2 1.0 collect.1
  128.2 1.1 collective-permute-done.16
  129.5 1.3 fusion.2
  130.8 1.1 reshape.70
  (76 shorter events, 0.6 us)
Async XLA Ops:
  0.7 13.9 %copy-start.14 = (s32[64,4]{0,1:T(4,128)S(1)}, s32[64,4]{0,1:T(4,128)}, u32[]{:S(2)}) copy-start(s32[64,4]{0,1:T(4,128)} %param.23) | copy-start | bytes 3076
  5.6 22.1 %copy-start.2 = (bf16[64,2560]{1,0:T(8,128)(2,1)}, bf16[64,2560]{1,0:T(8,128)(2,1)S(1)}, u32[]{:S(2)}) copy-start(bf16[64,2560]{1,0:T(8,128)(2,1)S(1)} %get-tuple-element.40.rest_0_) | copy-start | bytes 983044
  5.6 2.8 %collective-permute-start = (bf16[64,2560]{1,0:T(8,128)(2,1)S(1)}, bf16[64,2560]{1,0:T(8,128)(2,1)S(1)}, u32[]{:S(2)}, u32[]{:S(2)}) collective-permute-start(bf16[64,2560]{1,0:T(8,128)(2,1)S(1)} %get-tuple-element.41), channel_id=1, source_target_pairs={{0,1},{1,0},{2,3},{3,2},{4,5},{5,4},{6,7},{7,6},{8,9},{9,8},{10,11... | collective-permute-start | bytes 983048 | tf_op jit(solution)/shard_map/ppermute | solution.py:395
  8.4 19.3 %copy-start.10 = (bf16[64,2560]{1,0:T(8,128)(2,1)}, bf16[64,2560]{1,0:T(8,128)(2,1)S(1)}, u32[]{:S(2)}) copy-start(bf16[64,2560]{1,0:T(8,128)(2,1)S(1)} %collective-permute-done.rest_6_) | copy-start | bytes 983044
  8.4 13.9 %collective-permute-start.3 = (bf16[64,2560]{1,0:T(8,128)(2,1)S(1)}, bf16[64,2560]{1,0:T(8,128)(2,1)S(1)}, u32[]{:S(2)}, u32[]{:S(2)}) collective-permute-start(bf16[64,2560]{1,0:T(8,128)(2,1)S(1)} %collective-permute-done.rest_6_), channel_id=1, source_target_pairs={{0,96},{16,112},{32,0},{48,16},{64,32},{80,48},{96,64},{112,80},{1... | collective-permute-start | bytes 983048 | tf_op jit(solution)/shard_map/ppermute | solution.py:387
  10.9 11.4 %collective-permute-start.2 = (bf16[64,2560]{1,0:T(8,128)(2,1)S(1)}, bf16[64,2560]{1,0:T(8,128)(2,1)S(1)}, u32[]{:S(2)}, u32[]{:S(2)}) collective-permute-start(bf16[64,2560]{1,0:T(8,128)(2,1)S(1)} %collective-permute-done.rest_6_), channel_id=1, source_target_pairs={{0,32},{16,48},{32,64},{48,80},{64,96},{80,112},{96,0},{112,16},{1... | collective-permute-start | bytes 983048 | tf_op jit(solution)/shard_map/ppermute | solution.py:387
  10.9 11.4 %collective-permute-start.1 = (bf16[64,2560]{1,0:T(8,128)(2,1)S(1)}, bf16[64,2560]{1,0:T(8,128)(2,1)S(1)}, u32[]{:S(2)}, u32[]{:S(2)}) collective-permute-start(bf16[64,2560]{1,0:T(8,128)(2,1)S(1)} %get-tuple-element.40.rest_0_), channel_id=1, source_target_pairs={{0,16},{16,0},{32,48},{48,32},{64,80},{80,64},{96,112},{112,96},{1... | collective-permute-start | bytes 983048 | tf_op jit(solution)/shard_map/ppermute | solution.py:387
  15.4 14.5 %all-to-all-start = ((s32[8,1,256]{2,1,0:T(1,128)}), s32[8,1,256]{2,1,0:T(1,128)S(1)}, u32[]{:S(2)}, u32[]{:S(2)}) async-start(s32[8,1,256]{2,1,0:T(1,128)} %broadcast_in_dim.7), calls=%async_computation | async-start | bytes 16384 | tf_op jit(solution)/shard_map/all_to_all | solution.py:444
  19.3 47.0 %collective-permute-start.9 = (bf16[64,2560]{1,0:T(8,128)(2,1)S(1)}, bf16[64,2560]{1,0:T(8,128)(2,1)}, u32[]{:S(2)}, u32[]{:S(2)}) collective-permute-start(bf16[64,2560]{1,0:T(8,128)(2,1)S(1)} %collective-permute-done.rest_6_), channel_id=1, source_target_pairs={{0,16},{16,0},{32,48},{48,32},{64,80},{80,64},{96,112},{112,96},{1... | collective-permute-start | bytes 983048 | tf_op jit(solution)/shard_map/ppermute | solution.py:387
  22.3 5.4 %copy-start.6 = (bf16[64,2560]{1,0:T(8,128)(2,1)}, bf16[64,2560]{1,0:T(8,128)(2,1)S(1)}, u32[]{:S(2)}) copy-start(bf16[64,2560]{1,0:T(8,128)(2,1)S(1)} %collective-permute-done.3.rest_9_) | copy-start | bytes 983044
  22.3 5.4 %copy-start.7 = (bf16[64,2560]{1,0:T(8,128)(2,1)}, bf16[64,2560]{1,0:T(8,128)(2,1)S(1)}, u32[]{:S(2)}) copy-start(bf16[64,2560]{1,0:T(8,128)(2,1)S(1)} %collective-permute-done.2.rest_8_) | copy-start | bytes 983044
  22.3 17.5 %copy-start.8 = (bf16[64,2560]{1,0:T(8,128)(2,1)}, bf16[64,2560]{1,0:T(8,128)(2,1)S(1)}, u32[]{:S(2)}) copy-start(bf16[64,2560]{1,0:T(8,128)(2,1)S(1)} %collective-permute-done.1.rest_1_) | copy-start | bytes 983044
  23.8 22.9 %collective-permute-start.5 = (bf16[160,2560]{1,0:T(8,128)(2,1)}, bf16[160,2560]{1,0:T(8,128)(2,1)S(1)}, u32[]{:S(2)}, u32[]{:S(2)}) collective-permute-start(bf16[160,2560]{1,0:T(8,128)(2,1)} %get-tuple-element.38), channel_id=1, source_target_pairs={{0,96},{16,112},{32,0},{48,16},{64,32},{80,48},{96,64},{112,80},{1... | collective-permute-start | bytes 2457608 | tf_op jit(solution)/shard_map/ppermute | solution.py:387
  26.2 18.9 %collective-permute-start.4 = (bf16[160,2560]{1,0:T(8,128)(2,1)}, bf16[160,2560]{1,0:T(8,128)(2,1)S(1)}, u32[]{:S(2)}, u32[]{:S(2)}) collective-permute-start(bf16[160,2560]{1,0:T(8,128)(2,1)} %get-tuple-element.39), channel_id=1, source_target_pairs={{0,32},{16,48},{32,64},{48,80},{64,96},{80,112},{96,0},{112,16},{1... | collective-permute-start | bytes 2457608 | tf_op jit(solution)/shard_map/ppermute | solution.py:387
  27.7 39.5 %collective-permute-start.10 = (bf16[128,2560]{1,0:T(8,128)(2,1)}, bf16[128,2560]{1,0:T(8,128)(2,1)}, u32[]{:S(2)}, u32[]{:S(2)}) collective-permute-start(bf16[128,2560]{1,0:T(8,128)(2,1)} %constant_dynamic-update-slice_fusion), channel_id=1, source_target_pairs={{0,16},{16,0},{32,48},{48,32},{64,80},{80,64},{96,112},{112,96},{1... | collective-permute-start | bytes 1966088 | tf_op jit(solution)/shard_map/ppermute | solution.py:387
  29.9 0.6 copy-start.12
  39.9 16.1 %all-to-all-start.1 = ((bf16[8,64,512]{2,1,0:T(8,128)(2,1)}), bf16[8,64,512]{2,1,0:T(8,128)(2,1)S(1)}, u32[]{:S(2)}, u32[]{:S(2)}) async-start(bf16[8,64,512]{2,1,0:T(8,128)(2,1)} %bitcast.106), calls=%async_computation.1 | async-start | bytes 1048576 | tf_op jit(solution)/shard_map/all_to_all | solution.py:478
  45.1 10.9 %copy-start.4 = (bf16[160,2560]{1,0:T(8,128)(2,1)}, bf16[160,2560]{1,0:T(8,128)(2,1)S(1)}, u32[]{:S(2)}) copy-start(bf16[160,2560]{1,0:T(8,128)(2,1)S(1)} %collective-permute-done.4.rest_2_) | copy-start | bytes 2457604
  45.9 13.5 %collective-permute-start.7 = (bf16[64,2560]{1,0:T(8,128)(2,1)}, bf16[64,2560]{1,0:T(8,128)(2,1)}, u32[]{:S(2)}, u32[]{:S(2)}) collective-permute-start(bf16[64,2560]{1,0:T(8,128)(2,1)} %slice.108), channel_id=1, source_target_pairs={{0,32},{16,48},{32,64},{48,80},{64,96},{80,112},{96,0},{112,16},{1... | collective-permute-start | bytes 983048 | tf_op jit(solution)/shard_map/ppermute | solution.py:387
  46.6 2.8 %copy-start.3 = (bf16[160,2560]{1,0:T(8,128)(2,1)}, bf16[160,2560]{1,0:T(8,128)(2,1)S(1)}, u32[]{:S(2)}) copy-start(bf16[160,2560]{1,0:T(8,128)(2,1)S(1)} %collective-permute-done.5.rest_3_) | copy-start | bytes 2457604
  47.4 16.2 %collective-permute-start.8 = (bf16[64,2560]{1,0:T(8,128)(2,1)}, bf16[64,2560]{1,0:T(8,128)(2,1)}, u32[]{:S(2)}, u32[]{:S(2)}) collective-permute-start(bf16[64,2560]{1,0:T(8,128)(2,1)} %slice.109), channel_id=1, source_target_pairs={{0,96},{16,112},{32,0},{48,16},{64,32},{80,48},{96,64},{112,80},{1... | collective-permute-start | bytes 983048 | tf_op jit(solution)/shard_map/ppermute | solution.py:387
  49.4 6.6 %copy-start.9 = (bf16[64,2560]{1,0:T(8,128)(2,1)}, bf16[64,2560]{1,0:T(8,128)(2,1)S(1)}, u32[]{:S(2)}) copy-start(bf16[64,2560]{1,0:T(8,128)(2,1)S(1)} %pad_maximum_fusion.6.rest_10_) | copy-start | bytes 983044
  49.4 14.2 %collective-permute-start.11 = (bf16[64,2560]{1,0:T(8,128)(2,1)S(1)}, bf16[64,2560]{1,0:T(8,128)(2,1)}, u32[]{:S(2)}, u32[]{:S(2)}) collective-permute-start(bf16[64,2560]{1,0:T(8,128)(2,1)S(1)} %pad_maximum_fusion.6.rest_10_), channel_id=1, source_target_pairs={{0,16},{16,0},{32,48},{48,32},{64,80},{80,64},{96,112},{112,96},{1... | collective-permute-start | bytes 983048 | tf_op jit(solution)/shard_map/ppermute | solution.py:387
  56.0 0.8 copy-start.5
  59.3 7.8 %collective-permute-start.6 = (bf16[256,512]{1,0:T(8,128)(2,1)}, bf16[256,512]{1,0:T(8,128)(2,1)S(1)}, u32[]{:S(2)}, u32[]{:S(2)}) collective-permute-start(bf16[256,512]{1,0:T(8,128)(2,1)} %get-tuple-element.23.own_ref), channel_id=1, source_target_pairs={{0,1},{1,0},{2,3},{3,2},{4,5},{5,4},{6,7},{7,6},{8,9},{9,8},{10,11... | collective-permute-start | bytes 786440 | tf_op jit(solution)/shard_map/ppermute | solution.py:395
  63.6 16.0 %collective-permute-start.17 = (bf16[64,4096]{1,0:T(8,128)(2,1)S(1)}, bf16[64,4096]{1,0:T(8,128)(2,1)S(1)}, u32[]{:S(2)}, u32[]{:S(2)}) collective-permute-start(bf16[64,4096]{1,0:T(8,128)(2,1)S(1)} %get-tuple-element.26.rest_0_), channel_id=1, source_target_pairs={{0,32},{16,48},{32,64},{48,80},{64,96},{80,112},{96,0},{112,16},{1... | collective-permute-start | bytes 1572872 | tf_op jit(solution)/shard_map/ppermute | solution.py:387
  63.7 15.9 %collective-permute-start.18 = (bf16[64,4096]{1,0:T(8,128)(2,1)S(1)}, bf16[64,4096]{1,0:T(8,128)(2,1)S(1)}, u32[]{:S(2)}, u32[]{:S(2)}) collective-permute-start(bf16[64,4096]{1,0:T(8,128)(2,1)S(1)} %get-tuple-element.26.rest_0_), channel_id=1, source_target_pairs={{0,96},{16,112},{32,0},{48,16},{64,32},{80,48},{96,64},{112,80},{1... | collective-permute-start | bytes 1572872 | tf_op jit(solution)/shard_map/ppermute | solution.py:387
  66.3 14.4 %collective-permute-start.19 = (bf16[64,4096]{1,0:T(8,128)(2,1)S(1)}, bf16[64,4096]{1,0:T(8,128)(2,1)S(1)}, u32[]{:S(2)}, u32[]{:S(2)}) collective-permute-start(bf16[64,4096]{1,0:T(8,128)(2,1)S(1)} %get-tuple-element.26.rest_0_), channel_id=1, source_target_pairs={{0,16},{16,0},{32,48},{48,32},{64,80},{80,64},{96,112},{112,96},{1... | collective-permute-start | bytes 1572872 | tf_op jit(solution)/shard_map/ppermute | solution.py:387
  67.2 0.7 copy-start.11
  73.5 5.9 %copy-start.13 = (s32[4]{0:T(128)S(1)}, s32[4]{0:T(128)}, u32[]{:S(2)}) copy-start(s32[4]{0:T(128)} %lengths_ref.1) | copy-start | bytes 52
  73.5 25.3 %all-to-all-start.2 = ((bf16[16,16,2688]{2,1,0:T(8,128)(2,1)}), bf16[16,16,2688]{2,1,0:T(8,128)(2,1)}, u32[]{:S(2)}, u32[]{:S(2)}) async-start(bf16[16,16,2688]{2,1,0:T(8,128)(2,1)} %bitcast.94), calls=%async_computation.2 | async-start | bytes 2752512 | tf_op jit(solution)/shard_map/all_to_all | solution.py:494
  79.6 2.5 %copy-start = (bf16[64,4096]{1,0:T(8,128)(2,1)}, bf16[64,4096]{1,0:T(8,128)(2,1)S(1)}, u32[]{:S(2)}) copy-start(bf16[64,4096]{1,0:T(8,128)(2,1)S(1)} %collective-permute-done.18.rest_2_) | copy-start | bytes 1572868
  82.0 32.7 %collective-permute-start.20 = (bf16[96,4096]{1,0:T(8,128)(2,1)}, bf16[96,4096]{1,0:T(8,128)(2,1)S(1)}, u32[]{:S(2)}, u32[]{:S(2)}) collective-permute-start(bf16[96,4096]{1,0:T(8,128)(2,1)} %get-tuple-element.43), channel_id=1, source_target_pairs={{0,32},{16,48},{32,64},{48,80},{64,96},{80,112},{96,0},{112,16},{1... | collective-permute-start | bytes 2359304 | tf_op jit(solution)/shard_map/ppermute | solution.py:387
  82.0 32.8 %collective-permute-start.21 = (bf16[96,4096]{1,0:T(8,128)(2,1)}, bf16[96,4096]{1,0:T(8,128)(2,1)S(1)}, u32[]{:S(2)}, u32[]{:S(2)}) collective-permute-start(bf16[96,4096]{1,0:T(8,128)(2,1)} %get-tuple-element.42), channel_id=1, source_target_pairs={{0,96},{16,112},{32,0},{48,16},{64,32},{80,48},{96,64},{112,80},{1... | collective-permute-start | bytes 2359304 | tf_op jit(solution)/shard_map/ppermute | solution.py:387
  105.1 4.5 %collective-permute-start.12 = (bf16[16,4096]{1,0:T(8,128)(2,1)}, bf16[16,4096]{1,0:T(8,128)(2,1)S(1)}, u32[]{:S(2)}, u32[]{:S(2)}) collective-permute-start(bf16[16,4096]{1,0:T(8,128)(2,1)} %get-tuple-element.25), channel_id=1, source_target_pairs={{0,8},{1,9},{2,10},{3,11},{4,12},{5,13},{6,14},{7,15},{8,0},{9,1},... | collective-permute-start | bytes 393224 | tf_op jit(solution)/shard_map/ppermute | solution.py:395
  110.6 7.5 %collective-permute-start.13 = (bf16[2,16,4096]{2,1,0:T(8,128)(2,1)S(1)}, bf16[2,16,4096]{2,1,0:T(8,128)(2,1)S(1)}, u32[]{:S(2)}, u32[]{:S(2)}) collective-permute-start(bf16[2,16,4096]{2,1,0:T(8,128)(2,1)S(1)} %get-tuple-element.44), channel_id=1, source_target_pairs={{0,2},{1,3},{2,4},{3,5},{4,6},{5,7},{6,0},{7,1},{8,10},{9,11},{10,... | collective-permute-start | bytes 786440 | tf_op jit(solution)/shard_map/ppermute | solution.py:395
  110.6 14.1 %collective-permute-start.14 = (bf16[2,16,4096]{2,1,0:T(8,128)(2,1)S(1)}, bf16[2,16,4096]{2,1,0:T(8,128)(2,1)S(1)}, u32[]{:S(2)}, u32[]{:S(2)}) collective-permute-start(bf16[2,16,4096]{2,1,0:T(8,128)(2,1)S(1)} %get-tuple-element.44), channel_id=1, source_target_pairs={{0,4},{1,5},{2,6},{3,7},{4,0},{5,1},{6,2},{7,3},{8,12},{9,13},{10,... | collective-permute-start | bytes 786440 | tf_op jit(solution)/shard_map/ppermute | solution.py:395
  113.4 11.8 %collective-permute-start.15 = (bf16[2,16,4096]{2,1,0:T(8,128)(2,1)S(1)}, bf16[2,16,4096]{2,1,0:T(8,128)(2,1)S(1)}, u32[]{:S(2)}, u32[]{:S(2)}) collective-permute-start(bf16[2,16,4096]{2,1,0:T(8,128)(2,1)S(1)} %get-tuple-element.44), channel_id=1, source_target_pairs={{0,6},{1,7},{2,0},{3,1},{4,2},{5,3},{6,4},{7,5},{8,14},{9,15},{10,... | collective-permute-start | bytes 786440 | tf_op jit(solution)/shard_map/ppermute | solution.py:395
  114.8 12.4 %collective-permute-start.22 = (bf16[32,4096]{1,0:T(8,128)(2,1)S(1)}, bf16[32,4096]{1,0:T(8,128)(2,1)S(1)}, u32[]{:S(2)}, u32[]{:S(2)}) collective-permute-start(bf16[32,4096]{1,0:T(8,128)(2,1)S(1)} %slice.102), channel_id=1, source_target_pairs={{0,32},{16,48},{32,64},{48,80},{64,96},{80,112},{96,0},{112,16},{1... | collective-permute-start | bytes 786440 | tf_op jit(solution)/shard_map/ppermute | solution.py:387
  114.9 12.2 %collective-permute-start.23 = (bf16[32,4096]{1,0:T(8,128)(2,1)S(1)}, bf16[32,4096]{1,0:T(8,128)(2,1)S(1)}, u32[]{:S(2)}, u32[]{:S(2)}) collective-permute-start(bf16[32,4096]{1,0:T(8,128)(2,1)S(1)} %slice.103), channel_id=1, source_target_pairs={{0,96},{16,112},{32,0},{48,16},{64,32},{80,48},{96,64},{112,80},{1... | collective-permute-start | bytes 786440 | tf_op jit(solution)/shard_map/ppermute | solution.py:387
  117.8 9.3 %copy-start.1 = (bf16[64,4096]{1,0:T(8,128)(2,1)S(1)}, bf16[64,4096]{1,0:T(8,128)(2,1)}, u32[]{:S(2)}) copy-start(bf16[64,4096]{1,0:T(8,128)(2,1)} %copy-done) | copy-start | bytes 1572868
  125.4 3.9 %collective-permute-start.16 = (bf16[4,2,16,4096]{3,2,1,0:T(8,128)(2,1)S(1)}, bf16[4,2,16,4096]{3,2,1,0:T(8,128)(2,1)S(1)}, u32[]{:S(2)}, u32[]{:S(2)}) collective-permute-start(bf16[4,2,16,4096]{3,2,1,0:T(8,128)(2,1)S(1)} %pad_maximum_fusion), channel_id=1, source_target_pairs={{0,1},{1,0},{2,3},{3,2},{4,5},{5,4},{6,7},{7,6},{8,9},{9,8},{10,11... | collective-permute-start | bytes 3145736 | tf_op jit(solution)/shard_map/ppermute | solution.py:395
  128.1 1.4 %copy-start.15 = (bf16[256,512]{1,0:T(8,128)(2,1)S(1)}, bf16[256,512]{1,0:T(8,128)(2,1)}, u32[]{:S(2)}) copy-start(bf16[256,512]{1,0:T(8,128)(2,1)} %get-tuple-element.22) | copy-start | bytes 786436

commit v4 on v3

--- a/solution.py
+++ b/solution.py
@@ -478,7 +478,7 @@
     received = lax.all_to_all(
         sent.reshape(GROUPS, SLOTS, FEAT), "dp", split_axis=0, concat_axis=0, tiled=True
     ).reshape(GROUPS * SLOTS, FEAT)
-    received = tied(received, far_taken, out_local)
+    received = tied(received, out_local)
     blocks = jnp.stack(
         [
             ((my_x + 4 - step) % 4) * 2 + (my_z + flip) % 2

time: 132 us -> 132 us (level)
  transfers between devices with their start and end apart: 27 -> 27, of which waited for: 9 -> 8; matrix products, arithmetic and copies ran while one was open for 11% -> 11% of each run, Pallas kernels for 19% -> 19%
where the time goes in v4:
time: 132 us; the launch traced here: 131 us
  starting transfers between devices  53.8 us (41%)
  waiting for transfers between devices  26.8 us (20%)
  Pallas kernels  24.8 us (19%)
  other arithmetic  13.8 us (10%)
  local copies, waits for them, and re-layouts  9.32 us (7%)
    ppermute x17, starting transfers between devices, dp_permute(): return lax.ppermute(value, 'dp', pairs)  28.8 us
    all_to_all x1, waiting for transfers between devices, on_device(): lax.all_to_all(partial.reshape(16, 16, HALF + 128), 'tensor', split_axis=...  13.5 us
    ppermute x7, waiting for transfers between devices, tensor_permute(): return lax.ppermute(value, 'tensor', pairs)  12.4 us
    ppermute x7, starting transfers between devices, tensor_permute(): return lax.ppermute(value, 'tensor', pairs)  11.8 us
    pallas_call x1, Pallas kernels, lookup(): pl.pallas_call(lookup_kernel, grid=(steps,), in_specs=[pl.BlockSpec((GROU...  9.37 us
    pallas_call x1, Pallas kernels, attend(): pl.pallas_call(attend_kernel, grid=(heads,), in_specs=[pl.BlockSpec(memor...  6.23 us
    all_to_all x1, starting transfers between devices, on_device(): lax.all_to_all(partial.reshape(16, 16, HALF + 128), 'tensor', split_axis=...  5.85 us
    pallas_call x1, Pallas kernels, project(): pl.pallas_call(project_kernel, grid=(width // COLS,), in_specs=[pl.BlockS...  5.65 us
  transfers between devices with their start and end apart: 27, of which 8 were waited for; matrix products, arithmetic and copies ran while one was open for 11% of the time, Pallas kernels for 19%

profile of v4, /device:TPU:1, one launch (start us, length us, event | category | flops | bytes accessed | tf_op | source)
XLA Modules:
  0.0 131.1 jit_solution(15495600695285070874)
XLA Ops:
  0.7 4.9 %fusion.25 = (bf16[1,64,5120]{2,1,0:T(8,128)(2,1)S(1)}, f32[1,64,5120]{2,1,0:T(8,128)}, f32[1,64,5120]{2,1,0:T(8,128)}, f32[1,64,5120]{2,1,0:T(8,128)}) fusion(f32[1,64,5120]{2,1,0:T(8,128)} %param.13, bf16[1,64,5120]{2,1,0:T(8,128)(2,1)} %param.16, f32[1,64,5120]{2,1,0:T(8,128)} %param.14, f32[1,64,5120]{2,1,0:T(8,128)} %param.15), kind=kLoop, calls=%fused_computation.65 | loop fusion | flops 5570560 | bytes 9175040 | tf_op jit(solution)/shard_map/convert_element_type | solution.py:437
  5.6 1.5 %collective-permute-start = (bf16[64,2560]{1,0:T(8,128)(2,1)S(1)}, bf16[64,2560]{1,0:T(8,128)(2,1)S(1)}, u32[]{:S(2)}, u32[]{:S(2)}) collective-permute-start(bf16[64,2560]{1,0:T(8,128)(2,1)S(1)} %get-tuple-element.41), channel_id=1, source_target_pairs={{0,1},{1,0},{2,3},{3,2},{4,5},{5,4},{6,7},{7,6},{8,9},{9,8},{10,11... | collective-permute-start | bytes 983048 | tf_op jit(solution)/shard_map/ppermute | solution.py:395
  7.1 1.3 collective-permute-done.rest_6_
  8.4 2.6 %collective-permute-start.3 = (bf16[64,2560]{1,0:T(8,128)(2,1)S(1)}, bf16[64,2560]{1,0:T(8,128)(2,1)S(1)}, u32[]{:S(2)}, u32[]{:S(2)}) collective-permute-start(bf16[64,2560]{1,0:T(8,128)(2,1)S(1)} %collective-permute-done.rest_6_), channel_id=1, source_target_pairs={{0,96},{16,112},{32,0},{48,16},{64,32},{80,48},{96,64},{112,80},{1... | collective-permute-start | bytes 983048 | tf_op jit(solution)/shard_map/ppermute | solution.py:387
  10.9 3.6 %collective-permute-start.1 = (bf16[64,2560]{1,0:T(8,128)(2,1)S(1)}, bf16[64,2560]{1,0:T(8,128)(2,1)S(1)}, u32[]{:S(2)}, u32[]{:S(2)}) collective-permute-start(bf16[64,2560]{1,0:T(8,128)(2,1)S(1)} %get-tuple-element.40.rest_0_), channel_id=1, source_target_pairs={{0,16},{16,0},{32,48},{48,32},{64,80},{80,64},{96,112},{112,96},{1... | collective-permute-start | bytes 983048 | tf_op jit(solution)/shard_map/ppermute | solution.py:387
  14.5 0.1 copy.21
  14.6 0.1 broadcast_in_dim.6
  14.7 0.6 broadcast_in_dim.7
  15.4 4.0 %all-to-all-start = ((s32[8,1,256]{2,1,0:T(1,128)}), s32[8,1,256]{2,1,0:T(1,128)S(1)}, u32[]{:S(2)}, u32[]{:S(2)}) async-start(s32[8,1,256]{2,1,0:T(1,128)} %broadcast_in_dim.7), calls=%async_computation | async-start | bytes 16384 | tf_op jit(solution)/shard_map/all_to_all | solution.py:444
  19.3 3.0 %collective-permute-start.9 = (bf16[64,2560]{1,0:T(8,128)(2,1)S(1)}, bf16[64,2560]{1,0:T(8,128)(2,1)}, u32[]{:S(2)}, u32[]{:S(2)}) collective-permute-start(bf16[64,2560]{1,0:T(8,128)(2,1)S(1)} %collective-permute-done.rest_6_), channel_id=1, source_target_pairs={{0,16},{16,0},{32,48},{48,32},{64,80},{80,64},{96,112},{112,96},{1... | collective-permute-start | bytes 983048 | tf_op jit(solution)/shard_map/ppermute | solution.py:387
  22.4 1.4 %pad_maximum_fusion.5 = (bf16[160,2560]{1,0:T(8,128)(2,1)}, bf16[160,2560]{1,0:T(8,128)(2,1)}) fusion(bf16[32,2560]{1,0:T(8,128)(2,1)S(1)} %slice.105, bf16[64,2560]{1,0:T(8,128)(2,1)S(1)} %collective-permute-done.1.rest_1_, bf16[64,2560]{1,0:T(8,128)(2,1)S(1)} %get-tuple-element.40.rest_0_, bf16[32,2560]{1,0:T(8,128)(2,1)S(1)} %slice.104), kind=kLoop, calls=%fused_computation.17 | loop fusion | flops 3686400 | bytes 2621440 | tf_op jit(solution)/shard_map/concatenate | solution.py:451
  23.8 1.2 collective-permute-start.5
  24.9 1.5 %collective-permute-start.6 = (bf16[160,2560]{1,0:T(8,128)(2,1)}, bf16[160,2560]{1,0:T(8,128)(2,1)S(1)}, u32[]{:S(2)}, u32[]{:S(2)}) collective-permute-start(bf16[160,2560]{1,0:T(8,128)(2,1)} %get-tuple-element.38), channel_id=1, source_target_pairs={{0,96},{16,112},{32,0},{48,16},{64,32},{80,48},{96,64},{112,80},{1... | collective-permute-start | bytes 2457608 | tf_op jit(solution)/shard_map/ppermute | solution.py:387
  26.4 0.7 constant_dynamic-update-slice_fusion.1
  27.2 0.8 constant_dynamic-update-slice_fusion
  28.0 2.2 %collective-permute-start.10 = (bf16[128,2560]{1,0:T(8,128)(2,1)}, bf16[128,2560]{1,0:T(8,128)(2,1)}, u32[]{:S(2)}, u32[]{:S(2)}) collective-permute-start(bf16[128,2560]{1,0:T(8,128)(2,1)} %constant_dynamic-update-slice_fusion), channel_id=1, source_target_pairs={{0,16},{16,0},{32,48},{48,32},{64,80},{80,64},{96,112},{112,96},{1... | collective-permute-start | bytes 1966088 | tf_op jit(solution)/shard_map/ppermute | solution.py:387
  30.2 0.6 copy-done.12
  30.8 9.4 %lookup.1 = bf16[512,512]{1,0:T(8,128)(2,1)} custom-call(s32[8,1,256]{2,1,0:T(1,128)} %copy-done.12, bf16[512,9504]{1,0:T(8,128)(2,1)} %bitcast.109), custom_call_target="tpu_custom_call" | custom-call | flops 30000001024 | bytes 10000000 | tf_op jit(solution)/shard_map/lookup/pallas_call | solution.py:99
  40.2 3.5 %all-to-all-start.1 = ((bf16[8,64,512]{2,1,0:T(8,128)(2,1)}), bf16[8,64,512]{2,1,0:T(8,128)(2,1)S(1)}, u32[]{:S(2)}, u32[]{:S(2)}) async-start(bf16[8,64,512]{2,1,0:T(8,128)(2,1)} %bitcast.106), calls=%async_computation.1 | async-start | bytes 1048576 | tf_op jit(solution)/shard_map/all_to_all | solution.py:478
  43.7 0.8 slice.106
  44.5 1.4 %collective-permute-start.7 = (bf16[64,2560]{1,0:T(8,128)(2,1)}, bf16[64,2560]{1,0:T(8,128)(2,1)}, u32[]{:S(2)}, u32[]{:S(2)}) collective-permute-start(bf16[64,2560]{1,0:T(8,128)(2,1)} %slice.106), channel_id=1, source_target_pairs={{0,32},{16,48},{32,64},{48,80},{64,96},{80,112},{96,0},{112,16},{1... | collective-permute-start | bytes 983048 | tf_op jit(solution)/shard_map/ppermute | solution.py:387
  45.8 0.8 slice.107
  46.6 1.3 %collective-permute-start.8 = (bf16[64,2560]{1,0:T(8,128)(2,1)}, bf16[64,2560]{1,0:T(8,128)(2,1)}, u32[]{:S(2)}, u32[]{:S(2)}) collective-permute-start(bf16[64,2560]{1,0:T(8,128)(2,1)} %slice.107), channel_id=1, source_target_pairs={{0,96},{16,112},{32,0},{48,16},{64,32},{80,48},{96,64},{112,80},{1... | collective-permute-start | bytes 983048 | tf_op jit(solution)/shard_map/ppermute | solution.py:387
  48.0 2.9 %collective-permute-start.11 = (bf16[64,2560]{1,0:T(8,128)(2,1)S(1)}, bf16[64,2560]{1,0:T(8,128)(2,1)}, u32[]{:S(2)}, u32[]{:S(2)}) collective-permute-start(bf16[64,2560]{1,0:T(8,128)(2,1)S(1)} %pad_maximum_fusion.6.rest_10_), channel_id=1, source_target_pairs={{0,16},{16,0},{32,48},{48,32},{64,80},{80,64},{96,112},{112,96},{1... | collective-permute-start | bytes 983048 | tf_op jit(solution)/shard_map/ppermute | solution.py:387
  51.0 4.2 %convert_bitcast_fusion = (bf16[64,4096]{1,0:T(8,128)(2,1)S(1)}, f32[1,64,4096]{2,1,0:T(8,128)}, f32[1,64,4096]{2,1,0:T(8,128)}, f32[1,64,4096]{2,1,0:T(8,128)}) fusion(f32[1,64,4096]{2,1,0:T(8,128)} %param.17, bf16[1,64,4096]{2,1,0:T(8,128)(2,1)} %param.20, f32[1,64,4096]{2,1,0:T(8,128)} %param.18, f32[1,64,4096]{2,1,0:T(8,128)} %param.19), kind=kLoop, calls=%fused_computation.18 | loop fusion | flops 4456448 | bytes 7340032 | tf_op jit(solution)/shard_map/squeeze | solution.py:442
  55.2 0.8 copy-done.5
  56.0 2.6 %arrange.1 = (bf16[256,512]{1,0:T(8,128)(2,1)}, bf16[256,512]{1,0:T(8,128)(2,1)}, bf16[256,128]{1,0:T(8,128)(2,1)}) custom-call(s32[8,1,256]{2,1,0:T(1,128)} %copy-done.12, bf16[512,512]{1,0:T(8,128)(2,1)} %bitcast.96, f32[8,64]{1,0:T(8,128)} %gain_ref.1), custom_call_target="tpu_custom_call" | custom-call | tf_op jit(solution)/shard_map/arrange/pallas_call | solution.py:144
  58.5 4.2 %collective-permute-start.4 = (bf16[256,512]{1,0:T(8,128)(2,1)}, bf16[256,512]{1,0:T(8,128)(2,1)S(1)}, u32[]{:S(2)}, u32[]{:S(2)}) collective-permute-start(bf16[256,512]{1,0:T(8,128)(2,1)} %get-tuple-element.23.own_ref), channel_id=1, source_target_pairs={{0,1},{1,0},{2,3},{3,2},{4,5},{5,4},{6,7},{7,6},{8,9},{9,8},{10,11... | collective-permute-start | bytes 786440 | tf_op jit(solution)/shard_map/ppermute | solution.py:395
  62.7 2.7 %collective-permute-start.18 = (bf16[64,4096]{1,0:T(8,128)(2,1)S(1)}, bf16[64,4096]{1,0:T(8,128)(2,1)S(1)}, u32[]{:S(2)}, u32[]{:S(2)}) collective-permute-start(bf16[64,4096]{1,0:T(8,128)(2,1)S(1)} %get-tuple-element.26.rest_0_), channel_id=1, source_target_pairs={{0,96},{16,112},{32,0},{48,16},{64,32},{80,48},{96,64},{112,80},{1... | collective-permute-start | bytes 1572872 | tf_op jit(solution)/shard_map/ppermute | solution.py:387
  65.4 1.0 collective-permute-start.19
  66.4 0.7 copy-done.11
  67.1 5.6 %project.1 = bf16[256,2688]{1,0:T(8,128)(2,1)} custom-call(bf16[256,512]{1,0:T(8,128)(2,1)} %get-tuple-element.23.own_ref, bf16[256,512]{1,0:T(8,128)(2,1)} %copy-done.11, bf16[256,128]{1,0:T(8,128)(2,1)} %get-tuple-element.24.squares_ref, bf16[64,2560]{1,0:T(8,128)(2,1)} %copy-done.2, bf16[64,2560]{1,0:T(8,128)(2,1)} %copy-done.8, ...), custom_call_target="tpu_custom_call" | custom-call | flops 1342177280 | bytes 5242880 | tf_op jit(solution)/shard_map/project/pallas_call | solution.py:209
  72.7 0.0 copy-start.13
  72.8 5.8 %all-to-all-start.2 = ((bf16[16,16,2688]{2,1,0:T(8,128)(2,1)}), bf16[16,16,2688]{2,1,0:T(8,128)(2,1)}, u32[]{:S(2)}, u32[]{:S(2)}) async-start(bf16[16,16,2688]{2,1,0:T(8,128)(2,1)} %bitcast.94), calls=%async_computation.2 | async-start | bytes 2752512 | tf_op jit(solution)/shard_map/all_to_all | solution.py:494
  78.6 0.1 add_convert_fusion
  78.7 0.1 convert_element_type.41
  78.9 0.9 collective-permute-done.19.rest_3_
  79.8 1.4 %pad_maximum_fusion.1 = (bf16[96,4096]{1,0:T(8,128)(2,1)}, bf16[96,4096]{1,0:T(8,128)(2,1)}) fusion(bf16[64,4096]{1,0:T(8,128)(2,1)S(1)} %collective-permute-done.19.rest_3_, bf16[32,4096]{1,0:T(8,128)(2,1)S(1)} %slice.127, bf16[32,4096]{1,0:T(8,128)(2,1)S(1)} %slice.126), kind=kLoop, calls=%fused_computation.13 | loop fusion | flops 2752512 | bytes 2621440 | tf_op jit(solution)/shard_map/concatenate | solution.py:408
  81.1 2.7 %collective-permute-start.21 = (bf16[96,4096]{1,0:T(8,128)(2,1)}, bf16[96,4096]{1,0:T(8,128)(2,1)S(1)}, u32[]{:S(2)}, u32[]{:S(2)}) collective-permute-start(bf16[96,4096]{1,0:T(8,128)(2,1)} %get-tuple-element.42), channel_id=1, source_target_pairs={{0,96},{16,112},{32,0},{48,16},{64,32},{80,48},{96,64},{112,80},{1... | collective-permute-start | bytes 2359304 | tf_op jit(solution)/shard_map/ppermute | solution.py:387
  83.8 0.1 fusion.21
  83.9 0.7 pad_maximum_fusion.8
  84.6 13.5 %all-to-all-done.2.parts_ref = bf16[16,16,2688]{2,1,0:T(8,128)(2,1)} async-done(((bf16[16,16,2688]{2,1,0:T(8,128)(2,1)}), bf16[16,16,2688]{2,1,0:T(8,128)(2,1)}, u32[]{:S(2)}, u32[]{:S(2)}) %all-to-all-start.2) | async-done | bytes 1376288 | tf_op jit(solution)/shard_map/all_to_all | solution.py:494
  98.1 6.2 %attend.1 = (bf16[16,4096]{1,0:T(8,128)(2,1)}, bf16[16,1024]{1,0:T(8,128)(2,1)}) custom-call(s32[4]{0:T(128)} %lengths_ref.1, bf16[16,16,2688]{2,1,0:T(8,128)(2,1)} %all-to-all-done.2.parts_ref, f32[16,128]{1,0:T(8,128)} %get-tuple-element.49.cos_ref, f32[16,128]{1,0:T(8,128)} %get-tuple-element.50.sin_ref, bf16[4,4,384,256]{3,2,1,0:T(8,128)(2,1)} %cache_ref.1), custom_call_target="tpu_custom_call" | custom-call | tf_op jit(solution)/shard_map/attend/pallas_call | solution.py:302
  104.3 0.3 collective-permute-start.12
  104.7 0.1 stack.67.blocks_ref
  104.8 1.4 %reshape.71 = bf16[4,4,4,256]{3,2,1,0:T(4,128)(2,1)} reshape(bf16[16,1024]{1,0:T(8,128)(2,1)} %get-tuple-element.29) | data formatting | bytes 65536 | tf_op jit(solution)/shard_map/reshape | solution.py:498
  106.2 2.7 %collective-permute-done.12 = bf16[16,4096]{1,0:T(8,128)(2,1)S(1)} collective-permute-done((bf16[16,4096]{1,0:T(8,128)(2,1)}, bf16[16,4096]{1,0:T(8,128)(2,1)S(1)}, u32[]{:S(2)}, u32[]{:S(2)}) %collective-permute-start.12) | collective-permute-done | bytes 131104 | tf_op jit(solution)/shard_map/ppermute | solution.py:395
  108.8 0.9 pad_maximum_fusion.7
  109.8 0.1 collective-permute-start.13
  109.9 2.7 %collective-permute-start.14 = (bf16[2,16,4096]{2,1,0:T(8,128)(2,1)S(1)}, bf16[2,16,4096]{2,1,0:T(8,128)(2,1)S(1)}, u32[]{:S(2)}, u32[]{:S(2)}) collective-permute-start(bf16[2,16,4096]{2,1,0:T(8,128)(2,1)S(1)} %get-tuple-element.44), channel_id=1, source_target_pairs={{0,4},{1,5},{2,6},{3,7},{4,0},{5,1},{6,2},{7,3},{8,12},{9,13},{10,... | collective-permute-start | bytes 786440 | tf_op jit(solution)/shard_map/ppermute | solution.py:395
  112.6 1.4 %collective-permute-start.15 = (bf16[2,16,4096]{2,1,0:T(8,128)(2,1)S(1)}, bf16[2,16,4096]{2,1,0:T(8,128)(2,1)S(1)}, u32[]{:S(2)}, u32[]{:S(2)}) collective-permute-start(bf16[2,16,4096]{2,1,0:T(8,128)(2,1)S(1)} %get-tuple-element.44), channel_id=1, source_target_pairs={{0,6},{1,7},{2,0},{3,1},{4,2},{5,3},{6,4},{7,5},{8,14},{9,15},{10,... | collective-permute-start | bytes 786440 | tf_op jit(solution)/shard_map/ppermute | solution.py:395
  114.0 0.1 collective-permute-start.22
  114.1 2.7 %collective-permute-start.23 = (bf16[32,4096]{1,0:T(8,128)(2,1)S(1)}, bf16[32,4096]{1,0:T(8,128)(2,1)S(1)}, u32[]{:S(2)}, u32[]{:S(2)}) collective-permute-start(bf16[32,4096]{1,0:T(8,128)(2,1)S(1)} %slice.103), channel_id=1, source_target_pairs={{0,96},{16,112},{32,0},{48,16},{64,32},{80,48},{96,64},{112,80},{1... | collective-permute-start | bytes 786440 | tf_op jit(solution)/shard_map/ppermute | solution.py:387
  116.8 0.2 broadcast_in_dim.16
  117.0 0.0 copy-start.1
  117.1 0.1 collective-permute-done.13
  117.2 6.6 %collective-permute-done.14 = bf16[2,16,4096]{2,1,0:T(8,128)(2,1)S(1)} collective-permute-done((bf16[2,16,4096]{2,1,0:T(8,128)(2,1)S(1)}, bf16[2,16,4096]{2,1,0:T(8,128)(2,1)S(1)}, u32[]{:S(2)}, u32[]{:S(2)}) %collective-permute-start.14) | collective-permute-done | bytes 262176 | tf_op jit(solution)/shard_map/ppermute | solution.py:395
  123.8 0.6 collective-permute-done.15
  124.5 0.1 pad_maximum_fusion
  124.6 1.6 %collective-permute-start.16 = (bf16[4,2,16,4096]{3,2,1,0:T(8,128)(2,1)S(1)}, bf16[4,2,16,4096]{3,2,1,0:T(8,128)(2,1)S(1)}, u32[]{:S(2)}, u32[]{:S(2)}) collective-permute-start(bf16[4,2,16,4096]{3,2,1,0:T(8,128)(2,1)S(1)} %pad_maximum_fusion), channel_id=1, source_target_pairs={{0,1},{1,0},{2,3},{3,2},{4,5},{5,4},{6,7},{7,6},{8,9},{9,8},{10,11... | collective-permute-start | bytes 3145736 | tf_op jit(solution)/shard_map/ppermute | solution.py:395
  126.4 1.0 collect.1
  127.4 1.1 collective-permute-done.16
  128.7 1.3 fusion.2
  130.0 1.1 reshape.70
  (76 shorter events, 0.6 us)
Async XLA Ops:
  0.7 13.9 %copy-start.14 = (s32[64,4]{0,1:T(4,128)S(1)}, s32[64,4]{0,1:T(4,128)}, u32[]{:S(2)}) copy-start(s32[64,4]{0,1:T(4,128)} %param.23) | copy-start | bytes 3076
  5.6 22.3 %copy-start.2 = (bf16[64,2560]{1,0:T(8,128)(2,1)}, bf16[64,2560]{1,0:T(8,128)(2,1)S(1)}, u32[]{:S(2)}) copy-start(bf16[64,2560]{1,0:T(8,128)(2,1)S(1)} %get-tuple-element.40.rest_0_) | copy-start | bytes 983044
  5.6 2.8 %collective-permute-start = (bf16[64,2560]{1,0:T(8,128)(2,1)S(1)}, bf16[64,2560]{1,0:T(8,128)(2,1)S(1)}, u32[]{:S(2)}, u32[]{:S(2)}) collective-permute-start(bf16[64,2560]{1,0:T(8,128)(2,1)S(1)} %get-tuple-element.41), channel_id=1, source_target_pairs={{0,1},{1,0},{2,3},{3,2},{4,5},{5,4},{6,7},{7,6},{8,9},{9,8},{10,11... | collective-permute-start | bytes 983048 | tf_op jit(solution)/shard_map/ppermute | solution.py:395
  8.4 19.6 %copy-start.10 = (bf16[64,2560]{1,0:T(8,128)(2,1)}, bf16[64,2560]{1,0:T(8,128)(2,1)S(1)}, u32[]{:S(2)}) copy-start(bf16[64,2560]{1,0:T(8,128)(2,1)S(1)} %collective-permute-done.rest_6_) | copy-start | bytes 983044
  8.4 13.9 %collective-permute-start.3 = (bf16[64,2560]{1,0:T(8,128)(2,1)S(1)}, bf16[64,2560]{1,0:T(8,128)(2,1)S(1)}, u32[]{:S(2)}, u32[]{:S(2)}) collective-permute-start(bf16[64,2560]{1,0:T(8,128)(2,1)S(1)} %collective-permute-done.rest_6_), channel_id=1, source_target_pairs={{0,96},{16,112},{32,0},{48,16},{64,32},{80,48},{96,64},{112,80},{1... | collective-permute-start | bytes 983048 | tf_op jit(solution)/shard_map/ppermute | solution.py:387
  10.9 11.4 %collective-permute-start.2 = (bf16[64,2560]{1,0:T(8,128)(2,1)S(1)}, bf16[64,2560]{1,0:T(8,128)(2,1)S(1)}, u32[]{:S(2)}, u32[]{:S(2)}) collective-permute-start(bf16[64,2560]{1,0:T(8,128)(2,1)S(1)} %collective-permute-done.rest_6_), channel_id=1, source_target_pairs={{0,32},{16,48},{32,64},{48,80},{64,96},{80,112},{96,0},{112,16},{1... | collective-permute-start | bytes 983048 | tf_op jit(solution)/shard_map/ppermute | solution.py:387
  10.9 11.4 %collective-permute-start.1 = (bf16[64,2560]{1,0:T(8,128)(2,1)S(1)}, bf16[64,2560]{1,0:T(8,128)(2,1)S(1)}, u32[]{:S(2)}, u32[]{:S(2)}) collective-permute-start(bf16[64,2560]{1,0:T(8,128)(2,1)S(1)} %get-tuple-element.40.rest_0_), channel_id=1, source_target_pairs={{0,16},{16,0},{32,48},{48,32},{64,80},{80,64},{96,112},{112,96},{1... | collective-permute-start | bytes 983048 | tf_op jit(solution)/shard_map/ppermute | solution.py:387
  15.4 14.8 %all-to-all-start = ((s32[8,1,256]{2,1,0:T(1,128)}), s32[8,1,256]{2,1,0:T(1,128)S(1)}, u32[]{:S(2)}, u32[]{:S(2)}) async-start(s32[8,1,256]{2,1,0:T(1,128)} %broadcast_in_dim.7), calls=%async_computation | async-start | bytes 16384 | tf_op jit(solution)/shard_map/all_to_all | solution.py:444
  19.3 46.1 %collective-permute-start.9 = (bf16[64,2560]{1,0:T(8,128)(2,1)S(1)}, bf16[64,2560]{1,0:T(8,128)(2,1)}, u32[]{:S(2)}, u32[]{:S(2)}) collective-permute-start(bf16[64,2560]{1,0:T(8,128)(2,1)S(1)} %collective-permute-done.rest_6_), channel_id=1, source_target_pairs={{0,16},{16,0},{32,48},{48,32},{64,80},{80,64},{96,112},{112,96},{1... | collective-permute-start | bytes 983048 | tf_op jit(solution)/shard_map/ppermute | solution.py:387
  22.3 5.7 %copy-start.6 = (bf16[64,2560]{1,0:T(8,128)(2,1)}, bf16[64,2560]{1,0:T(8,128)(2,1)S(1)}, u32[]{:S(2)}) copy-start(bf16[64,2560]{1,0:T(8,128)(2,1)S(1)} %collective-permute-done.3.rest_9_) | copy-start | bytes 983044
  22.3 5.7 %copy-start.7 = (bf16[64,2560]{1,0:T(8,128)(2,1)}, bf16[64,2560]{1,0:T(8,128)(2,1)S(1)}, u32[]{:S(2)}) copy-start(bf16[64,2560]{1,0:T(8,128)(2,1)S(1)} %collective-permute-done.2.rest_8_) | copy-start | bytes 983044
  22.3 17.8 %copy-start.8 = (bf16[64,2560]{1,0:T(8,128)(2,1)}, bf16[64,2560]{1,0:T(8,128)(2,1)S(1)}, u32[]{:S(2)}) copy-start(bf16[64,2560]{1,0:T(8,128)(2,1)S(1)} %collective-permute-done.1.rest_1_) | copy-start | bytes 983044
  23.8 19.9 %collective-permute-start.5 = (bf16[160,2560]{1,0:T(8,128)(2,1)}, bf16[160,2560]{1,0:T(8,128)(2,1)S(1)}, u32[]{:S(2)}, u32[]{:S(2)}) collective-permute-start(bf16[160,2560]{1,0:T(8,128)(2,1)} %get-tuple-element.39), channel_id=1, source_target_pairs={{0,32},{16,48},{32,64},{48,80},{64,96},{80,112},{96,0},{112,16},{1... | collective-permute-start | bytes 2457608 | tf_op jit(solution)/shard_map/ppermute | solution.py:387
  24.9 20.9 %collective-permute-start.6 = (bf16[160,2560]{1,0:T(8,128)(2,1)}, bf16[160,2560]{1,0:T(8,128)(2,1)S(1)}, u32[]{:S(2)}, u32[]{:S(2)}) collective-permute-start(bf16[160,2560]{1,0:T(8,128)(2,1)} %get-tuple-element.38), channel_id=1, source_target_pairs={{0,96},{16,112},{32,0},{48,16},{64,32},{80,48},{96,64},{112,80},{1... | collective-permute-start | bytes 2457608 | tf_op jit(solution)/shard_map/ppermute | solution.py:387
  28.0 38.4 %collective-permute-start.10 = (bf16[128,2560]{1,0:T(8,128)(2,1)}, bf16[128,2560]{1,0:T(8,128)(2,1)}, u32[]{:S(2)}, u32[]{:S(2)}) collective-permute-start(bf16[128,2560]{1,0:T(8,128)(2,1)} %constant_dynamic-update-slice_fusion), channel_id=1, source_target_pairs={{0,16},{16,0},{32,48},{48,32},{64,80},{80,64},{96,112},{112,96},{1... | collective-permute-start | bytes 1966088 | tf_op jit(solution)/shard_map/ppermute | solution.py:387
  30.2 0.6 copy-start.12
  40.2 15.0 %all-to-all-start.1 = ((bf16[8,64,512]{2,1,0:T(8,128)(2,1)}), bf16[8,64,512]{2,1,0:T(8,128)(2,1)S(1)}, u32[]{:S(2)}, u32[]{:S(2)}) async-start(bf16[8,64,512]{2,1,0:T(8,128)(2,1)} %bitcast.106), calls=%async_computation.1 | async-start | bytes 1048576 | tf_op jit(solution)/shard_map/all_to_all | solution.py:478
  43.7 4.3 %copy-start.3 = (bf16[160,2560]{1,0:T(8,128)(2,1)}, bf16[160,2560]{1,0:T(8,128)(2,1)S(1)}, u32[]{:S(2)}) copy-start(bf16[160,2560]{1,0:T(8,128)(2,1)S(1)} %collective-permute-done.5.rest_2_) | copy-start | bytes 2457604
  44.5 14.1 %collective-permute-start.7 = (bf16[64,2560]{1,0:T(8,128)(2,1)}, bf16[64,2560]{1,0:T(8,128)(2,1)}, u32[]{:S(2)}, u32[]{:S(2)}) collective-permute-start(bf16[64,2560]{1,0:T(8,128)(2,1)} %slice.106), channel_id=1, source_target_pairs={{0,32},{16,48},{32,64},{48,80},{64,96},{80,112},{96,0},{112,16},{1... | collective-permute-start | bytes 983048 | tf_op jit(solution)/shard_map/ppermute | solution.py:387
  45.8 9.3 %copy-start.4 = (bf16[160,2560]{1,0:T(8,128)(2,1)}, bf16[160,2560]{1,0:T(8,128)(2,1)S(1)}, u32[]{:S(2)}) copy-start(bf16[160,2560]{1,0:T(8,128)(2,1)S(1)} %collective-permute-done.6.rest_3_) | copy-start | bytes 2457604
  46.6 16.1 %collective-permute-start.8 = (bf16[64,2560]{1,0:T(8,128)(2,1)}, bf16[64,2560]{1,0:T(8,128)(2,1)}, u32[]{:S(2)}, u32[]{:S(2)}) collective-permute-start(bf16[64,2560]{1,0:T(8,128)(2,1)} %slice.107), channel_id=1, source_target_pairs={{0,96},{16,112},{32,0},{48,16},{64,32},{80,48},{96,64},{112,80},{1... | collective-permute-start | bytes 983048 | tf_op jit(solution)/shard_map/ppermute | solution.py:387
  48.0 7.1 %copy-start.9 = (bf16[64,2560]{1,0:T(8,128)(2,1)}, bf16[64,2560]{1,0:T(8,128)(2,1)S(1)}, u32[]{:S(2)}) copy-start(bf16[64,2560]{1,0:T(8,128)(2,1)S(1)} %pad_maximum_fusion.6.rest_10_) | copy-start | bytes 983044
  48.0 14.7 %collective-permute-start.11 = (bf16[64,2560]{1,0:T(8,128)(2,1)S(1)}, bf16[64,2560]{1,0:T(8,128)(2,1)}, u32[]{:S(2)}, u32[]{:S(2)}) collective-permute-start(bf16[64,2560]{1,0:T(8,128)(2,1)S(1)} %pad_maximum_fusion.6.rest_10_), channel_id=1, source_target_pairs={{0,16},{16,0},{32,48},{48,32},{64,80},{80,64},{96,112},{112,96},{1... | collective-permute-start | bytes 983048 | tf_op jit(solution)/shard_map/ppermute | solution.py:387
  55.2 0.8 copy-start.5
  58.5 7.8 %collective-permute-start.4 = (bf16[256,512]{1,0:T(8,128)(2,1)}, bf16[256,512]{1,0:T(8,128)(2,1)S(1)}, u32[]{:S(2)}, u32[]{:S(2)}) collective-permute-start(bf16[256,512]{1,0:T(8,128)(2,1)} %get-tuple-element.23.own_ref), channel_id=1, source_target_pairs={{0,1},{1,0},{2,3},{3,2},{4,5},{5,4},{6,7},{7,6},{8,9},{9,8},{10,11... | collective-permute-start | bytes 786440 | tf_op jit(solution)/shard_map/ppermute | solution.py:395
  62.7 16.1 %collective-permute-start.17 = (bf16[64,4096]{1,0:T(8,128)(2,1)S(1)}, bf16[64,4096]{1,0:T(8,128)(2,1)S(1)}, u32[]{:S(2)}, u32[]{:S(2)}) collective-permute-start(bf16[64,4096]{1,0:T(8,128)(2,1)S(1)} %get-tuple-element.26.rest_0_), channel_id=1, source_target_pairs={{0,32},{16,48},{32,64},{48,80},{64,96},{80,112},{96,0},{112,16},{1... | collective-permute-start | bytes 1572872 | tf_op jit(solution)/shard_map/ppermute | solution.py:387
  62.7 16.0 %collective-permute-start.18 = (bf16[64,4096]{1,0:T(8,128)(2,1)S(1)}, bf16[64,4096]{1,0:T(8,128)(2,1)S(1)}, u32[]{:S(2)}, u32[]{:S(2)}) collective-permute-start(bf16[64,4096]{1,0:T(8,128)(2,1)S(1)} %get-tuple-element.26.rest_0_), channel_id=1, source_target_pairs={{0,96},{16,112},{32,0},{48,16},{64,32},{80,48},{96,64},{112,80},{1... | collective-permute-start | bytes 1572872 | tf_op jit(solution)/shard_map/ppermute | solution.py:387
  65.4 14.4 %collective-permute-start.19 = (bf16[64,4096]{1,0:T(8,128)(2,1)S(1)}, bf16[64,4096]{1,0:T(8,128)(2,1)S(1)}, u32[]{:S(2)}, u32[]{:S(2)}) collective-permute-start(bf16[64,4096]{1,0:T(8,128)(2,1)S(1)} %get-tuple-element.26.rest_0_), channel_id=1, source_target_pairs={{0,16},{16,0},{32,48},{48,32},{64,80},{80,64},{96,112},{112,96},{1... | collective-permute-start | bytes 1572872 | tf_op jit(solution)/shard_map/ppermute | solution.py:387
  66.4 0.7 copy-start.11
  72.7 5.9 %copy-start.13 = (s32[4]{0:T(128)S(1)}, s32[4]{0:T(128)}, u32[]{:S(2)}) copy-start(s32[4]{0:T(128)} %lengths_ref.1) | copy-start | bytes 52
  72.8 25.3 %all-to-all-start.2 = ((bf16[16,16,2688]{2,1,0:T(8,128)(2,1)}), bf16[16,16,2688]{2,1,0:T(8,128)(2,1)}, u32[]{:S(2)}, u32[]{:S(2)}) async-start(bf16[16,16,2688]{2,1,0:T(8,128)(2,1)} %bitcast.94), calls=%async_computation.2 | async-start | bytes 2752512 | tf_op jit(solution)/shard_map/all_to_all | solution.py:494
  78.8 2.4 %copy-start = (bf16[64,4096]{1,0:T(8,128)(2,1)}, bf16[64,4096]{1,0:T(8,128)(2,1)S(1)}, u32[]{:S(2)}) copy-start(bf16[64,4096]{1,0:T(8,128)(2,1)S(1)} %collective-permute-done.18.rest_2_) | copy-start | bytes 1572868
  81.1 32.8 %collective-permute-start.20 = (bf16[96,4096]{1,0:T(8,128)(2,1)}, bf16[96,4096]{1,0:T(8,128)(2,1)S(1)}, u32[]{:S(2)}, u32[]{:S(2)}) collective-permute-start(bf16[96,4096]{1,0:T(8,128)(2,1)} %get-tuple-element.43), channel_id=1, source_target_pairs={{0,32},{16,48},{32,64},{48,80},{64,96},{80,112},{96,0},{112,16},{1... | collective-permute-start | bytes 2359304 | tf_op jit(solution)/shard_map/ppermute | solution.py:387
  81.1 32.9 %collective-permute-start.21 = (bf16[96,4096]{1,0:T(8,128)(2,1)}, bf16[96,4096]{1,0:T(8,128)(2,1)S(1)}, u32[]{:S(2)}, u32[]{:S(2)}) collective-permute-start(bf16[96,4096]{1,0:T(8,128)(2,1)} %get-tuple-element.42), channel_id=1, source_target_pairs={{0,96},{16,112},{32,0},{48,16},{64,32},{80,48},{96,64},{112,80},{1... | collective-permute-start | bytes 2359304 | tf_op jit(solution)/shard_map/ppermute | solution.py:387
  104.3 4.5 %collective-permute-start.12 = (bf16[16,4096]{1,0:T(8,128)(2,1)}, bf16[16,4096]{1,0:T(8,128)(2,1)S(1)}, u32[]{:S(2)}, u32[]{:S(2)}) collective-permute-start(bf16[16,4096]{1,0:T(8,128)(2,1)} %get-tuple-element.25), channel_id=1, source_target_pairs={{0,8},{1,9},{2,10},{3,11},{4,12},{5,13},{6,14},{7,15},{8,0},{9,1},... | collective-permute-start | bytes 393224 | tf_op jit(solution)/shard_map/ppermute | solution.py:395
  109.8 7.5 %collective-permute-start.13 = (bf16[2,16,4096]{2,1,0:T(8,128)(2,1)S(1)}, bf16[2,16,4096]{2,1,0:T(8,128)(2,1)S(1)}, u32[]{:S(2)}, u32[]{:S(2)}) collective-permute-start(bf16[2,16,4096]{2,1,0:T(8,128)(2,1)S(1)} %get-tuple-element.44), channel_id=1, source_target_pairs={{0,2},{1,3},{2,4},{3,5},{4,6},{5,7},{6,0},{7,1},{8,10},{9,11},{10,... | collective-permute-start | bytes 786440 | tf_op jit(solution)/shard_map/ppermute | solution.py:395
  109.9 14.0 %collective-permute-start.14 = (bf16[2,16,4096]{2,1,0:T(8,128)(2,1)S(1)}, bf16[2,16,4096]{2,1,0:T(8,128)(2,1)S(1)}, u32[]{:S(2)}, u32[]{:S(2)}) collective-permute-start(bf16[2,16,4096]{2,1,0:T(8,128)(2,1)S(1)} %get-tuple-element.44), channel_id=1, source_target_pairs={{0,4},{1,5},{2,6},{3,7},{4,0},{5,1},{6,2},{7,3},{8,12},{9,13},{10,... | collective-permute-start | bytes 786440 | tf_op jit(solution)/shard_map/ppermute | solution.py:395
  112.6 11.9 %collective-permute-start.15 = (bf16[2,16,4096]{2,1,0:T(8,128)(2,1)S(1)}, bf16[2,16,4096]{2,1,0:T(8,128)(2,1)S(1)}, u32[]{:S(2)}, u32[]{:S(2)}) collective-permute-start(bf16[2,16,4096]{2,1,0:T(8,128)(2,1)S(1)} %get-tuple-element.44), channel_id=1, source_target_pairs={{0,6},{1,7},{2,0},{3,1},{4,2},{5,3},{6,4},{7,5},{8,14},{9,15},{10,... | collective-permute-start | bytes 786440 | tf_op jit(solution)/shard_map/ppermute | solution.py:395
  114.0 12.4 %collective-permute-start.22 = (bf16[32,4096]{1,0:T(8,128)(2,1)S(1)}, bf16[32,4096]{1,0:T(8,128)(2,1)S(1)}, u32[]{:S(2)}, u32[]{:S(2)}) collective-permute-start(bf16[32,4096]{1,0:T(8,128)(2,1)S(1)} %slice.102), channel_id=1, source_target_pairs={{0,32},{16,48},{32,64},{48,80},{64,96},{80,112},{96,0},{112,16},{1... | collective-permute-start | bytes 786440 | tf_op jit(solution)/shard_map/ppermute | solution.py:387
  114.1 12.3 %collective-permute-start.23 = (bf16[32,4096]{1,0:T(8,128)(2,1)S(1)}, bf16[32,4096]{1,0:T(8,128)(2,1)S(1)}, u32[]{:S(2)}, u32[]{:S(2)}) collective-permute-start(bf16[32,4096]{1,0:T(8,128)(2,1)S(1)} %slice.103), channel_id=1, source_target_pairs={{0,96},{16,112},{32,0},{48,16},{64,32},{80,48},{96,64},{112,80},{1... | collective-permute-start | bytes 786440 | tf_op jit(solution)/shard_map/ppermute | solution.py:387
  117.0 9.3 %copy-start.1 = (bf16[64,4096]{1,0:T(8,128)(2,1)S(1)}, bf16[64,4096]{1,0:T(8,128)(2,1)}, u32[]{:S(2)}) copy-start(bf16[64,4096]{1,0:T(8,128)(2,1)} %copy-done) | copy-start | bytes 1572868
  124.6 3.9 %collective-permute-start.16 = (bf16[4,2,16,4096]{3,2,1,0:T(8,128)(2,1)S(1)}, bf16[4,2,16,4096]{3,2,1,0:T(8,128)(2,1)S(1)}, u32[]{:S(2)}, u32[]{:S(2)}) collective-permute-start(bf16[4,2,16,4096]{3,2,1,0:T(8,128)(2,1)S(1)} %pad_maximum_fusion), channel_id=1, source_target_pairs={{0,1},{1,0},{2,3},{3,2},{4,5},{5,4},{6,7},{7,6},{8,9},{9,8},{10,11... | collective-permute-start | bytes 3145736 | tf_op jit(solution)/shard_map/ppermute | solution.py:395
  127.3 1.4 %copy-start.15 = (bf16[256,512]{1,0:T(8,128)(2,1)S(1)}, bf16[256,512]{1,0:T(8,128)(2,1)}, u32[]{:S(2)}) copy-start(bf16[256,512]{1,0:T(8,128)(2,1)} %get-tuple-element.22) | copy-start | bytes 786436
